TPU v7x, 32 devices: a whole 2x2x4 slice. The times are simulated.
32 devices in a mesh: seq: 2 (over x), blk: 4 (over z), head: 4 (over y, core).
Axes of the slice: x: 2, y: 2, z: 4, core: 2. Of those that a mesh axis runs over, the one named last changes fastest.
Arguments:
- layer_input: bfloat16 [2, 8192, 1024], P('seq', ('blk', 'head')), may hold values from -6 to 6
- weight_query: bfloat16 [1024, 1024], P(('seq', 'blk', 'head')), may hold values from -0.1875 to 0.1875
- weight_key: bfloat16 [1024, 1024], P(('seq', 'blk', 'head')), may hold values from -0.1875 to 0.1875
- weight_value: bfloat16 [1024, 1024], P(('seq', 'blk', 'head')), may hold values from -0.1875 to 0.1875
- weight_output: bfloat16 [1024, 1024], P(('seq', 'blk', 'head')), may hold values from -1.5 to 1.5
- weight_expand: bfloat16 [1024, 4096], P(('seq', 'blk', 'head')), may hold values from -0.1875 to 0.1875
- weight_reduce: bfloat16 [4096, 1024], P(('seq', 'blk', 'head')), may hold values from -0.09375 to 0.09375
- bias_query: bfloat16 [1024], P(('seq', 'blk', 'head')), may hold values from -3 to 3
- bias_value: bfloat16 [1024], P(('seq', 'blk', 'head')), may hold values from -3 to 3
- bias_output: bfloat16 [1024], P(('seq', 'blk', 'head')), may hold values from -3 to 3
- bias_expand: bfloat16 [4096], P(('seq', 'blk', 'head')), may hold values from -3 to 3
- bias_reduce: bfloat16 [1024], P(('seq', 'blk', 'head')), may hold values from -3 to 3
- first_gain: bfloat16 [1024], P(('seq', 'blk', 'head')), may hold values from 0.5 to 1.5
- first_shift: bfloat16 [1024], P(('seq', 'blk', 'head')), may hold values from -3 to 3
- second_gain: bfloat16 [1024], P(('seq', 'blk', 'head')), may hold values from 0.5 to 1.5
- second_shift: bfloat16 [1024], P(('seq', 'blk', 'head')), may hold values from -3 to 3
- cotangent: bfloat16 [2, 8192, 1024], P('seq', ('blk', 'head')), may hold values from -6 to 6
- doc_lengths: int32 [2, 32], P('seq'), may hold values from 0 to 7168, as said below
Outputs:
- layer_output: bfloat16 [2, 8192, 1024], P('seq', ('blk', 'head'))
- grad_input: float32 [2, 8192, 1024], P('seq', ('blk', 'head'))
- grad_weight_query: float32 [1024, 1024], P(('seq', 'blk', 'head'))
- grad_weight_key: float32 [1024, 1024], P(('seq', 'blk', 'head'))
- grad_weight_value: float32 [1024, 1024], P(('seq', 'blk', 'head'))
- grad_weight_output: float32 [1024, 1024], P(('seq', 'blk', 'head'))
- grad_weight_expand: float32 [1024, 4096], P(('seq', 'blk', 'head'))
- grad_weight_reduce: float32 [4096, 1024], P(('seq', 'blk', 'head'))
- grad_bias_query: float32 [1024], P(('seq', 'blk', 'head'))
- grad_bias_value: float32 [1024], P(('seq', 'blk', 'head'))
- grad_bias_output: float32 [1024], P(('seq', 'blk', 'head'))
- grad_bias_expand: float32 [4096], P(('seq', 'blk', 'head'))
- grad_bias_reduce: float32 [1024], P(('seq', 'blk', 'head'))
- grad_first_gain: float32 [1024], P(('seq', 'blk', 'head'))
- grad_first_shift: float32 [1024], P(('seq', 'blk', 'head'))
- grad_second_gain: float32 [1024], P(('seq', 'blk', 'head'))
- grad_second_shift: float32 [1024], P(('seq', 'blk', 'head'))
Inputs may be any that keep to these rules, and one draw needn't show every extreme that they name: `doc_lengths`: row s lists the lengths of the documents packed in order at the head of sequence s (zero for an unused slot); the tokens after them are padding. In each group of 1 sequence on one index of seq, one sequence, drawn from the seed, starts with a document of exactly 7168 tokens, leaves its last slot unused and ends with 1 to 512 tokens of padding; every other document is shorter, and every other sequence ends with more than 1024 tokens of padding.
All inputs are finite; a program needn't handle non-finite values.
Results may differ from a plain program's by a relative error of at most 0.022.
Values may be sent and summed in bfloat16 or wider, within the bound.
A program may use at most 256 MiB of HBM per device.

v0:
```python
import math

import jax
import jax.numpy as jnp
from jax import lax
from jax.sharding import PartitionSpec as P

HEADS = 16
HEAD_DIM = 64


NORM_EPS = 1e-05
INV_ROOT2 = 0.7071067811865476


def segment_ids(doc_lengths, positions):
    ends = jnp.cumsum(doc_lengths, axis=-1)
    counted = jnp.sum((ends[:, None, :] <= positions[None, :, None]).astype(jnp.int32), axis=-1)
    return jnp.where(positions[None, :] < ends[:, -1:], counted + 1, 0)


def layer_norm(values, gain, shift):
    center = values - jnp.mean(values, axis=-1, keepdims=True)
    spread = jnp.mean(center * center, axis=-1, keepdims=True)
    return center * lax.rsqrt(spread + NORM_EPS) * gain + shift


def gelu_curve(values):
    return 0.5 * values * (1.0 + lax.erf(values * INV_ROOT2))


def plain_dot(left, right):
    return jnp.dot(left, right, preferred_element_type=jnp.float32)


def left_dot(left, right):
    return lax.dot_general(
        left, right, (((0,), (0,)), ((), ())), preferred_element_type=jnp.float32
    )


def right_dot(left, right):
    return lax.dot_general(
        left, right, (((1,), (1,)), ((), ())), preferred_element_type=jnp.float32
    )


def score_grads(scores, allowed, grad_part, value_part, lse_part, delta_part):
    probs = jnp.where(allowed, jnp.exp(scores - lse_part[..., None]), 0.0)
    grad_probs = jnp.einsum(
        "sqhd,skhd->shqk", grad_part, value_part, preferred_element_type=jnp.float32
    )
    grad_scores = (probs * (grad_probs - delta_part[..., None])).astype(jnp.bfloat16)
    return (probs, grad_scores)


def shards(
    layer_input,
    weight_query,
    weight_key,
    weight_value,
    weight_output,
    weight_expand,
    weight_reduce,
    bias_query,
    bias_value,
    bias_output,
    bias_expand,
    bias_reduce,
    first_gain,
    first_shift,
    second_gain,
    second_shift,
    cotangent,
    doc_lengths,
):
    seq_count, tok_rows, model_width = layer_input.shape
    head_count = lax.axis_size("head")
    blk_count = lax.axis_size("blk")
    heads_here = HEADS // head_count
    score_scale = HEAD_DIM ** (-0.5)
    gathered = (
        lax.all_gather(weight_query, ("seq", "blk", "head"), axis=0, tiled=True),
        lax.all_gather(weight_key, ("seq", "blk", "head"), axis=0, tiled=True),
        lax.all_gather(weight_value, ("seq", "blk", "head"), axis=0, tiled=True),
        lax.all_gather(weight_output, ("seq", "blk", "head"), axis=0, tiled=True),
        lax.all_gather(weight_expand, ("seq", "blk", "head"), axis=0, tiled=True),
        lax.all_gather(weight_reduce, ("seq", "blk", "head"), axis=0, tiled=True),
        lax.all_gather(bias_query, ("seq", "blk", "head"), axis=0, tiled=True),
        lax.all_gather(bias_value, ("seq", "blk", "head"), axis=0, tiled=True),
        lax.all_gather(bias_output, ("seq", "blk", "head"), axis=0, tiled=True),
        lax.all_gather(bias_expand, ("seq", "blk", "head"), axis=0, tiled=True),
        lax.all_gather(bias_reduce, ("seq", "blk", "head"), axis=0, tiled=True),
        lax.all_gather(first_gain, ("seq", "blk", "head"), axis=0, tiled=True),
        lax.all_gather(first_shift, ("seq", "blk", "head"), axis=0, tiled=True),
        lax.all_gather(second_gain, ("seq", "blk", "head"), axis=0, tiled=True),
        lax.all_gather(second_shift, ("seq", "blk", "head"), axis=0, tiled=True),
    )
    w_query, w_key, w_value, w_output, w_expand, w_reduce = gathered[:6]
    b_query, b_value, b_output, b_expand, b_reduce, gain_one, shift_one, gain_two, shift_two = [
        vector.astype(jnp.float32) for vector in gathered[6:]
    ]
    flat_rows = layer_input.reshape(-1, model_width)
    queries = (
        (plain_dot(flat_rows, w_query) + b_query).astype(jnp.bfloat16).reshape(layer_input.shape)
    )
    key_rows = plain_dot(flat_rows, w_key).astype(jnp.bfloat16).reshape(layer_input.shape)
    value_rows = (
        (plain_dot(flat_rows, w_value) + b_value).astype(jnp.bfloat16).reshape(layer_input.shape)
    )
    query_heads, key_heads, value_heads = (
        lax.all_to_all(queries, "head", split_axis=2, concat_axis=1, tiled=True),
        lax.all_to_all(key_rows, "head", split_axis=2, concat_axis=1, tiled=True),
        lax.all_to_all(value_rows, "head", split_axis=2, concat_axis=1, tiled=True),
    )
    block_rows = query_heads.shape[1]
    block_first = lax.axis_index("blk") * block_rows
    query_seg = segment_ids(doc_lengths, block_first + lax.iota(jnp.int32, block_rows))
    query_split = query_heads.reshape(seq_count, block_rows, heads_here, HEAD_DIM)

    def key_block(shard_piece, block_index, block_width):
        key_offset = block_index * block_width
        key_part = lax.dynamic_slice_in_dim(shard_piece[0], key_offset, block_width, 1).reshape(
            seq_count, block_width, heads_here, HEAD_DIM
        )
        value_part = lax.dynamic_slice_in_dim(shard_piece[1], key_offset, block_width, 1).reshape(
            seq_count, block_width, heads_here, HEAD_DIM
        )
        key_seg = segment_ids(doc_lengths, key_offset + lax.iota(jnp.int32, block_width))
        allowed = query_seg[:, None, :, None] == key_seg[:, None, None, :]
        scores = (
            jnp.einsum("sqhd,skhd->shqk", query_split, key_part, preferred_element_type=jnp.float32)
            * score_scale
        )
        return (key_offset, key_part, value_part, allowed, scores)

    stat_shape = (seq_count, heads_here, block_rows)
    start_state = (
        jnp.full(stat_shape, -1e30, jnp.float32),
        jnp.zeros(stat_shape, jnp.float32),
        jnp.zeros(stat_shape + (HEAD_DIM,), jnp.float32),
    )
    shard_piece = (
        lax.all_gather(key_heads, "blk", axis=1, tiled=True),
        lax.all_gather(value_heads, "blk", axis=1, tiled=True),
    )
    piece_rows = shard_piece[0].shape[1]
    block_width = math.gcd(piece_rows, 512)

    def advance(block_index, loop_state):
        running_max, row_total, accum = loop_state
        key_offset, key_part, value_part, allowed, scores = key_block(
            shard_piece, block_index, block_width
        )
        scores = jnp.where(allowed, scores, -1e30)
        new_max = jnp.maximum(running_max, jnp.max(scores, axis=-1))
        rescale = jnp.exp(running_max - new_max)
        weights = jnp.where(allowed, jnp.exp(scores - new_max[..., None]), 0.0)
        row_total = row_total * rescale + jnp.sum(weights, axis=-1)
        accum = accum * rescale[..., None] + jnp.einsum(
            "shqk,skhd->shqd",
            weights.astype(jnp.bfloat16),
            value_part,
            preferred_element_type=jnp.float32,
        )
        return (new_max, row_total, accum)

    running_max, row_total, accum = lax.fori_loop(
        0, piece_rows // block_width, advance, start_state
    )
    log_total = running_max + jnp.log(row_total)
    attn_heads = accum / row_total[..., None]
    attn_send = (
        attn_heads.transpose(0, 2, 1, 3)
        .reshape(seq_count, block_rows, heads_here * HEAD_DIM)
        .astype(jnp.bfloat16)
    )
    attn_tokens = lax.all_to_all(attn_send, "head", split_axis=1, concat_axis=2, tiled=True)
    attn_flat = attn_tokens.reshape(-1, model_width)
    resid_one = flat_rows.astype(jnp.float32) + plain_dot(attn_flat, w_output) + b_output
    normed_one, norm_one_pull = jax.vjp(layer_norm, resid_one, gain_one, shift_one)
    normed_low = normed_one.astype(jnp.bfloat16)
    pre_act = plain_dot(normed_low, w_expand) + b_expand
    hidden_f32, gelu_pull = jax.vjp(gelu_curve, pre_act)
    hidden = hidden_f32.astype(jnp.bfloat16)
    resid_two = normed_one + plain_dot(hidden, w_reduce) + b_reduce
    result, norm_two_pull = jax.vjp(layer_norm, resid_two, gain_two, shift_two)
    layer_output = result.astype(jnp.bfloat16).reshape(layer_input.shape)
    tok_first = (lax.axis_index("blk") * head_count + lax.axis_index("head")) * tok_rows
    tok_seg = segment_ids(doc_lengths, tok_first + lax.iota(jnp.int32, tok_rows))
    live = (tok_seg > 0).astype(jnp.float32)
    grad_out = (cotangent.astype(jnp.float32) * live[..., None]).reshape(-1, model_width)
    grad_resid_two, grad_gain_two, grad_shift_two = norm_two_pull(grad_out)
    grad_ffn = grad_resid_two.astype(jnp.bfloat16)
    grad_w_reduce = left_dot(hidden, grad_ffn)
    grad_b_reduce = jnp.sum(grad_ffn.astype(jnp.float32), axis=0)
    (grad_pre,) = gelu_pull(right_dot(grad_ffn, w_reduce))
    grad_pre = grad_pre.astype(jnp.bfloat16)
    grad_w_expand = left_dot(normed_low, grad_pre)
    grad_b_expand = jnp.sum(grad_pre.astype(jnp.float32), axis=0)
    grad_normed = grad_resid_two + right_dot(grad_pre, w_expand)
    grad_resid_one, grad_gain_one, grad_shift_one = norm_one_pull(grad_normed)
    grad_branch = grad_resid_one.astype(jnp.bfloat16)
    grad_w_output = left_dot(attn_flat, grad_branch)
    grad_b_output = jnp.sum(grad_branch.astype(jnp.float32), axis=0)
    grad_attn = right_dot(grad_branch, w_output).astype(jnp.bfloat16).reshape(layer_input.shape)
    grad_attn_heads = lax.all_to_all(grad_attn, "head", split_axis=2, concat_axis=1, tiled=True)
    grad_attn_split = grad_attn_heads.reshape(seq_count, block_rows, heads_here, HEAD_DIM)
    row_delta = jnp.einsum("sqhd,shqd->shq", grad_attn_split.astype(jnp.float32), attn_heads)
    full_rows = blk_count * block_rows
    query_zero = jnp.zeros((seq_count, block_rows, heads_here, HEAD_DIM), jnp.float32)
    back_state = (
        query_zero,
        jnp.zeros((seq_count, full_rows, heads_here * HEAD_DIM), jnp.float32),
        jnp.zeros((seq_count, full_rows, heads_here * HEAD_DIM), jnp.float32),
    )
    fold_shard_piece = (
        lax.all_gather(key_heads, "blk", axis=1, tiled=True),
        lax.all_gather(value_heads, "blk", axis=1, tiled=True),
    )
    piece_rows = fold_shard_piece[0].shape[1]
    fold_block_width = math.gcd(piece_rows, 512)

    def advance(block_index, loop_state):
        grad_query, grad_keys, grad_values = loop_state
        key_offset, key_part, value_part, allowed, scores = key_block(
            fold_shard_piece, block_index, fold_block_width
        )
        probs, grad_scores = score_grads(
            scores, allowed, grad_attn_split, value_part, log_total, row_delta
        )
        grad_query = (
            grad_query
            + jnp.einsum(
                "shqk,skhd->sqhd", grad_scores, key_part, preferred_element_type=jnp.float32
            )
            * score_scale
        )
        key_term = (
            jnp.einsum(
                "shqk,sqhd->skhd", grad_scores, query_split, preferred_element_type=jnp.float32
            )
            * score_scale
        )
        value_term = jnp.einsum(
            "shqk,sqhd->skhd",
            probs.astype(jnp.bfloat16),
            grad_attn_split,
            preferred_element_type=jnp.float32,
        )
        grad_keys = lax.dynamic_update_slice_in_dim(
            grad_keys,
            key_term.reshape(seq_count, fold_block_width, heads_here * HEAD_DIM),
            key_offset,
            1,
        )
        grad_values = lax.dynamic_update_slice_in_dim(
            grad_values,
            value_term.reshape(seq_count, fold_block_width, heads_here * HEAD_DIM),
            key_offset,
            1,
        )
        return (grad_query, grad_keys, grad_values)

    back_out = lax.fori_loop(0, piece_rows // fold_block_width, advance, back_state)
    grad_query = back_out[0]
    key_share, value_share = (
        lax.psum_scatter(
            back_out[1].astype(jnp.bfloat16), "blk", scatter_dimension=1, tiled=True
        ).astype(jnp.float32),
        lax.psum_scatter(
            back_out[2].astype(jnp.bfloat16), "blk", scatter_dimension=1, tiled=True
        ).astype(jnp.float32),
    )
    query_send = grad_query.reshape(seq_count, block_rows, heads_here * HEAD_DIM).astype(
        jnp.bfloat16
    )
    query_back, key_back, value_back = (
        lax.all_to_all(query_send, "head", split_axis=1, concat_axis=2, tiled=True),
        lax.all_to_all(
            key_share.astype(jnp.bfloat16), "head", split_axis=1, concat_axis=2, tiled=True
        ),
        lax.all_to_all(
            value_share.astype(jnp.bfloat16), "head", split_axis=1, concat_axis=2, tiled=True
        ),
    )
    query_back = query_back.reshape(-1, model_width)
    key_back = key_back.reshape(-1, model_width)
    value_back = value_back.reshape(-1, model_width)
    grad_w_query = left_dot(flat_rows, query_back)
    grad_w_key = left_dot(flat_rows, key_back)
    grad_w_value = left_dot(flat_rows, value_back)
    grad_b_query = jnp.sum(query_back.astype(jnp.float32), axis=0)
    grad_b_value = jnp.sum(value_back.astype(jnp.float32), axis=0)
    grad_input = (
        grad_resid_one
        + right_dot(query_back, w_query)
        + right_dot(key_back, w_key)
        + right_dot(value_back, w_value)
    )
    grad_input = grad_input.reshape(layer_input.shape)
    shares_all = (
        lax.psum_scatter(grad_w_query, ("seq", "blk", "head"), scatter_dimension=0, tiled=True),
        lax.psum_scatter(grad_w_key, ("seq", "blk", "head"), scatter_dimension=0, tiled=True),
        lax.psum_scatter(grad_w_value, ("seq", "blk", "head"), scatter_dimension=0, tiled=True),
        lax.psum_scatter(grad_w_output, ("seq", "blk", "head"), scatter_dimension=0, tiled=True),
        lax.psum_scatter(grad_w_expand, ("seq", "blk", "head"), scatter_dimension=0, tiled=True),
        lax.psum_scatter(grad_w_reduce, ("seq", "blk", "head"), scatter_dimension=0, tiled=True),
        lax.psum_scatter(grad_b_query, ("seq", "blk", "head"), scatter_dimension=0, tiled=True),
        lax.psum_scatter(grad_b_value, ("seq", "blk", "head"), scatter_dimension=0, tiled=True),
        lax.psum_scatter(grad_b_output, ("seq", "blk", "head"), scatter_dimension=0, tiled=True),
        lax.psum_scatter(grad_b_expand, ("seq", "blk", "head"), scatter_dimension=0, tiled=True),
        lax.psum_scatter(grad_b_reduce, ("seq", "blk", "head"), scatter_dimension=0, tiled=True),
        lax.psum_scatter(grad_gain_one, ("seq", "blk", "head"), scatter_dimension=0, tiled=True),
        lax.psum_scatter(grad_shift_one, ("seq", "blk", "head"), scatter_dimension=0, tiled=True),
        lax.psum_scatter(grad_gain_two, ("seq", "blk", "head"), scatter_dimension=0, tiled=True),
        lax.psum_scatter(grad_shift_two, ("seq", "blk", "head"), scatter_dimension=0, tiled=True),
    )
    return (
        layer_output,
        grad_input,
        shares_all[0],
        shares_all[1],
        shares_all[2],
        shares_all[3],
        shares_all[4],
        shares_all[5],
        shares_all[6],
        shares_all[7],
        shares_all[8],
        shares_all[9],
        shares_all[10],
        shares_all[11],
        shares_all[12],
        shares_all[13],
        shares_all[14],
    )


def solution(mesh):
    placed = (
        P("seq", ("blk", "head"), None),
        P(("seq", "blk", "head"), None),
        P(("seq", "blk", "head"), None),
        P(("seq", "blk", "head"), None),
        P(("seq", "blk", "head"), None),
        P(("seq", "blk", "head"), None),
        P(("seq", "blk", "head"), None),
        P(("seq", "blk", "head")),
        P(("seq", "blk", "head")),
        P(("seq", "blk", "head")),
        P(("seq", "blk", "head")),
        P(("seq", "blk", "head")),
        P(("seq", "blk", "head")),
        P(("seq", "blk", "head")),
        P(("seq", "blk", "head")),
        P(("seq", "blk", "head")),
        P("seq", ("blk", "head"), None),
        P("seq", None),
    )
    return jax.shard_map(
        shards,
        mesh=mesh,
        in_specs=placed,
        out_specs=(
            P("seq", ("blk", "head"), None),
            P("seq", ("blk", "head"), None),
            P(("seq", "blk", "head"), None),
            P(("seq", "blk", "head"), None),
            P(("seq", "blk", "head"), None),
            P(("seq", "blk", "head"), None),
            P(("seq", "blk", "head"), None),
            P(("seq", "blk", "head"), None),
            P(("seq", "blk", "head")),
            P(("seq", "blk", "head")),
            P(("seq", "blk", "head")),
            P(("seq", "blk", "head")),
            P(("seq", "blk", "head")),
            P(("seq", "blk", "head")),
            P(("seq", "blk", "head")),
            P(("seq", "blk", "head")),
            P(("seq", "blk", "head")),
        ),
        check_vma=False,
    )
```

profile of v0, /device:TPU:0, one launch (start us, length us, event | category | flops | bytes accessed | tf_op | source)
XLA Modules:
  0.0 3207.6 jit_solution(9315251633225668228)
XLA Ops:
  16.2 42.4 %all-reduce.20 = (bf16[1024]{0:T(1024)(128)(2,1)S(1)}, bf16[1024]{0:T(1024)(128)(2,1)S(1)}, bf16[1024]{0:T(1024)(128)(2,1)}, bf16[1024]{0:T(1024)(128)(2,1)}, bf...) all-reduce(bf16[1024]{0:T(1024)(128)(2,1)S(1)} %dynamic-update-slic, ...), channel_id=1, replica_groups=mesh['seq'=2,'blk'=4,'head'=4] {'seq','blk','head'}, use_global_device_ids=true, to_apply=%add | all-reduce | flops 8192 | bytes 32768
  83.5 17.9 all_to_all.126
  104.2 24.2 all-gather.10.cloned.1.call-done
  140.9 18.0 all_to_all.127
  164.4 22.1 all-gather.14.cloned.1.call-done
  221.4 46.3 %all-gather.18.cloned.1.call-done = bf16[1,8192,256]{2,1,0:T(8,128)(2,1)} async-done(((bf16[1,2048,256]{2,1,0:T(8,128)(2,1)}), bf16[1,8192,256]{2,1,0:T(8,128)(2,1)}) %all-gather.18.cloned.1.call-update) | async-done | bytes 4194320 | tf_op jit(solution)/shard_map/all_gather | solution.py:145
  274.0 74.9 %all-gather.12.cloned.1.call-done = bf16[1,8192,256]{2,1,0:T(8,128)(2,1)} async-done(((bf16[1,2048,256]{2,1,0:T(8,128)(2,1)}), bf16[1,8192,256]{2,1,0:T(8,128)(2,1)}) %all-gather.12.cloned.1.call-update) | async-done | bytes 4194320 | tf_op jit(solution)/shard_map/all_gather | solution.py:144
  355.4 431.2 %while.40 = (s32[]{:T(128)}, f32[1,4,2048]{2,1,0:T(4,128)S(1)}, f32[1,4,2048]{2,1,0:T(4,128)S(1)}, f32[1,4,2048,64]{2,3,1,0:T(8,128)}, s32[1,2048]{1,0:T(1,128)S...) while((s32[]{:T(128)}, f32[1,4,2048]{2,1,0:T(4,128)S(1)}, ...), condition=%wide.region_6.7_spmd.clone, body=%wide.region_2.6_spmd.clone.sunk | while | flops 1130989568 | bytes 128995688 | solution.py:168
  813.4 43.1 %all-gather = bf16[32,1,128]{2,1,0:T(2,128)(2,1)S(1)} all-gather(bf16[1,1,128]{2,1,0:T(2,128)(2,1)S(1)} %bitcast.380), channel_id=1, replica_groups=mesh['seq'=2,'blk'=4,'head'=4] {'seq','blk','head'}, dimensions={0}, use_global_device_ids=true | all-gather | bytes 8448 | tf_op jit(solution)/shard_map/all_gather | solution.py:92
  892.8 14.3 convert_reduce_fusion.2
  943.0 13.8 all-to-all-done.4
  970.5 699.4 %while.41 = (s32[]{:T(128)}, f32[1,2048,4,64]{1,3,2,0:T(8,128)}, bf16[1,8192,256]{1,2,0:T(8,128)(2,1)}, bf16[1,8192,256]{1,2,0:T(8,128)(2,1)}, bf16[1,8192,256]{...) while((s32[]{:T(128)}, f32[1,2048,4,64]{1,3,2,0:T(8,128)}, ...), condition=%wide.region_18.19_spmd.clone, body=%wide.region_16.18_spmd.clone.sunk | while | flops 2729232384 | bytes 160813552 | solution.py:265
  1669.9 17.8 copy.215
  1687.7 17.9 copy.217
  1724.8 16.9 all_to_all.128
  1754.6 511.5 %all-reduce.24.cloned.1.call-done = (bf16[1,8192,256]{2,0,1:T(2,128)(2,1)}, bf16[1,8192,256]{2,0,1:T(2,128)(2,1)}) async-done(((bf16[1,8192,256]{2,0,1:T(2,128)(2,1)}, bf16[1,8192,256]{2,0,1:T(2,128)(2,1)}), (bf16[1,8192,256]{2,0,1:T(2,128)(2,1)}, bf16[1,8192,256]{2,0,1:T(2,128)(2,1)})) %all-reduce.24.cloned.1.call-update) | async-done | bytes 8388624
  2286.5 22.8 all_to_all.129
  2339.6 23.0 all_to_all.130
  2406.3 42.3 %all-reduce.19 = (f32[1024]{0:T(1024)S(1)}, f32[1024]{0:T(1024)S(1)}, f32[1024]{0:T(1024)S(1)}, f32[4096]{0:T(1024)S(1)}, f32[1024]{0:T(1024)S(1)}, /*index=5*/f...) all-reduce(f32[1024]{0:T(1024)S(1)} %bitcast.376, ...), channel_id=10, replica_groups=mesh['seq'=2,'blk'=4,'head'=4] {'seq','blk','head'}, use_global_device_ids=true, to_apply=%region_28.29.clone | all-reduce | flops 12288 | bytes 98304
  2459.9 90.0 %reduce-scatter.19.cloned.1.call-done = f32[32,1024]{1,0:T(8,128)} async-done(((f32[1024,1024]{1,0:T(8,128)}), f32[32,1024]{1,0:T(8,128)}) %reduce-scatter.19.cloned.1.call-update) | async-done | bytes 131088
  2549.9 140.2 %reduce-scatter.23.cloned.1.call-done = f32[32,1024]{1,0:T(8,128)} async-done(((f32[1024,1024]{1,0:T(8,128)}), f32[32,1024]{1,0:T(8,128)}) %reduce-scatter.23.cloned.1.call-update) | async-done | bytes 131088
  2690.1 140.2 %reduce-scatter.21.cloned.1.call-done = f32[32,1024]{1,0:T(8,128)} async-done(((f32[1024,1024]{1,0:T(8,128)}), f32[32,1024]{1,0:T(8,128)}) %reduce-scatter.21.cloned.1.call-update) | async-done | bytes 131088
  2830.4 183.0 %reduce-scatter.15.cloned.1.call-done = f32[32,4096]{1,0:T(8,128)} async-done(((f32[1024,4096]{1,0:T(8,128)}), f32[32,4096]{1,0:T(8,128)}) %reduce-scatter.15.cloned.1.call-update) | async-done | bytes 524304 | tf_op jit(solution)/shard_map/reduce_scatter | solution.py:307
  3013.4 187.3 %reduce-scatter.17.cloned.1.call-done = f32[128,1024]{1,0:T(8,128)} async-done(((f32[4096,1024]{1,0:T(8,128)}), f32[128,1024]{1,0:T(8,128)}) %reduce-scatter.17.cloned.1.call-update) | async-done | bytes 524304 | tf_op jit(solution)/shard_map/reduce_scatter | solution.py:308
  (862 shorter events, 1479.1 us)
Async XLA Ops:
  7.2 62.9 %all-gather.16.cloned.1.call-start = ((), (), s32[]{:S(2)}) async-start(), calls=%async_computation.17 | async-start | bytes 2162688 | tf_op jit(solution)/shard_map/all_gather | solution.py:85
  7.9 120.5 %all-gather.10.cloned.1.call-start = ((), (), s32[]{:S(2)}) async-start(), calls=%async_computation.14 | async-start | bytes 2162688 | tf_op jit(solution)/shard_map/all_gather | solution.py:84
  8.7 177.9 %all-gather.14.cloned.1.call-start = ((), (), s32[]{:S(2)}) async-start(), calls=%async_computation.16 | async-start | bytes 2162688 | tf_op jit(solution)/shard_map/all_gather | solution.py:83
  9.4 258.3 %all-gather.18.cloned.1.call-start = ((), (), s32[]{:S(2)}) async-start(), calls=%async_computation.18 | async-start | bytes 5242880 | tf_op jit(solution)/shard_map/all_gather | solution.py:145
  104.0 245.0 %all-gather.12.cloned.1.call-start = ((), (), s32[]{:S(2)}) async-start(), calls=%async_computation.15 | async-start | bytes 5242880 | tf_op jit(solution)/shard_map/all_gather | solution.py:144
  161.5 702.4 %all-gather.20.cloned.1.call-start = ((), (), s32[]{:S(2)}) async-start(), calls=%async_computation.19 | async-start | bytes 2162688 | tf_op jit(solution)/shard_map/all_gather | solution.py:86
  162.1 705.8 %all-gather.22.cloned.1.call-start = ((), (), s32[]{:S(2)}) async-start(), calls=%async_computation.20 | async-start | bytes 8650752 | tf_op jit(solution)/shard_map/all_gather | solution.py:87
  162.8 715.9 %all-gather.24.cloned.1.call-start = ((), (), s32[]{:S(2)}) async-start(), calls=%async_computation.21 | async-start | bytes 8650752 | tf_op jit(solution)/shard_map/all_gather | solution.py:88
  200.4 18.1 all-to-all-start.1
  274.0 81.3 %copy-start.17 = (f32[1,4,2048]{2,1,0:T(4,128)S(1)}, f32[1,4,2048]{2,1,0:T(4,128)}, u32[]{:S(2)}) copy-start(f32[1,4,2048]{2,1,0:T(4,128)} %custom-call) | copy-start | bytes 98308
  274.0 81.4 %copy-start.18 = (f32[1,4,2048]{2,1,0:T(4,128)S(1)}, f32[1,4,2048]{2,1,0:T(4,128)}, u32[]{:S(2)}) copy-start(f32[1,4,2048]{2,1,0:T(4,128)} %custom-call.1) | copy-start | bytes 98308
  805.5 51.1 %copy-start.51 = (bf16[1024]{0:T(1024)(128)(2,1)S(1)}, bf16[1024]{0:T(1024)(128)(2,1)}, u32[]{:S(2)}) copy-start(bf16[1024]{0:T(1024)(128)(2,1)} %get-tuple-element.862) | copy-start | bytes 6148
  805.5 51.1 %copy-start.50 = (bf16[1024]{0:T(1024)(128)(2,1)S(1)}, bf16[1024]{0:T(1024)(128)(2,1)}, u32[]{:S(2)}) copy-start(bf16[1024]{0:T(1024)(128)(2,1)} %get-tuple-element.861) | copy-start | bytes 6148
  809.1 48.4 %all-to-all-start.3 = ((bf16[4,2,65536]{2,1,0:T(2,128)(2,1)}), bf16[4,2,65536]{2,1,0:T(2,128)(2,1)}, u32[]{:S(2)}, u32[]{:S(2)}) async-start(bf16[4,2,65536]{2,1,0:T(2,128)(2,1)} %reshape.878), calls=%async_computation.3 | async-start | bytes 2097152 | tf_op jit(solution)/shard_map/all_to_all | solution.py:178
  813.4 102.0 %copy-start.42 = (f32[1024]{0:T(1024)}, f32[1024]{0:T(1024)S(1)}, u32[]{:S(2)}) copy-start(f32[1024]{0:T(1024)S(1)} %convert_element_type.228) | copy-start | bytes 12292
  813.4 65.4 %copy-start.48 = (f32[1024]{0:T(1024)}, f32[1024]{0:T(1024)S(1)}, u32[]{:S(2)}) copy-start(f32[1024]{0:T(1024)S(1)} %convert_element_type.229) | copy-start | bytes 12292
  938.1 18.8 all-to-all-start.4
  942.3 1323.7 %all-reduce.24.cloned.1.call-start = ((), (), s32[]{:S(2)}) async-start(), calls=%async_computation.28 | async-start | bytes 33554432
  1705.6 754.3 %reduce-scatter.13.cloned.1.call-start = ((), (), s32[]{:S(2)}) async-start(), calls=%async_computation.22 | async-start | bytes 4325376 | tf_op jit(solution)/shard_map/reduce_scatter | solution.py:306
  1710.3 839.6 %reduce-scatter.19.cloned.1.call-start = ((), (), s32[]{:S(2)}) async-start(), calls=%async_computation.25 | async-start | bytes 4325376
  1752.7 937.4 %reduce-scatter.23.cloned.1.call-start = ((), (), s32[]{:S(2)}) async-start(), calls=%async_computation.27 | async-start | bytes 4325376
  2324.3 506.1 %reduce-scatter.21.cloned.1.call-start = ((), (), s32[]{:S(2)}) async-start(), calls=%async_computation.26 | async-start | bytes 4325376
  2376.6 636.8 %reduce-scatter.15.cloned.1.call-start = ((), (), s32[]{:S(2)}) async-start(), calls=%async_computation.23 | async-start | bytes 17301504 | tf_op jit(solution)/shard_map/reduce_scatter | solution.py:307
  2388.7 812.0 %reduce-scatter.17.cloned.1.call-start = ((), (), s32[]{:S(2)}) async-start(), calls=%async_computation.24 | async-start | bytes 17301504 | tf_op jit(solution)/shard_map/reduce_scatter | solution.py:308
  (131 other events, 1304.8 us)
Sparse Core Ops, SparseCore 0:
  10.9 59.1 all-gather.15
  73.0 55.3 all-gather.9
  131.3 55.2 all-gather.13
  188.0 79.6 all-gather.17
  269.6 79.2 all-gather.11
  351.7 54.9 all-gather.19
  409.6 76.4 all-gather.21
  489.0 76.1 all-gather.23
  1705.7 560.2 all-reduce.23
  2268.7 140.2 reduce-scatter.12
  2411.9 137.9 reduce-scatter.18
  2552.6 137.4 reduce-scatter.22
  2693.0 137.3 reduce-scatter.20
  2833.1 180.2 reduce-scatter.14
  3016.1 184.5 reduce-scatter.16
where the time goes:
time: 3220 us; the launch traced here: 3210 us
  waiting for transfers between devices  1460 us (45%)
  matrix products  955 us (30%)
  local copies, waits for them, and re-layouts  302 us (9%)
  other arithmetic  229 us (7%)
  blocking collectives  226 us (7%)
    unnamed x19, waiting for transfers between devices  886 us
    reduce_scatter x1, waiting for transfers between devices, shards(): lax.psum_scatter(grad_w_reduce, ('seq', 'blk', 'head'), scatter_dimension...  187 us
    reduce_scatter x1, waiting for transfers between devices, shards(): lax.psum_scatter(grad_w_expand, ('seq', 'blk', 'head'), scatter_dimension...  183 us
    dot_general x16, matrix products, advance(): jnp.einsum('shqk,skhd->shqd', weights.astype(jnp.bfloat16), value_part, p...  172 us
    dot_general x16, matrix products, advance(): jnp.einsum('shqk,sqhd->skhd', probs.astype(jnp.bfloat16), grad_attn_split...  158 us
    dot_general x32, matrix products, key_block(): jnp.einsum('sqhd,skhd->shqk', query_split, key_part, preferred_element_ty...  158 us
    dot_general x16, matrix products, score_grads(): jnp.einsum('sqhd,skhd->shqk', grad_part, value_part, preferred_element_ty...  148 us
    dot_general x16, matrix products, advance(): jnp.einsum('shqk,skhd->sqhd', grad_scores, key_part, preferred_element_ty...  110 us
  transfers between devices with their start and end apart: 18, of which 13 were waited for; matrix products, arithmetic and copies ran while one was open for 20% of the time, Pallas kernels for 0%

commit v1 on v0

--- a/solution.py
+++ b/solution.py
@@ -1,8 +1,11 @@
+import functools
 import math
 
 import jax
 import jax.numpy as jnp
 from jax import lax
+from jax.experimental import pallas as pl
+from jax.experimental.pallas import tpu as pltpu
 from jax.sharding import PartitionSpec as P
 
 HEADS = 16
@@ -54,7 +57,7 @@
     return (probs, grad_scores)
 
 
-def shards(
+def shards_general(
     layer_input,
     weight_query,
     weight_key,
@@ -337,6 +340,370 @@
     )
 
 
+LOG2E = 1.4426950408889634
+RR=(((1,),(1,)),((),()))
+def fwd_kernel(bq,ck,q_ref,k_ref,v_ref,sc_ref,sr_ref,p_ref,pt_ref,o_ref,l_ref,kk,vv,s0,s1,m0,m1):
+    g=pl.program_id(0); ng=pl.num_programs(0)
+    L=q_ref.shape[1]; Lm=p_ref.shape[1]; T=L-Lm; nc=Lm//ck
+    nb=Lm//bq
+    c=LOG2E*HEAD_DIM**-0.5
+    def qblk(start):
+        q=q_ref[:,pl.ds(pl.multiple_of(start,bq),bq)].astype(jnp.float32)*c
+        hi=q.astype(jnp.bfloat16).astype(jnp.float32)
+        return jnp.concatenate([hi,q-hi],0).T.astype(jnp.bfloat16)
+    def phase1(qb,s,j,mx):
+        r=jnp.dot(qb,kk[:,j*ck:(j+1)*ck],preferred_element_type=jnp.float32)
+        s[:,j*ck:(j+1)*ck]=r
+        for t in range(ck//128):
+            x=r[:,t*128:(t+1)*128]
+            mx=x if mx is None else jnp.maximum(mx,x)
+        return mx
+    def setm(m,mx):
+        m[...]=jnp.broadcast_to(jnp.max(mx,axis=1,keepdims=True),m.shape)
+    def phase2(s,m,j,row,acc):
+        p=jnp.exp2(s[:,j*ck:(j+1)*ck]-m[:,:1]).astype(jnp.bfloat16)
+        p_ref[row:row+bq,j*ck:(j+1)*ck]=p
+        r=lax.dot_general(vv[:,j*ck:(j+1)*ck],p,RR,preferred_element_type=jnp.float32)
+        return r if acc is None else acc+r
+    def finish(acc,start):
+        il=1.0/acc[HEAD_DIM:HEAD_DIM+1]
+        o_ref[:,pl.ds(pl.multiple_of(start,bq),bq)]=(acc[:HEAD_DIM]*il).astype(jnp.bfloat16)
+        l_ref[:,pl.ds(pl.multiple_of(start,bq),bq)]=jnp.broadcast_to(il,(8,bq))
+    @pl.when(g==0)
+    def _():
+        kk[0:HEAD_DIM,:]=k_ref[...]; kk[HEAD_DIM:,:]=k_ref[...]
+        vv[0:HEAD_DIM,:]=v_ref[...]
+        vv[HEAD_DIM:,:]=(lax.broadcasted_iota(jnp.int32,(16,L),0)==0).astype(jnp.float32).astype(jnp.bfloat16)
+        qb=qblk(0); mx=None
+        for j in range(nc): mx=phase1(qb,s0,j,mx)
+        setm(m0,mx)
+    for h,(sa,ma,sb,mb) in enumerate(((s0,m0,s1,m1),(s1,m1,s0,m0))):
+        nxt=jnp.minimum(2*g+h+1,nb-1)*bq
+        qb=qblk(nxt); acc=None; mx=None
+        for j in range(nc):
+            acc=phase2(sa,ma,j,h*bq,acc)
+            mx=phase1(qb,sb,j,mx)
+        setm(mb,mx)
+        finish(acc,(2*g+h)*bq)
+    @pl.when(g==ng-1)
+    def _():
+        for i in range(T//bq):
+            qb=qblk(Lm+i*bq)
+            s=jnp.dot(qb,kk[:,Lm:],preferred_element_type=jnp.float32)
+            s=jnp.where(sc_ref[i*bq:(i+1)*bq,:1]==sr_ref[:1,:],s,-1e30)
+            m=jnp.max(s,axis=1,keepdims=True)
+            p=jnp.exp2(s-m).astype(jnp.bfloat16)
+            pt_ref[i*bq:(i+1)*bq,:]=p
+            finish(lax.dot_general(vv[:,Lm:],p,RR,preferred_element_type=jnp.float32),Lm+i*bq)
+
+def attn_fwd(qT,kT,vT,seg,Lm,bq=256,ck=1024):
+    L=qT.shape[1]; T=L-Lm
+    sc=jnp.broadcast_to(seg[:,None],(T,128)); sr=jnp.broadcast_to(seg[None,:],(8,T))
+    full=lambda s: pl.BlockSpec(s,lambda g:(0,)*len(s))
+    ng=Lm//bq//2
+    return pl.pallas_call(functools.partial(fwd_kernel,bq,ck),
+        grid=(ng,),
+        in_specs=[full((HEAD_DIM,L))]*3+[full((T,128)),full((8,T))],
+        out_specs=[pl.BlockSpec((2*bq,Lm),lambda g:(g,0)),full((T,T)),full((HEAD_DIM,L)),full((8,L))],
+        out_shape=[jax.ShapeDtypeStruct((Lm,Lm),jnp.bfloat16),jax.ShapeDtypeStruct((T,T),jnp.bfloat16),jax.ShapeDtypeStruct((HEAD_DIM,L),jnp.bfloat16),jax.ShapeDtypeStruct((8,L),jnp.float32)],
+        scratch_shapes=[pltpu.VMEM((2*HEAD_DIM,L),jnp.bfloat16),pltpu.VMEM((HEAD_DIM+16,L),jnp.bfloat16),pltpu.VMEM((bq,Lm),jnp.float32),pltpu.VMEM((bq,Lm),jnp.float32),pltpu.VMEM((bq,128),jnp.float32),pltpu.VMEM((bq,128),jnp.float32)],
+        compiler_params=pltpu.CompilerParams(vmem_limit_bytes=60*2**20),
+        cost_estimate=pl.CostEstimate(flops=4*Lm*Lm*256,bytes_accessed=2*Lm*Lm,transcendentals=Lm*Lm),
+        name="attn_fwd")(qT,kT,vT,sc,sr)
+
+def bwd_kernel(bq,ck,p_ref,pt_ref,q_ref,k_ref,v_ref,o_ref,do_ref,l_ref,dq_ref,dk_ref,dv_ref,vv,dka,dva):
+    g=pl.program_id(0); ng=pl.num_programs(0)
+    L=q_ref.shape[1]; Lm=p_ref.shape[1]; T=L-Lm; nc=Lm//ck
+    @pl.when(g==0)
+    def _():
+        vv[0:HEAD_DIM,:]=v_ref[...]
+        vv[HEAD_DIM:,:]=(lax.broadcasted_iota(jnp.int32,(16,L),0)<2).astype(jnp.float32).astype(jnp.bfloat16)
+        dka[...]=jnp.zeros_like(dka); dva[...]=jnp.zeros_like(dva)
+    def prep(start,n):
+        sl=pl.ds(pl.multiple_of(start,n),n)
+        do=do_ref[:,sl].astype(jnp.float32); il=l_ref[:1,sl]
+        dl=-jnp.sum(do*o_ref[:,sl].astype(jnp.float32),axis=0,keepdims=True)*il
+        dh=dl.astype(jnp.bfloat16).astype(jnp.float32)
+        row=lax.broadcasted_iota(jnp.int32,(16,n),0)
+        extra=jnp.where(row==0,dh,jnp.where(row==1,dl-dh,0.0))
+        d=do*il
+        A=jnp.concatenate([d,extra],0).T.astype(jnp.bfloat16)
+        return A,d.astype(jnp.bfloat16),q_ref[:,sl]
+    def chunk(A,d,q,p,kc,vc,dq):
+        dp=jnp.dot(A,vc,preferred_element_type=jnp.float32)
+        ds=(p.astype(jnp.float32)*dp).astype(jnp.bfloat16)
+        dv=jnp.dot(d,p,preferred_element_type=jnp.float32)
+        dk=jnp.dot(q,ds,preferred_element_type=jnp.float32)
+        r=lax.dot_general(kc,ds,RR,preferred_element_type=jnp.float32)
+        return (r if dq is None else dq+r),dk,dv
+    A,d,q=prep(g*bq,bq); dq=None
+    for j in range(nc):
+        sl=slice(j*ck,(j+1)*ck)
+        dq,dk,dv=chunk(A,d,q,p_ref[:,sl],k_ref[:,sl],vv[:,sl],dq)
+        dka[:,sl]+=dk; dva[:,sl]+=dv
+    dq_ref[:,pl.ds(pl.multiple_of(g*bq,bq),bq)]=(dq*HEAD_DIM**-0.5).astype(jnp.bfloat16)
+    @pl.when(g==ng-1)
+    def _():
+        for i in range(T//bq):
+            A,d,q=prep(Lm+i*bq,bq)
+            dq,dk,dv=chunk(A,d,q,pt_ref[i*bq:(i+1)*bq,:],k_ref[:,Lm:],vv[:,Lm:],None)
+            dka[:,Lm:]+=dk; dva[:,Lm:]+=dv
+            dq_ref[:,Lm+i*bq:Lm+(i+1)*bq]=(dq*HEAD_DIM**-0.5).astype(jnp.bfloat16)
+        dk_ref[...]=(dka[...]*HEAD_DIM**-0.5).astype(jnp.bfloat16)
+        dv_ref[...]=dva[...].astype(jnp.bfloat16)
+
+def attn_bwd(P,Pt,qT,kT,vT,oT,doT,il,Lm,bq=512,ck=1024):
+    L=qT.shape[1]; T=L-Lm
+    full=lambda s: pl.BlockSpec(s,lambda g:(0,)*len(s))
+    f=jax.ShapeDtypeStruct((HEAD_DIM,L),jnp.bfloat16)
+    return pl.pallas_call(functools.partial(bwd_kernel,bq,ck),
+        grid=(Lm//bq,),
+        in_specs=[pl.BlockSpec((bq,Lm),lambda g:(g,0)),full((T,T))]+[full((HEAD_DIM,L))]*5+[full((8,L))],
+        out_specs=[full((HEAD_DIM,L))]*3,
+        out_shape=[f]*3,
+        scratch_shapes=[pltpu.VMEM((HEAD_DIM+16,L),jnp.bfloat16),pltpu.VMEM((HEAD_DIM,L),jnp.float32),pltpu.VMEM((HEAD_DIM,L),jnp.float32)],
+        compiler_params=pltpu.CompilerParams(vmem_limit_bytes=60*2**20),
+        cost_estimate=pl.CostEstimate(flops=8*Lm*Lm*256,bytes_accessed=2*Lm*Lm,transcendentals=0),
+        name="attn_bwd")(P,Pt,qT,kT,vT,oT,doT,il)
+
+
+MESH = pl.DeviceIdType.MESH
+GROUP = ("blk", "head")
+EVERY = ("seq", "blk", "head")
+
+
+def greet_group(me, count, heads):
+    barrier = pltpu.get_barrier_semaphore()
+    for step in range(1, count):
+        peer = lax.rem(me + step, count)
+        pl.semaphore_signal(
+            barrier,
+            inc=1,
+            device_id={"blk": peer // heads, "head": lax.rem(peer, heads)},
+            device_id_type=MESH,
+        )
+    pl.semaphore_wait(barrier, count - 1)
+
+
+def swap_kernel(to_heads, blks, heads, in_ref, out_ref, send_sem, recv_sem, own_sem):
+    count = blks * heads
+    me = lax.axis_index("blk") * heads + lax.axis_index("head")
+    greet_group(me, count, heads)
+    if to_heads:
+        rows = in_ref.shape[2]
+        width = in_ref.shape[3]
+        take = lambda owner: in_ref.at[:, owner]
+        place = lambda source: out_ref.at[
+            :, :, pl.ds(pl.multiple_of(source * width, width), width)
+        ]
+    else:
+        rows = in_ref.shape[1]
+        width = in_ref.shape[2] // count
+        take = lambda owner: in_ref.at[:, :, pl.ds(pl.multiple_of(owner * width, width), width)]
+        place = lambda source: out_ref.at[:, source]
+    own = pltpu.make_async_copy(take(me), place(me), own_sem)
+    own.start()
+    copies = []
+    for step in range(1, count):
+        peer = lax.rem(me + step, count)
+        copy = pltpu.make_async_remote_copy(
+            src_ref=take(peer),
+            dst_ref=place(me),
+            send_sem=send_sem.at[step],
+            recv_sem=recv_sem.at[step],
+            device_id={"blk": peer // heads, "head": lax.rem(peer, heads)},
+            device_id_type=MESH,
+        )
+        copy.start()
+        copies.append(copy)
+    own.wait()
+    for copy in copies:
+        copy.wait_send()
+        copy.wait_recv()
+
+
+def swap(values, to_heads, collective_id):
+    blks, heads = lax.axis_size("blk"), lax.axis_size("head")
+    count = blks * heads
+    parts = values.shape[0]
+    if to_heads:
+        shape = (parts, values.shape[2], values.shape[3] * count)
+    else:
+        shape = (parts, count, values.shape[1], values.shape[2] // count)
+    return pl.pallas_call(
+        functools.partial(swap_kernel, to_heads, blks, heads),
+        out_shape=jax.ShapeDtypeStruct(shape, values.dtype),
+        in_specs=[pl.BlockSpec(memory_space=pl.ANY)],
+        out_specs=pl.BlockSpec(memory_space=pl.ANY),
+        scratch_shapes=[
+            pltpu.SemaphoreType.DMA((count,)),
+            pltpu.SemaphoreType.DMA((count,)),
+            pltpu.SemaphoreType.DMA,
+        ],
+        compiler_params=pltpu.CompilerParams(collective_id=collective_id, has_side_effects=True),
+        name="swap_to_heads" if to_heads else "swap_to_tokens",
+    )(values)
+
+
+def tail_segments(doc_lengths, first, rows):
+    return segment_ids(doc_lengths, first + lax.iota(jnp.int32, rows))
+
+
+def shards_heads(
+    layer_input,
+    weight_query,
+    weight_key,
+    weight_value,
+    weight_output,
+    weight_expand,
+    weight_reduce,
+    bias_query,
+    bias_value,
+    bias_output,
+    bias_expand,
+    bias_reduce,
+    first_gain,
+    first_shift,
+    second_gain,
+    second_shift,
+    cotangent,
+    doc_lengths,
+):
+    tok_rows, model_width = layer_input.shape[1:]
+    head_count = lax.axis_size("head")
+    blk_count = lax.axis_size("blk")
+    count = head_count * blk_count
+    seq_len = tok_rows * count
+    long_rows = seq_len - seq_len // blk_count // 2
+    flat_rows = layer_input.reshape(tok_rows, model_width)
+
+    vectors = (
+        bias_query,
+        bias_value,
+        bias_output,
+        bias_reduce,
+        first_gain,
+        first_shift,
+        second_gain,
+        second_shift,
+        bias_expand,
+    )
+    sizes = [vector.shape[0] for vector in vectors]
+    packed = lax.all_gather(jnp.concatenate(vectors), EVERY, axis=0).astype(jnp.float32)
+    whole, start = [], 0
+    for size in sizes:
+        whole.append(packed[:, start : start + size].reshape(-1))
+        start += size
+    b_query, b_value, b_output, b_reduce, gain_one, shift_one, gain_two, shift_two, b_expand = whole
+
+    w_qkv = lax.all_gather(
+        jnp.concatenate((weight_query, weight_key, weight_value), axis=1), EVERY, axis=0, tiled=True
+    )
+    w_output = lax.all_gather(weight_output, EVERY, axis=0, tiled=True)
+    w_expand = lax.all_gather(weight_expand, EVERY, axis=0, tiled=True)
+    w_reduce = lax.all_gather(weight_reduce, EVERY, axis=0, tiled=True)
+
+    b_qkv = jnp.concatenate((b_query, jnp.zeros_like(b_query), b_value))
+    qkv = lax.dot_general(
+        w_qkv, flat_rows, (((0,), (1,)), ((), ())), preferred_element_type=jnp.float32
+    )
+    qkv = (qkv + b_qkv[:, None]).astype(jnp.bfloat16).reshape(3, HEADS, HEAD_DIM, tok_rows)
+    qkv = swap(qkv, True, 0)
+    query, key, value = qkv[0], qkv[1], qkv[2]
+    seg = tail_segments(doc_lengths, long_rows, seq_len - long_rows)[0]
+    probs, tail_probs, attn, inv_total = attn_fwd(query, key, value, seg, long_rows)
+    attn_flat = swap(attn[None], False, 1).reshape(model_width, tok_rows)
+
+    resid_one = flat_rows.astype(jnp.float32) + left_dot(attn_flat, w_output) + b_output
+    normed_one, norm_one_pull = jax.vjp(layer_norm, resid_one, gain_one, shift_one)
+    normed_low = normed_one.astype(jnp.bfloat16)
+    pre_act = plain_dot(normed_low, w_expand) + b_expand
+    hidden_f32, gelu_pull = jax.vjp(gelu_curve, pre_act)
+    hidden = hidden_f32.astype(jnp.bfloat16)
+    resid_two = normed_one + plain_dot(hidden, w_reduce) + b_reduce
+    result, norm_two_pull = jax.vjp(layer_norm, resid_two, gain_two, shift_two)
+    layer_output = result.astype(jnp.bfloat16).reshape(layer_input.shape)
+    tok_first = (lax.axis_index("blk") * head_count + lax.axis_index("head")) * tok_rows
+    tok_seg = segment_ids(doc_lengths, tok_first + lax.iota(jnp.int32, tok_rows))
+    live = (tok_seg > 0).astype(jnp.float32)
+    grad_out = (cotangent.astype(jnp.float32) * live[..., None]).reshape(-1, model_width)
+    grad_resid_two, grad_gain_two, grad_shift_two = norm_two_pull(grad_out)
+    grad_ffn = grad_resid_two.astype(jnp.bfloat16)
+    grad_w_reduce = left_dot(hidden, grad_ffn)
+    grad_b_reduce = jnp.sum(grad_ffn.astype(jnp.float32), axis=0)
+    (grad_pre,) = gelu_pull(right_dot(grad_ffn, w_reduce))
+    grad_pre = grad_pre.astype(jnp.bfloat16)
+    grad_w_expand = left_dot(normed_low, grad_pre)
+    grad_b_expand = jnp.sum(grad_pre.astype(jnp.float32), axis=0)
+    grad_normed = grad_resid_two + right_dot(grad_pre, w_expand)
+    grad_resid_one, grad_gain_one, grad_shift_one = norm_one_pull(grad_normed)
+    grad_branch = grad_resid_one.astype(jnp.bfloat16)
+    grad_w_output = plain_dot(attn_flat, grad_branch)
+    grad_b_output = jnp.sum(grad_branch.astype(jnp.float32), axis=0)
+    grad_attn = right_dot(w_output, grad_branch).astype(jnp.bfloat16)
+    grad_attn = swap(grad_attn.reshape(1, HEADS, HEAD_DIM, tok_rows), True, 2)[0]
+
+    def share(grad):
+        return lax.psum_scatter(
+            grad.astype(jnp.bfloat16), EVERY, scatter_dimension=0, tiled=True
+        ).astype(jnp.float32)
+
+    grad_w_output = share(grad_w_output)
+    grad_w_expand = share(grad_w_expand)
+    grad_w_reduce = share(grad_w_reduce)
+
+    grad_qkv = attn_bwd(
+        probs, tail_probs, query, key, value, attn, grad_attn, inv_total, long_rows
+    )
+    grad_qkv = swap(jnp.stack(grad_qkv), False, 3).reshape(3 * model_width, tok_rows)
+    grad_w_qkv = lax.dot_general(
+        flat_rows, grad_qkv, (((0,), (1,)), ((), ())), preferred_element_type=jnp.float32
+    )
+    grad_w_qkv = share(grad_w_qkv)
+    grad_input = grad_resid_one + lax.dot_general(
+        grad_qkv, w_qkv, (((0,), (1,)), ((), ())), preferred_element_type=jnp.float32
+    )
+    grad_b_qkv = jnp.sum(grad_qkv.astype(jnp.float32), axis=1)
+
+    sums = (
+        grad_b_qkv[:model_width],
+        grad_b_qkv[2 * model_width :],
+        grad_b_output,
+        grad_b_reduce,
+        grad_gain_one,
+        grad_shift_one,
+        grad_gain_two,
+        grad_shift_two,
+        grad_b_expand,
+    )
+    sums = jnp.concatenate([term.reshape(-1, size) for term, size in zip(sums, sizes)], axis=1)
+    sums = lax.psum_scatter(sums, EVERY, scatter_dimension=0, tiled=True).reshape(-1)
+    parts, start = [], 0
+    for size in sizes:
+        parts.append(sums[start : start + size])
+        start += size
+    g_query, g_value, g_output, g_reduce, g_gain_one, g_shift_one, g_gain_two, g_shift_two, g_expand = parts
+    return (
+        layer_output,
+        grad_input.reshape(layer_input.shape),
+        grad_w_qkv[:, :model_width],
+        grad_w_qkv[:, model_width : 2 * model_width],
+        grad_w_qkv[:, 2 * model_width :],
+        grad_w_output,
+        grad_w_expand,
+        grad_w_reduce,
+        g_query,
+        g_value,
+        g_output,
+        g_expand,
+        g_reduce,
+        g_gain_one,
+        g_shift_one,
+        g_gain_two,
+        g_shift_two,
+    )
+
+
 def solution(mesh):
     placed = (
         P("seq", ("blk", "head"), None),
@@ -358,8 +725,10 @@
         P("seq", ("blk", "head"), None),
         P("seq", None),
     )
+    group = mesh.shape["blk"] * mesh.shape["head"]
+    body = shards_heads if group == HEADS else shards_general
     return jax.shard_map(
-        shards,
+        body,
         mesh=mesh,
         in_specs=placed,
         out_specs=(

time: 3220 us -> 1060 us (0.33)
  waiting for transfers between devices: 1460 us -> 418 us
  matrix products: 955 us -> 94 us
  Pallas kernels: 0 us -> 371 us
  local copies, waits for them, and re-layouts: 302 us -> 33.9 us
  other arithmetic: 229 us -> 21.8 us
  blocking collectives: 226 us -> 101 us
    unnamed x19 -> x9, waiting for transfers between devices: 886 us -> 41.5 us
    dot_general x112 -> x3, matrix products: 855 us -> 24.2 us  [the longest x1 8.66 us: shards_heads(): lax.dot_general(w_qkv, flat_rows, (((0,), (1,)), ((), ())), preferred_ele...]
    pallas_call x0 -> x6, Pallas kernels: none -> 371 us  [the longest x4 188 us: swap(): pl.pallas_call(functools.partial(swap_kernel, to_heads, blks, heads), out...]
    all_to_all x5 -> x0, blocking collectives: 98.5 us -> none  [the longest x1 23 us: shards(): lax.all_to_all(key_share.astype(jnp.bfloat16), 'head', split_axis=1, conc...]
    all_gather x8 -> x4, waiting for transfers between devices: 179 us -> 84.9 us  [the longest x1 65.3 us: shards_heads(): w_reduce = lax.all_gather(weight_reduce, EVERY, axis=0, tiled=True)]
    unnamed x173 -> x51, local copies, waits for them, and re-layouts: 96.7 us -> 17.1 us
    reduce_scatter x3, waiting for transfers between devices: 370 us -> 292 us  [share(): lax.psum_scatter(grad.astype(jnp.bfloat16), EVERY, scatter_dimension=0, t...]
    unnamed x13 -> x1, other arithmetic: 74.5 us -> 0.01 us
  transfers between devices with their start and end apart: 18 -> 8, of which waited for: 13 -> 5; matrix products, arithmetic and copies ran while one was open for 20% -> 9% of each run, Pallas kernels for 0% -> 33%
where the time goes in v1:
time: 1060 us; the launch traced here: 1050 us
  waiting for transfers between devices  418 us (39%)
  Pallas kernels  371 us (35%)
  blocking collectives  101 us (10%)
  matrix products  94 us (9%)
  local copies, waits for them, and re-layouts  33.9 us (3%)
  other arithmetic  21.8 us (2%)
  between operations  14.7 us (1%)
    reduce_scatter x3, waiting for transfers between devices, share(): lax.psum_scatter(grad.astype(jnp.bfloat16), EVERY, scatter_dimension=0, t...  292 us
    pallas_call x4, Pallas kernels, swap(): pl.pallas_call(functools.partial(swap_kernel, to_heads, blks, heads), out...  188 us
    pallas_call x1, Pallas kernels, attn_bwd(): pl.pallas_call(functools.partial(bwd_kernel, bq, ck), grid=(Lm // bq,), i...  104 us
    pallas_call x1, Pallas kernels, attn_fwd(): pl.pallas_call(functools.partial(fwd_kernel, bq, ck), grid=(ng,), in_spec...  78.9 us
    all_gather x1, waiting for transfers between devices, shards_heads(): w_reduce = lax.all_gather(weight_reduce, EVERY, axis=0, tiled=True)  65.3 us
    unnamed x1, blocking collectives  57.5 us
    all_gather x1, blocking collectives, shards_heads(): lax.all_gather(jnp.concatenate(vectors), EVERY, axis=0).astype(jnp.float32)  43.5 us
    unnamed x9, waiting for transfers between devices  41.5 us
  transfers between devices with their start and end apart: 8, of which 5 were waited for; matrix products, arithmetic and copies ran while one was open for 9% of the time, Pallas kernels for 33%

profile of v1, /device:TPU:0, one launch (start us, length us, event | category | flops | bytes accessed | tf_op | source)
XLA Modules:
  0.0 1054.7 jit_solution(12274668780789087087)
XLA Ops:
  11.0 6.1 concatenate.13
  17.1 43.5 %all-gather.1 = bf16[32,1,384]{2,1,0:T(2,128)(2,1)S(1)} all-gather(bf16[1,1,384]{2,1,0:T(2,128)(2,1)S(1)} %reshape.362), channel_id=2, replica_groups=mesh['seq'=2,'blk'=4,'head'=4] {'seq','blk','head'}, dimensions={0}, use_global_device_ids=true | all-gather | bytes 25344 | tf_op jit(solution)/shard_map/all_gather | solution.py:592
  64.3 19.5 %all-gather.7.cloned.1.call-done = bf16[1024,3072]{1,0:T(8,128)(2,1)} async-done(((bf16[32,3072]{1,0:T(8,128)(2,1)}), bf16[1024,3072]{1,0:T(8,128)(2,1)}) %all-gather.7.cloned.1.call-update) | async-done | bytes 6291472 | tf_op jit(solution)/shard_map/all_gather | solution.py:599
  83.8 8.7 add_convert_fusion.1
  92.5 57.2 %swap_to_heads.2 = bf16[3,64,8192]{2,1,0:T(8,128)(2,1)} custom-call(bf16[3,16,64,512]{3,2,1,0:T(8,128)(2,1)} %bitcast.91), custom_call_target="tpu_custom_call" | custom-call | tf_op jit(solution)/shard_map/swap_to_heads/pallas_call | solution.py:533
  155.0 78.9 %attn_fwd.1 = (bf16[7168,7168]{1,0:T(8,128)(2,1)}, bf16[1024,1024]{1,0:T(8,128)(2,1)}, bf16[64,8192]{1,0:T(8,128)(2,1)}, f32[8,8192]{1,0:T(8,128)}) custom-call(bf16[64,8192]{1,0:T(8,128)(2,1)} %get-tuple-element.99.q_ref, bf16[64,8192]{1,0:T(8,128)(2,1)} %get-tuple-element.98.k_ref, bf16[64,8192]{1,0:T(8,128)(2,1)} %get-tuple-element.97.v_ref, ...), custom_call_target="tpu_custom_call" | custom-call | flops 52613349376 | bytes 102760448 | tf_op jit(solution)/shard_map/attn_fwd/pallas_call | solution.py:404
  233.8 47.2 %swap_to_tokens.2 = bf16[1,16,64,512]{3,2,1,0:T(8,128)(2,1)} custom-call(bf16[1,64,8192]{2,1,0:T(8,128)(2,1)} %bitcast.92), custom_call_target="tpu_custom_call" | custom-call | tf_op jit(solution)/shard_map/swap_to_tokens/pallas_call | solution.py:533
  284.8 10.4 multiply_convert_fusion
  295.3 65.3 %all-gather.13.cloned.1.call-done = bf16[4096,1024]{1,0:T(8,128)(2,1)} async-done(((bf16[128,1024]{1,0:T(8,128)(2,1)}), bf16[4096,1024]{1,0:T(8,128)(2,1)}) %all-gather.13.cloned.1.call-update) | async-done | bytes 8388624 | tf_op jit(solution)/shard_map/all_gather | solution.py:604
  360.6 8.9 fusion.19
  375.0 14.1 %convert_reduce_fusion = (f32[4096]{0:T(1024)}, bf16[512,4096]{1,0:T(8,128)(2,1)}) fusion(f32[512,4096]{1,0:T(8,128)} %get-tuple-element.125, f32[4096]{0:T(1024)S(1)} %slice_bitcast_fusion.3, bf16[512,1024]{1,0:T(8,128)(2,1)S(1)} %get-tuple-element.90, bf16[4096,1024]{1,0:T(8,128)(2,1)} %all-gather.13.cloned.1.call-done), kind=kOutput, calls=%fused_computation | convolution fusion | flops 4328517632 | bytes 22052864 | tf_op jit(solution)/shard_map/dot_general | solution.py:46
  389.2 8.2 multiply_reduce_fusion
  408.9 20.9 %swap_to_heads.3 = bf16[1,64,8192]{2,1,0:T(8,128)(2,1)} custom-call(bf16[1,16,64,512]{3,2,1,0:T(8,128)(2,1)} %bitcast.88), custom_call_target="tpu_custom_call" | custom-call | tf_op jit(solution)/shard_map/swap_to_heads/pallas_call | solution.py:533
  429.9 103.5 %attn_bwd.1 = (bf16[64,8192]{1,0:T(8,128)(2,1)}, bf16[64,8192]{1,0:T(8,128)(2,1)}, bf16[64,8192]{1,0:T(8,128)(2,1)}) custom-call(bf16[7168,7168]{1,0:T(8,128)(2,1)} %get-tuple-element.25.p_ref, bf16[1024,1024]{1,0:T(8,128)(2,1)} %get-tuple-element.26.pt_ref, bf16[64,8192]{1,0:T(8,128)(2,1)} %get-tuple-element.99.q_ref, ...), custom_call_target="tpu_custom_call" | custom-call | flops 105226698752 | bytes 102760448 | tf_op jit(solution)/shard_map/attn_bwd/pallas_call | solution.py:459
  537.3 63.1 %swap_to_tokens.3 = bf16[3,16,64,512]{3,2,1,0:T(8,128)(2,1)} custom-call(bf16[3,64,8192]{2,1,0:T(8,128)(2,1)} %pad_maximum_fusion.in_ref), custom_call_target="tpu_custom_call" | custom-call | tf_op jit(solution)/shard_map/swap_to_tokens/pallas_call | solution.py:533
  600.4 7.3 convert_bitcast_fusion
  607.7 8.7 copy.47
  617.0 9.2 convolution_convert_fusion.1
  627.4 9.2 convolution_convert_fusion
  640.4 57.5 %all-reduce = f32[32,384]{1,0:T(8,128)S(1)} all-reduce(f32[32,384]{1,0:T(8,128)S(1)} %concatenate.15), channel_id=7, replica_groups=mesh['seq'=2,'blk'=4,'head'=4] {'seq','blk','head'}, use_global_device_ids=true, to_apply=%region_23.24.clone | all-reduce | flops 12288 | bytes 98304
  699.0 8.2 add_bitcast_fusion
  708.8 39.6 %reduce-scatter.13.cloned.1.call-done = bf16[32,3072]{1,0:T(8,128)(2,1)} async-done(((bf16[1024,3072]{1,0:T(8,128)(2,1)}), bf16[32,3072]{1,0:T(8,128)(2,1)}) %reduce-scatter.13.cloned.1.call-update) | async-done | bytes 196624
  752.3 146.5 %reduce-scatter.9.cloned.1.call-done = bf16[32,4096]{1,0:T(8,128)(2,1)} async-done(((bf16[1024,4096]{1,0:T(8,128)(2,1)}), bf16[32,4096]{1,0:T(8,128)(2,1)}) %reduce-scatter.9.cloned.1.call-update) | async-done | bytes 262160 | tf_op jit(solution)/shard_map/reduce_scatter | solution.py:647
  900.6 145.2 %reduce-scatter.11.cloned.1.call-done = bf16[128,1024]{1,0:T(8,128)(2,1)} async-done(((bf16[4096,1024]{1,0:T(8,128)(2,1)}), bf16[128,1024]{1,0:T(8,128)(2,1)}) %reduce-scatter.11.cloned.1.call-update) | async-done | bytes 262160 | tf_op jit(solution)/shard_map/reduce_scatter | solution.py:647
  (132 shorter events, 53.1 us)
Async XLA Ops:
  7.2 76.6 %all-gather.7.cloned.1.call-start = ((), (), s32[]{:S(2)}) async-start(), calls=%async_computation.4 | async-start | bytes 6488064 | tf_op jit(solution)/shard_map/all_gather | solution.py:599
  8.9 272.2 %all-gather.9.cloned.1.call-start = ((), (), s32[]{:S(2)}) async-start(), calls=%async_computation.5 | async-start | bytes 2162688 | tf_op jit(solution)/shard_map/all_gather | solution.py:602
  9.6 275.2 %all-gather.11.cloned.1.call-start = ((), (), s32[]{:S(2)}) async-start(), calls=%async_computation.6 | async-start | bytes 8650752 | tf_op jit(solution)/shard_map/all_gather | solution.py:603
  10.3 350.2 %all-gather.13.cloned.1.call-start = ((), (), s32[]{:S(2)}) async-start(), calls=%async_computation.7 | async-start | bytes 8650752 | tf_op jit(solution)/shard_map/all_gather | solution.py:604
  10.9 696.4 %reduce-scatter.7.cloned.1.call-start = ((), (), s32[]{:S(2)}) async-start(), calls=%async_computation.8 | async-start | bytes 2162688 | tf_op jit(solution)/shard_map/reduce_scatter | solution.py:647
  62.5 298.1 %copy-start.16 = (f32[1024]{0:T(1024)}, f32[1024]{0:T(1024)S(1)}, u32[]{:S(2)}) copy-start(f32[1024]{0:T(1024)S(1)} %add.181) | copy-start | bytes 12292
  63.6 308.5 %copy-start.8 = (f32[512]{0:T(512)}, f32[512]{0:T(512)S(1)}, u32[]{:S(2)}) copy-start(f32[512]{0:T(512)S(1)} %fusion.7) | copy-start | bytes 6148
  233.8 47.2 %copy-start.6 = (bf16[1,512,1024]{2,1,0:T(8,128)(2,1)S(1)}, bf16[1,512,1024]{2,1,0:T(8,128)(2,1)}, u32[]{:S(2)}) copy-start(bf16[1,512,1024]{2,1,0:T(8,128)(2,1)} %param.18) | copy-start | bytes 3145732
  374.2 15.0 %slice-start = ((s8[8388608]{0:T(1024)(128)(4,1)}), s8[4194304]{0:T(1024)(128)(4,1)S(1)}, s32[]{:S(2)}) async-start(s8[8388608]{0:T(1024)(128)(4,1)} %bitcast.102), calls=%async_computation.12 | async-start | bytes 8388608
  375.0 14.2 %copy-start.4 = (bf16[512,1024]{1,0:T(8,128)(2,1)}, bf16[512,1024]{1,0:T(8,128)(2,1)S(1)}, u32[]{:S(2)}) copy-start(bf16[512,1024]{1,0:T(8,128)(2,1)S(1)} %get-tuple-element.90) | copy-start | bytes 3145732
  375.0 14.2 %slice-start.1 = ((s8[8388608]{0:T(1024)(128)(4,1)}), s8[4194304]{0:T(1024)(128)(4,1)S(1)}, s32[]{:S(2)}) async-start(s8[8388608]{0:T(1024)(128)(4,1)} %bitcast.102), calls=%async_computation.13 | async-start | bytes 8388608
  398.1 4.7 copy-start.14
  429.9 318.5 %reduce-scatter.13.cloned.1.call-start = ((), (), s32[]{:S(2)}) async-start(), calls=%async_computation.11 | async-start | bytes 6488064
  537.3 63.1 %copy-start.7 = (bf16[1,512,1024]{2,1,0:T(8,128)(2,1)S(1)}, bf16[1,512,1024]{2,1,0:T(8,128)(2,1)}, u32[]{:S(2)}) copy-start(bf16[1,512,1024]{2,1,0:T(8,128)(2,1)} %param.18) | copy-start | bytes 3145732
  616.4 282.4 %reduce-scatter.9.cloned.1.call-start = ((), (), s32[]{:S(2)}) async-start(), calls=%async_computation.9 | async-start | bytes 8650752 | tf_op jit(solution)/shard_map/reduce_scatter | solution.py:647
  626.2 419.6 %reduce-scatter.11.cloned.1.call-start = ((), (), s32[]{:S(2)}) async-start(), calls=%async_computation.10 | async-start | bytes 8650752 | tf_op jit(solution)/shard_map/reduce_scatter | solution.py:647
  636.6 2.6 copy-start
  637.3 2.6 copy-start.12
  637.3 2.7 copy-start.11
  637.3 2.7 copy-start.19
  637.3 2.8 copy-start.18
  637.3 2.9 copy-start.10
  637.3 2.9 copy-start.13
  639.1 59.9 %copy-start.15 = (f32[512]{0:T(512)S(1)}, f32[512]{0:T(512)}, u32[]{:S(2)}) copy-start(f32[512]{0:T(512)} %copy-done.14) | copy-start | bytes 6148
  (6 other events, 7.3 us)
Sparse Core Ops, SparseCore 0:
  11.5 72.2 all-gather.6
  86.7 102.1 all-gather.8
  191.7 91.1 all-gather.10
  285.6 74.9 all-gather.12
  430.0 144.7 reduce-scatter.6
  616.5 131.8 reduce-scatter.12
  750.7 148.0 reduce-scatter.8
  901.1 144.6 reduce-scatter.10

commit v2 on v1

--- a/solution.py
+++ b/solution.py
@@ -340,136 +340,720 @@
     )
 
 
+MESH = pl.DeviceIdType.MESH
+EVERY = ("seq", "blk", "head")
+EDGE = 32
+UNIT = 1024
+
+
+class Place:
+    def __init__(self, blks):
+        self.blks = blks
+        self.x = lax.axis_index("seq")
+        self.z = lax.axis_index("blk")
+        lane = lax.axis_index("head")
+        self.y = lane // 2
+        self.c = lax.rem(lane, 2)
+
+    def at(self, x=None, z=None, y=None, c=None):
+        x = self.x if x is None else x
+        z = self.z if z is None else z
+        y = self.y if y is None else y
+        c = self.c if c is None else c
+        return {"seq": x, "blk": z, "head": y * 2 + c}
+
+    def column(self):
+        return [lax.rem(self.z + step, self.blks) for step in range(1, self.blks)]
+
+    def near(self):
+        return [self.at(z=z) for z in self.column()] + [
+            self.at(x=1 - self.x),
+            self.at(y=1 - self.y),
+            self.at(c=1 - self.c),
+        ]
+
+    def others(self, devices):
+        own = (self.x * self.blks + self.z) * 4 + self.y * 2 + self.c
+        found = []
+        for step in range(1, devices):
+            index = lax.rem(own + step, devices)
+            found.append(
+                {
+                    "seq": index // (self.blks * 4),
+                    "blk": lax.rem(index // 4, self.blks),
+                    "head": lax.rem(index, 4),
+                }
+            )
+        return own, found
+
+
+def greet(devices):
+    barrier = pltpu.get_barrier_semaphore()
+    for device in devices:
+        pl.semaphore_signal(barrier, inc=1, device_id=device, device_id_type=MESH)
+    pl.semaphore_wait(barrier, len(devices))
+
+
+class Wires:
+    def __init__(self, send, recv):
+        self.send, self.recv, self.used = send, recv, 0
+
+    def copy(self, source, target, device):
+        slot = self.used
+        self.used += 1
+        return pltpu.make_async_remote_copy(
+            src_ref=source,
+            dst_ref=target,
+            send_sem=self.send.at[slot],
+            recv_sem=self.recv.at[slot],
+            device_id=device,
+            device_id_type=MESH,
+        )
+
+
+def view(ref, index, piece):
+    rows, cols = piece
+    return ref.at[tuple(index) + (pl.ds(*rows), pl.ds(*cols))]
+
+
+ALL = slice(None)
+
+
+class Gather:
+    WIRES = 7
+
+    def __init__(self, me, wires, ref, piece, turned):
+        x, z, y, c = me.x, me.z, me.y, me.c
+        own = view(ref, (x, z, y, c), piece)
+        self.first = [wires.copy(own, own, me.at(z=peer)) for peer in me.column()]
+        line = view(ref, (x, ALL, y, c), piece)
+        if turned:
+            half, rest = view(ref, (ALL, ALL, y, c), piece), view(ref, (ALL, ALL, 1 - y, c), piece)
+            self.second = wires.copy(line, line, me.at(x=1 - x))
+            self.third = wires.copy(half, half, me.at(y=1 - y))
+        else:
+            half, rest = view(ref, (x, ALL, ALL, c), piece), view(ref, (1 - x, ALL, ALL, c), piece)
+            self.second = wires.copy(line, line, me.at(y=1 - y))
+            self.third = wires.copy(half, half, me.at(x=1 - x))
+        self.near = wires.copy(half, half, me.at(c=1 - c))
+        self.far = wires.copy(rest, rest, me.at(c=1 - c))
+
+    def stage(self, index):
+        if index == 0:
+            for copy in self.first:
+                copy.start()
+        elif index == 1:
+            for copy in self.first:
+                copy.wait_recv()
+            self.second.start()
+        elif index == 2:
+            self.second.wait_recv()
+            self.third.start()
+            self.near.start()
+        elif index == 3:
+            self.third.wait_recv()
+            self.far.start()
+        else:
+            self.near.wait_recv()
+            self.far.wait_recv()
+            for copy in (*self.first, self.second, self.third, self.near, self.far):
+                copy.wait_send()
+
+
+class Reduce:
+    WIRES = 6
+
+    def __init__(self, me, wires, ref, piece, turned, own, own_sem, r0, r1, r2, r3, out, out_piece):
+        x, z, y, c = me.x, me.z, me.y, me.c
+        self.place, self.turned, self.out, self.out_piece = me, turned, out, out_piece
+        self.own, self.r0, self.r1, self.r2, self.r3 = own, r0, r1, r2, r3
+        self.load = pltpu.make_async_copy(view(ref, (ALL, ALL, ALL, c), piece), own, own_sem)
+        self.zero = wires.copy(view(ref, (ALL, ALL, ALL, 1 - c), piece), r0, me.at(c=1 - c))
+        if turned:
+            self.one = wires.copy(r0.at[:, :, 1 - y], r1, me.at(y=1 - y))
+            self.two = wires.copy(r0.at[1 - x, :, y], r2, me.at(x=1 - x))
+        else:
+            self.one = wires.copy(r0.at[1 - x], r1, me.at(x=1 - x))
+            self.two = wires.copy(r0.at[x, :, 1 - y], r2, me.at(y=1 - y))
+        self.three = [
+            wires.copy(r0.at[x, peer, y], r3.at[slot], me.at(z=peer))
+            for slot, peer in enumerate(me.column())
+        ]
+
+    def stage(self, index):
+        x, z, y = self.place.x, self.place.z, self.place.y
+        blks = self.place.blks
+        r0 = self.r0
+
+        def add(target, term):
+            total = r0[target].astype(jnp.float32) + term.astype(jnp.float32)
+            r0[target] = total.astype(r0.dtype)
+
+        if index == 0:
+            self.zero.start()
+        elif index == 1:
+            self.load.start()
+        elif index == 2:
+            self.load.wait()
+            self.zero.wait_recv()
+
+            @pl.loop(0, 4 * blks)
+            def _(i):
+                at = (i // (2 * blks), lax.rem(i // 2, blks), lax.rem(i, 2))
+                add(at, self.own[at])
+
+            self.one.start()
+        elif index == 3:
+            self.one.wait_recv()
+
+            @pl.loop(0, 2 * blks)
+            def _(i):
+                if self.turned:
+                    a, b = i // blks, lax.rem(i, blks)
+                    add((a, b, y), self.r1[a, b])
+                else:
+                    a, b = i // 2, lax.rem(i, 2)
+                    add((x, a, b), self.r1[a, b])
+
+            self.two.start()
+        elif index == 4:
+            self.two.wait_recv()
+
+            @pl.loop(0, blks)
+            def _(i):
+                add((x, i, y), self.r2[i])
+
+            for copy in self.three:
+                copy.start()
+        else:
+            for copy in self.three:
+                copy.wait_recv()
+            total = r0[x, z, y].astype(jnp.float32)
+            for slot in range(blks - 1):
+                total = total + self.r3[slot].astype(jnp.float32)
+            rows, cols = self.out_piece
+            self.out[rows[0] : rows[0] + rows[1], cols[0] : cols[0] + cols[1]] = total
+            for copy in (self.zero, self.one, self.two, *self.three):
+                copy.wait_send()
+
+
+def reduce_scratch(units, blks, dtype=jnp.bfloat16):
+    return [
+        pltpu.VMEM((2, 2, blks, 2, EDGE, UNIT), dtype),
+        pltpu.VMEM((units, 2, blks, 2, EDGE, UNIT), dtype),
+        pltpu.VMEM((units // 2 + units % 2, blks, 2, EDGE, UNIT), dtype),
+        pltpu.VMEM((max(units // 2, 1), 2, blks, EDGE, UNIT), dtype),
+        pltpu.VMEM((units, blks, EDGE, UNIT), dtype),
+        pltpu.VMEM((units, blks - 1, EDGE, UNIT), dtype),
+        pltpu.SemaphoreType.DMA((2,)),
+        pltpu.SemaphoreType.DMA((Reduce.WIRES * units,)),
+        pltpu.SemaphoreType.DMA((Reduce.WIRES * units,)),
+    ]
+
+
+def final_kernel(blks, devices, grad, sums, out, sums_out, own, r0, r1a, r1b, r2, r3, own_sem, send, recv, landed, sums_send, sums_recv, sums_sem):
+    me = Place(blks)
+    index, others = me.others(devices)
+    greet(others)
+    wires = Wires(send, recv)
+    units = r0.shape[0]
+    plan = [
+        Reduce(
+            me,
+            wires,
+            grad,
+            ((0, EDGE), (unit * UNIT, UNIT)),
+            unit % 2 == 1,
+            own.at[unit % 2],
+            own_sem.at[unit % 2],
+            r0.at[unit],
+            (r1b if unit % 2 else r1a).at[unit // 2],
+            r2.at[unit],
+            r3.at[unit],
+            out,
+            ((0, EDGE), (unit * UNIT, UNIT)),
+        )
+        for unit in range(units)
+    ]
+    small = []
+    for slot, device in enumerate(others):
+        peer = (device["seq"] * blks + device["blk"]) * 4 + device["head"]
+        small.append(
+            pltpu.make_async_remote_copy(
+                src_ref=sums.at[peer],
+                dst_ref=landed.at[slot],
+                send_sem=sums_send.at[slot],
+                recv_sem=sums_recv.at[slot],
+                device_id=device,
+                device_id_type=MESH,
+            )
+        )
+    for unit in plan:
+        unit.stage(0)
+    plan[0].stage(1)
+    plan[1].stage(1)
+    for copy in small:
+        copy.start()
+    mine = pltpu.make_async_copy(sums.at[index], landed.at[devices - 1], sums_sem)
+    mine.start()
+    for number, unit in enumerate(plan):
+        unit.stage(2)
+        if number + 2 < units:
+            plan[number + 2].stage(1)
+    for index in (3, 4):
+        for unit in plan:
+            unit.stage(index)
+    mine.wait()
+    for copy in small:
+        copy.wait()
+    sums_out[...] = jnp.sum(landed[...], axis=0)
+    for unit in plan:
+        unit.stage(5)
+
+
+def final_reduce(grad, sums, collective_id):
+    seqs, blks, heads = (lax.axis_size(name) for name in EVERY)
+    devices = seqs * blks * heads
+    units = grad.shape[1] // UNIT
+    shares = grad.reshape(seqs, blks, heads // 2, 2, EDGE, grad.shape[1])
+    return pl.pallas_call(
+        functools.partial(final_kernel, blks, devices),
+        out_shape=[
+            jax.ShapeDtypeStruct((EDGE, grad.shape[1]), jnp.float32),
+            jax.ShapeDtypeStruct(sums.shape[1:], jnp.float32),
+        ],
+        in_specs=[pl.BlockSpec(memory_space=pl.ANY)] * 2,
+        out_specs=[pl.BlockSpec(memory_space=pltpu.VMEM)] * 2,
+        scratch_shapes=[
+            *reduce_scratch(units, blks),
+            pltpu.VMEM((devices,) + sums.shape[1:], jnp.float32),
+            pltpu.SemaphoreType.DMA((devices,)),
+            pltpu.SemaphoreType.DMA((devices,)),
+            pltpu.SemaphoreType.DMA,
+        ],
+        compiler_params=pltpu.CompilerParams(
+            collective_id=collective_id, has_side_effects=True, vmem_limit_bytes=40 * 2**20
+        ),
+        name="final_reduce",
+    )(shares, sums)
+
+
+def first_kernel(blks, devices, wq, wk, wv, vec, out, vec_out, own_sem, send, recv, vec_send, vec_recv):
+    me = Place(blks)
+    index, others = me.others(devices)
+    local = [
+        pltpu.make_async_copy(
+            ref, out.at[me.x, me.z, me.y, me.c, :, pl.ds(unit * UNIT, UNIT)], own_sem.at[unit]
+        )
+        for unit, ref in enumerate((wq, wk, wv))
+    ]
+    local.append(pltpu.make_async_copy(vec, vec_out.at[index], own_sem.at[3]))
+    for copy in local:
+        copy.start()
+    greet(others)
+    for copy in local:
+        copy.wait()
+    wires = Wires(send, recv)
+    plan = [
+        Gather(me, wires, out, ((0, EDGE), (half * UNIT // 2, UNIT // 2)), half % 2 == 1)
+        for half in range(6)
+    ]
+    small = []
+    for slot, device in enumerate(others):
+        small.append(
+            pltpu.make_async_remote_copy(
+                src_ref=vec,
+                dst_ref=vec_out.at[index],
+                send_sem=vec_send.at[slot],
+                recv_sem=vec_recv.at[slot],
+                device_id=device,
+                device_id_type=MESH,
+            )
+        )
+    for unit in plan:
+        unit.stage(0)
+    for copy in small:
+        copy.start()
+    for wave in range(3 + 4):
+        for pair in range(3):
+            index = wave - pair + 1
+            if 1 <= index <= 4:
+                for unit in plan[2 * pair : 2 * pair + 2]:
+                    unit.stage(index)
+    for copy in small:
+        copy.wait()
+
+
+def first_gather(wq, wk, wv, vec, collective_id):
+    seqs, blks, heads = (lax.axis_size(name) for name in EVERY)
+    devices = seqs * blks * heads
+    return pl.pallas_call(
+        functools.partial(first_kernel, blks, devices),
+        out_shape=[
+            jax.ShapeDtypeStruct((seqs, blks, heads // 2, 2, EDGE, 3 * UNIT), wq.dtype),
+            jax.ShapeDtypeStruct((devices,) + vec.shape, vec.dtype),
+        ],
+        in_specs=[pl.BlockSpec(memory_space=pl.ANY)] * 4,
+        out_specs=[pl.BlockSpec(memory_space=pl.ANY)] * 2,
+        scratch_shapes=[
+            pltpu.SemaphoreType.DMA((4,)),
+            pltpu.SemaphoreType.DMA((6 * Gather.WIRES,)),
+            pltpu.SemaphoreType.DMA((6 * Gather.WIRES,)),
+            pltpu.SemaphoreType.DMA((devices,)),
+            pltpu.SemaphoreType.DMA((devices,)),
+        ],
+        compiler_params=pltpu.CompilerParams(collective_id=collective_id, has_side_effects=True),
+        name="first_gather",
+    )(wq, wk, wv, vec)
+
+
 LOG2E = 1.4426950408889634
-RR=(((1,),(1,)),((),()))
-def fwd_kernel(bq,ck,q_ref,k_ref,v_ref,sc_ref,sr_ref,p_ref,pt_ref,o_ref,l_ref,kk,vv,s0,s1,m0,m1):
-    g=pl.program_id(0); ng=pl.num_programs(0)
-    L=q_ref.shape[1]; Lm=p_ref.shape[1]; T=L-Lm; nc=Lm//ck
-    nb=Lm//bq
-    c=LOG2E*HEAD_DIM**-0.5
-    def qblk(start):
-        q=q_ref[:,pl.ds(pl.multiple_of(start,bq),bq)].astype(jnp.float32)*c
-        hi=q.astype(jnp.bfloat16).astype(jnp.float32)
-        return jnp.concatenate([hi,q-hi],0).T.astype(jnp.bfloat16)
-    def phase1(qb,s,j,mx):
-        r=jnp.dot(qb,kk[:,j*ck:(j+1)*ck],preferred_element_type=jnp.float32)
-        s[:,j*ck:(j+1)*ck]=r
-        for t in range(ck//128):
-            x=r[:,t*128:(t+1)*128]
-            mx=x if mx is None else jnp.maximum(mx,x)
-        return mx
-    def setm(m,mx):
-        m[...]=jnp.broadcast_to(jnp.max(mx,axis=1,keepdims=True),m.shape)
-    def phase2(s,m,j,row,acc):
-        p=jnp.exp2(s[:,j*ck:(j+1)*ck]-m[:,:1]).astype(jnp.bfloat16)
-        p_ref[row:row+bq,j*ck:(j+1)*ck]=p
-        r=lax.dot_general(vv[:,j*ck:(j+1)*ck],p,RR,preferred_element_type=jnp.float32)
-        return r if acc is None else acc+r
-    def finish(acc,start):
-        il=1.0/acc[HEAD_DIM:HEAD_DIM+1]
-        o_ref[:,pl.ds(pl.multiple_of(start,bq),bq)]=(acc[:HEAD_DIM]*il).astype(jnp.bfloat16)
-        l_ref[:,pl.ds(pl.multiple_of(start,bq),bq)]=jnp.broadcast_to(il,(8,bq))
-    @pl.when(g==0)
+BY_LAST = (((1,), (1,)), ((), ()))
+
+
+def weight_units(edges):
+    out_rows, expand_cols, reduce_rows = edges
+    units = [(0, ((0, out_rows), (0, UNIT)))]
+    expand = [(1, ((0, EDGE), (first, UNIT))) for first in range(0, expand_cols, UNIT)]
+    reduce = [(2, ((first, EDGE), (0, UNIT))) for first in range(0, reduce_rows, EDGE)]
+    for pair in zip(expand, reduce):
+        units.extend(pair)
+    return units
+
+
+def attn_fwd_kernel(
+    blks, rows, cols, q_ref, k_ref, v_ref, down_ref, across_ref, wo, we, wr,
+    p_ref, tail_ref, o_ref, inv_ref, go, ge, gr,
+    keys, values, s0, s1, m0, m1, own_sem, send, recv,
+):
+    step, steps = pl.program_id(0), pl.num_programs(0)
+    length, long = q_ref.shape[1], p_ref.shape[1]
+    tail, chunks, blocks = length - long, long // cols, long // rows
+    scale = LOG2E * HEAD_DIM**-0.5
+
+    me = Place(blks)
+    wires = Wires(send, recv)
+    shares, wholes = (wo, we, wr), (go, ge, gr)
+    units = weight_units((wo.shape[0], we.shape[1], wr.shape[0]))
+    plan = [
+        Gather(me, wires, wholes[which], piece, number % 2 == 1)
+        for number, (which, piece) in enumerate(units)
+    ]
+    moves = {0: []}
+    for number, unit in enumerate(plan):
+        begin = number if number < 2 else number - 1
+        for stage, at in enumerate((begin, begin + 1, begin + 2, begin + 4, blocks)):
+            moves.setdefault(min(at, blocks // 2 - 1), []).append((stage, number, unit))
+
+    def take_queries(start):
+        part = q_ref[:, pl.ds(pl.multiple_of(start, rows), rows)].astype(jnp.float32) * scale
+        high = part.astype(jnp.bfloat16).astype(jnp.float32)
+        return jnp.concatenate([high, part - high], 0).T.astype(jnp.bfloat16)
+
+    def score(queries, store, j, peak):
+        found = jnp.dot(
+            queries, keys[:, j * cols : (j + 1) * cols], preferred_element_type=jnp.float32
+        )
+        store[:, j * cols : (j + 1) * cols] = found
+        for first in range(0, cols, 128):
+            piece = found[:, first : first + 128]
+            peak = piece if peak is None else jnp.maximum(peak, piece)
+        return peak
+
+    def keep_peak(store, peak):
+        store[...] = jnp.broadcast_to(jnp.max(peak, axis=1, keepdims=True), store.shape)
+
+    def weigh(store, peak, j, row, total):
+        weights = jnp.exp2(store[:, j * cols : (j + 1) * cols] - peak[:, :1]).astype(jnp.bfloat16)
+        p_ref[row : row + rows, j * cols : (j + 1) * cols] = weights
+        term = lax.dot_general(
+            values[:, j * cols : (j + 1) * cols],
+            weights,
+            BY_LAST,
+            preferred_element_type=jnp.float32,
+        )
+        return term if total is None else total + term
+
+    def finish(total, start):
+        place = pl.ds(pl.multiple_of(start, rows), rows)
+        inverse = 1.0 / total[HEAD_DIM : HEAD_DIM + 1]
+        o_ref[:, place] = (total[:HEAD_DIM] * inverse).astype(jnp.bfloat16)
+        inv_ref[:, place] = jnp.broadcast_to(inverse, (8, rows))
+
+    @pl.when(step == 0)
     def _():
-        kk[0:HEAD_DIM,:]=k_ref[...]; kk[HEAD_DIM:,:]=k_ref[...]
-        vv[0:HEAD_DIM,:]=v_ref[...]
-        vv[HEAD_DIM:,:]=(lax.broadcasted_iota(jnp.int32,(16,L),0)==0).astype(jnp.float32).astype(jnp.bfloat16)
-        qb=qblk(0); mx=None
-        for j in range(nc): mx=phase1(qb,s0,j,mx)
-        setm(m0,mx)
-    for h,(sa,ma,sb,mb) in enumerate(((s0,m0,s1,m1),(s1,m1,s0,m0))):
-        nxt=jnp.minimum(2*g+h+1,nb-1)*bq
-        qb=qblk(nxt); acc=None; mx=None
-        for j in range(nc):
-            acc=phase2(sa,ma,j,h*bq,acc)
-            mx=phase1(qb,sb,j,mx)
-        setm(mb,mx)
-        finish(acc,(2*g+h)*bq)
-    @pl.when(g==ng-1)
+        local = [
+            pltpu.make_async_copy(share, whole.at[me.x, me.z, me.y, me.c], own_sem.at[number])
+            for number, (share, whole) in enumerate(zip(shares, wholes))
+        ]
+        for copy in local:
+            copy.start()
+        keys[0:HEAD_DIM, :] = k_ref[...]
+        keys[HEAD_DIM:, :] = k_ref[...]
+        values[0:HEAD_DIM, :] = v_ref[...]
+        values[HEAD_DIM:, :] = (
+            (lax.broadcasted_iota(jnp.int32, (16, length), 0) == 0)
+            .astype(jnp.float32)
+            .astype(jnp.bfloat16)
+        )
+        greet(me.near())
+        for copy in local:
+            copy.wait()
+
+    for at, todo in sorted(moves.items()):
+
+        @pl.when(step == at)
+        def _():
+            for stage, number, unit in sorted(todo, key=lambda entry: (-entry[0], entry[1])):
+                if stage < 4:
+                    unit.stage(stage)
+
+    @pl.when(step == 0)
     def _():
-        for i in range(T//bq):
-            qb=qblk(Lm+i*bq)
-            s=jnp.dot(qb,kk[:,Lm:],preferred_element_type=jnp.float32)
-            s=jnp.where(sc_ref[i*bq:(i+1)*bq,:1]==sr_ref[:1,:],s,-1e30)
-            m=jnp.max(s,axis=1,keepdims=True)
-            p=jnp.exp2(s-m).astype(jnp.bfloat16)
-            pt_ref[i*bq:(i+1)*bq,:]=p
-            finish(lax.dot_general(vv[:,Lm:],p,RR,preferred_element_type=jnp.float32),Lm+i*bq)
-
-def attn_fwd(qT,kT,vT,seg,Lm,bq=256,ck=1024):
-    L=qT.shape[1]; T=L-Lm
-    sc=jnp.broadcast_to(seg[:,None],(T,128)); sr=jnp.broadcast_to(seg[None,:],(8,T))
-    full=lambda s: pl.BlockSpec(s,lambda g:(0,)*len(s))
-    ng=Lm//bq//2
-    return pl.pallas_call(functools.partial(fwd_kernel,bq,ck),
-        grid=(ng,),
-        in_specs=[full((HEAD_DIM,L))]*3+[full((T,128)),full((8,T))],
-        out_specs=[pl.BlockSpec((2*bq,Lm),lambda g:(g,0)),full((T,T)),full((HEAD_DIM,L)),full((8,L))],
-        out_shape=[jax.ShapeDtypeStruct((Lm,Lm),jnp.bfloat16),jax.ShapeDtypeStruct((T,T),jnp.bfloat16),jax.ShapeDtypeStruct((HEAD_DIM,L),jnp.bfloat16),jax.ShapeDtypeStruct((8,L),jnp.float32)],
-        scratch_shapes=[pltpu.VMEM((2*HEAD_DIM,L),jnp.bfloat16),pltpu.VMEM((HEAD_DIM+16,L),jnp.bfloat16),pltpu.VMEM((bq,Lm),jnp.float32),pltpu.VMEM((bq,Lm),jnp.float32),pltpu.VMEM((bq,128),jnp.float32),pltpu.VMEM((bq,128),jnp.float32)],
-        compiler_params=pltpu.CompilerParams(vmem_limit_bytes=60*2**20),
-        cost_estimate=pl.CostEstimate(flops=4*Lm*Lm*256,bytes_accessed=2*Lm*Lm,transcendentals=Lm*Lm),
-        name="attn_fwd")(qT,kT,vT,sc,sr)
-
-def bwd_kernel(bq,ck,p_ref,pt_ref,q_ref,k_ref,v_ref,o_ref,do_ref,l_ref,dq_ref,dk_ref,dv_ref,vv,dka,dva):
-    g=pl.program_id(0); ng=pl.num_programs(0)
-    L=q_ref.shape[1]; Lm=p_ref.shape[1]; T=L-Lm; nc=Lm//ck
-    @pl.when(g==0)
+        queries, peak = take_queries(0), None
+        for j in range(chunks):
+            peak = score(queries, s0, j, peak)
+        keep_peak(m0, peak)
+
+    for half, (old, old_peak, new, new_peak) in enumerate(((s0, m0, s1, m1), (s1, m1, s0, m0))):
+        queries = take_queries(jnp.minimum(2 * step + half + 1, blocks - 1) * rows)
+        total, peak = None, None
+        for j in range(chunks):
+            total = weigh(old, old_peak, j, half * rows, total)
+            peak = score(queries, new, j, peak)
+        keep_peak(new_peak, peak)
+        finish(total, (2 * step + half) * rows)
+
+    @pl.when(step == steps - 1)
     def _():
-        vv[0:HEAD_DIM,:]=v_ref[...]
-        vv[HEAD_DIM:,:]=(lax.broadcasted_iota(jnp.int32,(16,L),0)<2).astype(jnp.float32).astype(jnp.bfloat16)
-        dka[...]=jnp.zeros_like(dka); dva[...]=jnp.zeros_like(dva)
-    def prep(start,n):
-        sl=pl.ds(pl.multiple_of(start,n),n)
-        do=do_ref[:,sl].astype(jnp.float32); il=l_ref[:1,sl]
-        dl=-jnp.sum(do*o_ref[:,sl].astype(jnp.float32),axis=0,keepdims=True)*il
-        dh=dl.astype(jnp.bfloat16).astype(jnp.float32)
-        row=lax.broadcasted_iota(jnp.int32,(16,n),0)
-        extra=jnp.where(row==0,dh,jnp.where(row==1,dl-dh,0.0))
-        d=do*il
-        A=jnp.concatenate([d,extra],0).T.astype(jnp.bfloat16)
-        return A,d.astype(jnp.bfloat16),q_ref[:,sl]
-    def chunk(A,d,q,p,kc,vc,dq):
-        dp=jnp.dot(A,vc,preferred_element_type=jnp.float32)
-        ds=(p.astype(jnp.float32)*dp).astype(jnp.bfloat16)
-        dv=jnp.dot(d,p,preferred_element_type=jnp.float32)
-        dk=jnp.dot(q,ds,preferred_element_type=jnp.float32)
-        r=lax.dot_general(kc,ds,RR,preferred_element_type=jnp.float32)
-        return (r if dq is None else dq+r),dk,dv
-    A,d,q=prep(g*bq,bq); dq=None
-    for j in range(nc):
-        sl=slice(j*ck,(j+1)*ck)
-        dq,dk,dv=chunk(A,d,q,p_ref[:,sl],k_ref[:,sl],vv[:,sl],dq)
-        dka[:,sl]+=dk; dva[:,sl]+=dv
-    dq_ref[:,pl.ds(pl.multiple_of(g*bq,bq),bq)]=(dq*HEAD_DIM**-0.5).astype(jnp.bfloat16)
-    @pl.when(g==ng-1)
+        for first in range(0, tail, rows):
+            queries = take_queries(long + first)
+            found = jnp.dot(queries, keys[:, long:], preferred_element_type=jnp.float32)
+            allowed = down_ref[first : first + rows, :1] == across_ref[:1, :]
+            found = jnp.where(allowed, found, -1e30)
+            peak = jnp.max(found, axis=1, keepdims=True)
+            weights = jnp.exp2(found - peak).astype(jnp.bfloat16)
+            tail_ref[first : first + rows, :] = weights
+            total = lax.dot_general(
+                values[:, long:], weights, BY_LAST, preferred_element_type=jnp.float32
+            )
+            finish(total, long + first)
+        for unit in plan:
+            unit.stage(4)
+
+
+def once(shape):
+    return pl.BlockSpec(shape, lambda step: (0,) * len(shape), pipeline_mode=pl.Buffered(1))
+
+
+def attn_fwd(query, key, value, seg, long, shares, collective_id, rows=256, cols=1024):
+    blks = lax.axis_size("blk")
+    lead = (lax.axis_size("seq"), blks, lax.axis_size("head") // 2, 2)
+    length = query.shape[1]
+    tail = length - long
+    down = jnp.broadcast_to(seg[:, None], (tail, 128))
+    across = jnp.broadcast_to(seg[None, :], (8, tail))
+    anywhere = pl.BlockSpec(memory_space=pl.ANY)
+    wires = Gather.WIRES * len(
+        weight_units((shares[0].shape[0], shares[1].shape[1], shares[2].shape[0]))
+    )
+    return pl.pallas_call(
+        functools.partial(attn_fwd_kernel, blks, rows, cols),
+        grid=(long // rows // 2,),
+        in_specs=[once((HEAD_DIM, length))] * 3
+        + [once((tail, 128)), once((8, tail))]
+        + [anywhere] * 3,
+        out_specs=[
+            pl.BlockSpec((2 * rows, long), lambda step: (step, 0)),
+            once((tail, tail)),
+            once((HEAD_DIM, length)),
+            once((8, length)),
+        ]
+        + [anywhere] * 3,
+        out_shape=[
+            jax.ShapeDtypeStruct((long, long), jnp.bfloat16),
+            jax.ShapeDtypeStruct((tail, tail), jnp.bfloat16),
+            jax.ShapeDtypeStruct((HEAD_DIM, length), jnp.bfloat16),
+            jax.ShapeDtypeStruct((8, length), jnp.float32),
+        ]
+        + [jax.ShapeDtypeStruct(lead + share.shape, share.dtype) for share in shares],
+        scratch_shapes=[
+            pltpu.VMEM((2 * HEAD_DIM, length), jnp.bfloat16),
+            pltpu.VMEM((HEAD_DIM + 16, length), jnp.bfloat16),
+            pltpu.VMEM((rows, long), jnp.float32),
+            pltpu.VMEM((rows, long), jnp.float32),
+            pltpu.VMEM((rows, 128), jnp.float32),
+            pltpu.VMEM((rows, 128), jnp.float32),
+            pltpu.SemaphoreType.DMA((3,)),
+            pltpu.SemaphoreType.DMA((wires,)),
+            pltpu.SemaphoreType.DMA((wires,)),
+        ],
+        compiler_params=pltpu.CompilerParams(
+            collective_id=collective_id, has_side_effects=True, vmem_limit_bytes=56 * 2**20
+        ),
+        cost_estimate=pl.CostEstimate(
+            flops=4 * long * long * HEAD_DIM,
+            bytes_accessed=2 * long * long,
+            transcendentals=long * long,
+        ),
+        name="attn_fwd",
+    )(query, key, value, down, across, *shares)
+
+
+def attn_bwd_kernel(
+    blks, rows, cols, p_ref, tail_ref, q_ref, k_ref, v_ref, o_ref, do_ref, inv_ref, wo, we, wr,
+    dq_ref, dk_ref, dv_ref, go, ge, gr,
+    values, dk_sum, dv_sum, own, r0, r1a, r1b, r2, r3, own_sem, send, recv,
+):
+    step, steps = pl.program_id(0), pl.num_programs(0)
+    length, long = q_ref.shape[1], p_ref.shape[1]
+    tail, chunks = length - long, long // cols
+    scale = HEAD_DIM**-0.5
+
+    me = Place(blks)
+    wires = Wires(send, recv)
+    partials, totals = (wo, we, wr), (go, ge, gr)
+    units = weight_units((wo.shape[4], we.shape[5], wr.shape[4]))
+    last = long // rows - 1
+    plan, moves = [], {}
+    for number, (which, piece) in enumerate(units):
+        turned = number % 2 == 1
+        unit = Reduce(
+            me,
+            wires,
+            partials[which],
+            piece,
+            turned,
+            own.at[number % 2],
+            own_sem.at[number % 2],
+            r0.at[number],
+            (r1b if turned else r1a).at[number // 2],
+            r2.at[number],
+            r3.at[number],
+            totals[which],
+            piece,
+        )
+        plan.append(unit)
+        for stage, at in enumerate((0, number, number + 1, number + 3, number + 4)):
+            moves.setdefault(min(at, last), []).append((stage, number, unit))
+
+    def prepare(start, width):
+        place = pl.ds(pl.multiple_of(start, width), width)
+        grads, inverse = do_ref[:, place].astype(jnp.float32), inv_ref[:1, place]
+        delta = -jnp.sum(grads * o_ref[:, place].astype(jnp.float32), axis=0, keepdims=True)
+        delta = delta * inverse
+        high = delta.astype(jnp.bfloat16).astype(jnp.float32)
+        row = lax.broadcasted_iota(jnp.int32, (16, width), 0)
+        extra = jnp.where(row == 0, high, jnp.where(row == 1, delta - high, 0.0))
+        grads = grads * inverse
+        wide = jnp.concatenate([grads, extra], 0).T.astype(jnp.bfloat16)
+        return wide, grads.astype(jnp.bfloat16), q_ref[:, place]
+
+    def part(wide, grads, queries, weights, keys_here, values_here, dq):
+        dp = jnp.dot(wide, values_here, preferred_element_type=jnp.float32)
+        ds = (weights.astype(jnp.float32) * dp).astype(jnp.bfloat16)
+        dv = jnp.dot(grads, weights, preferred_element_type=jnp.float32)
+        dk = jnp.dot(queries, ds, preferred_element_type=jnp.float32)
+        term = lax.dot_general(keys_here, ds, BY_LAST, preferred_element_type=jnp.float32)
+        return (term if dq is None else dq + term), dk, dv
+
+    @pl.when(step == 0)
     def _():
-        for i in range(T//bq):
-            A,d,q=prep(Lm+i*bq,bq)
-            dq,dk,dv=chunk(A,d,q,pt_ref[i*bq:(i+1)*bq,:],k_ref[:,Lm:],vv[:,Lm:],None)
-            dka[:,Lm:]+=dk; dva[:,Lm:]+=dv
-            dq_ref[:,Lm+i*bq:Lm+(i+1)*bq]=(dq*HEAD_DIM**-0.5).astype(jnp.bfloat16)
-        dk_ref[...]=(dka[...]*HEAD_DIM**-0.5).astype(jnp.bfloat16)
-        dv_ref[...]=dva[...].astype(jnp.bfloat16)
-
-def attn_bwd(P,Pt,qT,kT,vT,oT,doT,il,Lm,bq=512,ck=1024):
-    L=qT.shape[1]; T=L-Lm
-    full=lambda s: pl.BlockSpec(s,lambda g:(0,)*len(s))
-    f=jax.ShapeDtypeStruct((HEAD_DIM,L),jnp.bfloat16)
-    return pl.pallas_call(functools.partial(bwd_kernel,bq,ck),
-        grid=(Lm//bq,),
-        in_specs=[pl.BlockSpec((bq,Lm),lambda g:(g,0)),full((T,T))]+[full((HEAD_DIM,L))]*5+[full((8,L))],
-        out_specs=[full((HEAD_DIM,L))]*3,
-        out_shape=[f]*3,
-        scratch_shapes=[pltpu.VMEM((HEAD_DIM+16,L),jnp.bfloat16),pltpu.VMEM((HEAD_DIM,L),jnp.float32),pltpu.VMEM((HEAD_DIM,L),jnp.float32)],
-        compiler_params=pltpu.CompilerParams(vmem_limit_bytes=60*2**20),
-        cost_estimate=pl.CostEstimate(flops=8*Lm*Lm*256,bytes_accessed=2*Lm*Lm,transcendentals=0),
-        name="attn_bwd")(P,Pt,qT,kT,vT,oT,doT,il)
-
-
-MESH = pl.DeviceIdType.MESH
+        greet(me.near())
+
+    for at, todo in sorted(moves.items()):
+
+        @pl.when(step == at)
+        def _():
+            for stage, number, unit in sorted(todo, key=lambda entry: (-entry[0], entry[1])):
+                unit.stage(stage)
+
+    @pl.when(step == 0)
+    def _():
+        values[0:HEAD_DIM, :] = v_ref[...]
+        values[HEAD_DIM:, :] = (
+            (lax.broadcasted_iota(jnp.int32, (16, length), 0) < 2)
+            .astype(jnp.float32)
+            .astype(jnp.bfloat16)
+        )
+        dk_sum[...] = jnp.zeros_like(dk_sum)
+        dv_sum[...] = jnp.zeros_like(dv_sum)
+
+    wide, grads, queries = prepare(step * rows, rows)
+    dq = None
+    for j in range(chunks):
+        here = slice(j * cols, (j + 1) * cols)
+        dq, dk, dv = part(
+            wide, grads, queries, p_ref[:, here], k_ref[:, here], values[:, here], dq
+        )
+        dk_sum[:, here] += dk
+        dv_sum[:, here] += dv
+    dq_ref[:, pl.ds(pl.multiple_of(step * rows, rows), rows)] = (dq * scale).astype(jnp.bfloat16)
+
+    @pl.when(step == steps - 1)
+    def _():
+        for first in range(0, tail, rows):
+            wide, grads, queries = prepare(long + first, rows)
+            dq, dk, dv = part(
+                wide,
+                grads,
+                queries,
+                tail_ref[first : first + rows, :],
+                k_ref[:, long:],
+                values[:, long:],
+                None,
+            )
+            dk_sum[:, long:] += dk
+            dv_sum[:, long:] += dv
+            dq_ref[:, long + first : long + first + rows] = (dq * scale).astype(jnp.bfloat16)
+        dk_ref[...] = (dk_sum[...] * scale).astype(jnp.bfloat16)
+        dv_ref[...] = dv_sum[...].astype(jnp.bfloat16)
+        for unit in plan:
+            unit.stage(5)
+
+
+def attn_bwd(
+    probs, tail_probs, query, key, value, attn, grad_attn, inv_total, long, partials,
+    collective_id, rows=512, cols=1024,
+):
+    blks = lax.axis_size("blk")
+    lead = (lax.axis_size("seq"), blks, lax.axis_size("head") // 2, 2)
+    devices = math.prod(lead)
+    length = query.shape[1]
+    tail = length - long
+    anywhere = pl.BlockSpec(memory_space=pl.ANY)
+    edges = [(partial.shape[0] // devices, partial.shape[1]) for partial in partials]
+    units = len(weight_units((edges[0][0], edges[1][1], edges[2][0])))
+    narrow = jax.ShapeDtypeStruct((HEAD_DIM, length), jnp.bfloat16)
+    return pl.pallas_call(
+        functools.partial(attn_bwd_kernel, blks, rows, cols),
+        grid=(long // rows,),
+        in_specs=[pl.BlockSpec((rows, long), lambda step: (step, 0)), once((tail, tail))]
+        + [once((HEAD_DIM, length))] * 5
+        + [once((8, length))]
+        + [anywhere] * 3,
+        out_specs=[once((HEAD_DIM, length))] * 3 + [once(edge) for edge in edges],
+        out_shape=[narrow] * 3 + [jax.ShapeDtypeStruct(edge, jnp.float32) for edge in edges],
+        scratch_shapes=[
+            pltpu.VMEM((HEAD_DIM + 16, length), jnp.bfloat16),
+            pltpu.VMEM((HEAD_DIM, length), jnp.float32),
+            pltpu.VMEM((HEAD_DIM, length), jnp.float32),
+            *reduce_scratch(units, blks),
+        ],
+        compiler_params=pltpu.CompilerParams(
+            collective_id=collective_id, has_side_effects=True, vmem_limit_bytes=62 * 2**20
+        ),
+        cost_estimate=pl.CostEstimate(
+            flops=8 * long * long * HEAD_DIM, bytes_accessed=2 * long * long, transcendentals=0
+        ),
+        name="attn_bwd",
+    )(
+        probs, tail_probs, query, key, value, attn, grad_attn, inv_total,
+        *[partial.reshape(lead + edge) for partial, edge in zip(partials, edges)],
+    )
+
+
 GROUP = ("blk", "head")
-EVERY = ("seq", "blk", "head")
 
 
 def greet_group(me, count, heads):
@@ -589,20 +1173,20 @@
         bias_expand,
     )
     sizes = [vector.shape[0] for vector in vectors]
-    packed = lax.all_gather(jnp.concatenate(vectors), EVERY, axis=0).astype(jnp.float32)
+    lanes = 128
+    spare = 16 * lanes - sum(sizes)
+    packed = jnp.concatenate(vectors + (jnp.zeros((spare,), layer_input.dtype),))
+    w_qkv, packed = first_gather(
+        weight_query, weight_key, weight_value, packed.reshape(16, lanes), 4
+    )
+    w_qkv = w_qkv.reshape(model_width, 3 * model_width)
+    packed = packed.reshape(-1, 16 * lanes).astype(jnp.float32)
     whole, start = [], 0
     for size in sizes:
         whole.append(packed[:, start : start + size].reshape(-1))
         start += size
     b_query, b_value, b_output, b_reduce, gain_one, shift_one, gain_two, shift_two, b_expand = whole
 
-    w_qkv = lax.all_gather(
-        jnp.concatenate((weight_query, weight_key, weight_value), axis=1), EVERY, axis=0, tiled=True
-    )
-    w_output = lax.all_gather(weight_output, EVERY, axis=0, tiled=True)
-    w_expand = lax.all_gather(weight_expand, EVERY, axis=0, tiled=True)
-    w_reduce = lax.all_gather(weight_reduce, EVERY, axis=0, tiled=True)
-
     b_qkv = jnp.concatenate((b_query, jnp.zeros_like(b_query), b_value))
     qkv = lax.dot_general(
         w_qkv, flat_rows, (((0,), (1,)), ((), ())), preferred_element_type=jnp.float32
@@ -611,7 +1195,18 @@
     qkv = swap(qkv, True, 0)
     query, key, value = qkv[0], qkv[1], qkv[2]
     seg = tail_segments(doc_lengths, long_rows, seq_len - long_rows)[0]
-    probs, tail_probs, attn, inv_total = attn_fwd(query, key, value, seg, long_rows)
+    probs, tail_probs, attn, inv_total, w_output, w_expand, w_reduce = attn_fwd(
+        query,
+        key,
+        value,
+        seg,
+        long_rows,
+        (weight_output, weight_expand, weight_reduce),
+        5,
+    )
+    w_output = w_output.reshape(-1, weight_output.shape[1])
+    w_expand = w_expand.reshape(-1, weight_expand.shape[1])
+    w_reduce = w_reduce.reshape(-1, weight_reduce.shape[1])
     attn_flat = swap(attn[None], False, 1).reshape(model_width, tok_rows)
 
     resid_one = flat_rows.astype(jnp.float32) + left_dot(attn_flat, w_output) + b_output
@@ -643,23 +1238,23 @@
     grad_attn = right_dot(w_output, grad_branch).astype(jnp.bfloat16)
     grad_attn = swap(grad_attn.reshape(1, HEADS, HEAD_DIM, tok_rows), True, 2)[0]
 
-    def share(grad):
-        return lax.psum_scatter(
-            grad.astype(jnp.bfloat16), EVERY, scatter_dimension=0, tiled=True
-        ).astype(jnp.float32)
-
-    grad_w_output = share(grad_w_output)
-    grad_w_expand = share(grad_w_expand)
-    grad_w_reduce = share(grad_w_reduce)
-
-    grad_qkv = attn_bwd(
-        probs, tail_probs, query, key, value, attn, grad_attn, inv_total, long_rows
+    *grad_qkv, grad_w_output, grad_w_expand, grad_w_reduce = attn_bwd(
+        probs,
+        tail_probs,
+        query,
+        key,
+        value,
+        attn,
+        grad_attn,
+        inv_total,
+        long_rows,
+        [grad.astype(jnp.bfloat16) for grad in (grad_w_output, grad_w_expand, grad_w_reduce)],
+        6,
     )
     grad_qkv = swap(jnp.stack(grad_qkv), False, 3).reshape(3 * model_width, tok_rows)
     grad_w_qkv = lax.dot_general(
         flat_rows, grad_qkv, (((0,), (1,)), ((), ())), preferred_element_type=jnp.float32
     )
-    grad_w_qkv = share(grad_w_qkv)
     grad_input = grad_resid_one + lax.dot_general(
         grad_qkv, w_qkv, (((0,), (1,)), ((), ())), preferred_element_type=jnp.float32
     )
@@ -677,7 +1272,9 @@
         grad_b_expand,
     )
     sums = jnp.concatenate([term.reshape(-1, size) for term, size in zip(sums, sizes)], axis=1)
-    sums = lax.psum_scatter(sums, EVERY, scatter_dimension=0, tiled=True).reshape(-1)
+    sums = jnp.pad(sums, ((0, 0), (0, 8 * lanes - sums.shape[1]))).reshape(-1, 8, lanes)
+    grad_w_qkv, sums = final_reduce(grad_w_qkv.astype(jnp.bfloat16), sums, 7)
+    sums = sums.reshape(-1)
     parts, start = [], 0
     for size in sizes:
         parts.append(sums[start : start + size])

time: 1060 us -> 761 us (0.72)
  waiting for transfers between devices: 418 us -> 0 us
  Pallas kernels: 371 us -> 630 us
  blocking collectives: 101 us -> 0 us
  between operations: 14.7 us -> 1.46 us
    reduce_scatter x3 -> x0, waiting for transfers between devices: 292 us -> none  [share(): lax.psum_scatter(grad.astype(jnp.bfloat16), EVERY, scatter_dimension=0, t...]
    pallas_call x2 -> x4, Pallas kernels: 182 us -> 458 us  [the longest x1 200 us: attn_fwd(): pl.pallas_call(functools.partial(attn_fwd_kernel, blks, rows, cols), grid...]
    all_gather x4 -> x0, waiting for transfers between devices: 84.9 us -> none  [the longest x1 65.3 us: shards_heads(): w_reduce = lax.all_gather(weight_reduce, EVERY, axis=0, tiled=True)]
    unnamed x1 -> x0, blocking collectives: 57.5 us -> none
    all_gather x1 -> x0, blocking collectives: 43.5 us -> none  [shards_heads(): lax.all_gather(jnp.concatenate(vectors), EVERY, axis=0).astype(jnp.float32)]
    unnamed x9 -> x0, waiting for transfers between devices: 41.5 us -> none
    pallas_call x4, Pallas kernels: 188 us -> 172 us  [swap(): pl.pallas_call(functools.partial(swap_kernel, to_heads, blks, heads), out...]
  transfers between devices with their start and end apart: 8 -> 0, of which waited for: 5 -> 0; matrix products, arithmetic and copies ran while one was open for 9% -> 0% of each run, Pallas kernels for 33% -> 0%
where the time goes in v2:
time: 761 us; the launch traced here: 756 us
  Pallas kernels  630 us (83%)
  matrix products  84.1 us (11%)
  local copies, waits for them, and re-layouts  24.2 us (3%)
  other arithmetic  15.9 us (2%)
    pallas_call x1, Pallas kernels, attn_fwd(): pl.pallas_call(functools.partial(attn_fwd_kernel, blks, rows, cols), grid...  200 us
    pallas_call x4, Pallas kernels, swap(): pl.pallas_call(functools.partial(swap_kernel, to_heads, blks, heads), out...  172 us
    pallas_call x1, Pallas kernels, attn_bwd(): pl.pallas_call(functools.partial(attn_bwd_kernel, blks, rows, cols), grid...  137 us
    pallas_call x1, Pallas kernels, final_reduce(): pl.pallas_call(functools.partial(final_kernel, blks, devices), out_shape=...  67.7 us
    pallas_call x1, Pallas kernels, first_gather(): pl.pallas_call(functools.partial(first_kernel, blks, devices), out_shape=...  53.1 us
    dot_general x3, matrix products, right_dot(): lax.dot_general(left, right, (((1,), (1,)), ((), ())), preferred_element_...  22.9 us
    dot_general x3, matrix products, plain_dot(): return jnp.dot(left, right, preferred_element_type=jnp.float32)  20.9 us
    dot_general x3, matrix products, left_dot(): lax.dot_general(left, right, (((0,), (0,)), ((), ())), preferred_element_...  17.5 us

profile of v2, /device:TPU:0, one launch (start us, length us, event | category | flops | bytes accessed | tf_op | source)
XLA Modules:
  0.0 755.7 jit_solution(10425581204248792685)
XLA Ops:
  0.7 6.7 concatenate.9
  7.3 53.1 %first_gather.1 = (bf16[2,4,2,2,32,3072]{5,4,3,2,1,0:T(8,128)(2,1)}, bf16[32,16,128]{2,1,0:T(8,128)(2,1)}) custom-call(bf16[32,1024]{1,0:T(8,128)(2,1)} %wq.1, bf16[32,1024]{1,0:T(8,128)(2,1)} %wk.1, bf16[32,1024]{1,0:T(8,128)(2,1)} %wv.1, bf16[16,128]{1,0:T(8,128)(2,1)} %bitcast.105), custom_call_target="tpu_custom_call" | custom-call | tf_op jit(solution)/shard_map/first_gather/pallas_call | solution.py:690
  61.8 8.6 %add_convert_fusion.1 = bf16[3072,512]{1,0:T(8,128)(2,1)} fusion(bf16[1024,3072]{1,0:T(8,128)(2,1)} %bitcast.108, f32[3072]{0:T(1024)S(1)} %pad_maximum_fusion.1, bf16[1,512,1024]{2,1,0:T(8,128)(2,1)} %param.18), kind=kOutput, calls=%fused_computation.7 | convolution fusion | flops 3224371200 | bytes 10498048 | tf_op jit(solution)/shard_map/dot_general | solution.py:1191
  70.4 55.1 %swap_to_heads.2 = bf16[3,64,8192]{2,1,0:T(8,128)(2,1)} custom-call(bf16[3,16,64,512]{3,2,1,0:T(8,128)(2,1)} %bitcast.93), custom_call_target="tpu_custom_call" | custom-call | tf_op jit(solution)/shard_map/swap_to_heads/pallas_call | solution.py:1117
  125.5 3.6 slice_bitcast_fusion
  132.3 200.4 %attn_fwd.1 = (bf16[7168,7168]{1,0:T(8,128)(2,1)}, bf16[1024,1024]{1,0:T(8,128)(2,1)}, bf16[64,8192]{1,0:T(8,128)(2,1)}, f32[8,8192]{1,0:T(8,128)}, bf16[2,4,2,2...) custom-call(bf16[64,8192]{1,0:T(8,128)(2,1)} %get-tuple-element.68.q, ...), custom_call_target="tpu_custom_call" | custom-call | flops 13153337344 | bytes 102760448 | tf_op jit(solution)/shard_map/attn_fwd/pallas_call | solution.py:860
  332.8 34.8 %swap_to_tokens.2 = bf16[1,16,64,512]{3,2,1,0:T(8,128)(2,1)} custom-call(bf16[1,64,8192]{2,1,0:T(8,128)(2,1)} %bitcast.89), custom_call_target="tpu_custom_call" | custom-call | tf_op jit(solution)/shard_map/swap_to_tokens/pallas_call | solution.py:1117
  367.6 3.3 fusion.18
  371.4 10.6 %multiply_convert_fusion = (bf16[512,4096]{1,0:T(8,128)(2,1)S(1)}, f32[512,4096]{1,0:T(8,128)}) fusion(f32[4096]{0:T(1024)S(1)} %slice_bitcast_fusion.3, bf16[1024,4096]{1,0:T(8,128)(2,1)} %bitcast.110, f32[512,1024]{1,0:T(8,128)S(1)} %get-tuple-element.92, f32[1024]{0:T(1024)S(1)} %add.173, f32[1024]{0:T(1024)S(1)} %mul.157, f32[512]{0:T(512)S(1)} %fusion.7, ...), kind=kOutput, calls=%fused_computation.2 | convolution fusion | flops 4310171648 | bytes 23097344 | tf_op jit(solution)/shard_map/dot_general | solution.py:36
  382.0 6.0 fusion.19
  393.4 3.6 fusion.13
  397.2 13.5 %convert_reduce_fusion = (f32[4096]{0:T(1024)S(1)}, bf16[512,4096]{1,0:T(8,128)(2,1)}) fusion(f32[512,4096]{1,0:T(8,128)} %get-tuple-element.94, f32[4096]{0:T(1024)S(1)} %slice_bitcast_fusion.3, bf16[512,1024]{1,0:T(8,128)(2,1)S(1)} %get-tuple-element.59, bf16[4096,1024]{1,0:T(8,128)(2,1)} %bitcast.114), kind=kOutput, calls=%fused_computation | convolution fusion | flops 4328517632 | bytes 22052864 | tf_op jit(solution)/shard_map/dot_general | solution.py:46
  410.8 7.2 multiply_reduce_fusion
  423.7 27.4 %swap_to_heads.3 = bf16[1,64,8192]{2,1,0:T(8,128)(2,1)} custom-call(bf16[1,16,64,512]{3,2,1,0:T(8,128)(2,1)} %bitcast.97), custom_call_target="tpu_custom_call" | custom-call | tf_op jit(solution)/shard_map/swap_to_heads/pallas_call | solution.py:1117
  451.1 4.2 convolution_convert_fusion.3
  455.3 7.5 convolution_convert_fusion.1
  462.9 6.8 convolution_convert_fusion
  469.6 137.0 %attn_bwd.1 = (bf16[64,8192]{1,0:T(8,128)(2,1)}, bf16[64,8192]{1,0:T(8,128)(2,1)}, bf16[64,8192]{1,0:T(8,128)(2,1)}, f32[32,1024]{1,0:T(8,128)}, f32[32,4096]{1,0:T(8,128)}, /*index=5*/f32[128,1024]{1,0:T(8,128)}) custom-call(bf16[7168,7168]{1,0:T(8,128)(2,1)} %get-tuple-element.40.p_ref, bf16[1024,1024]{1,0:T(8,128)(2,1)} %get-tuple-element.41.tail_ref, ...), custom_call_target="tpu_custom_call" | custom-call | flops 26306674688 | bytes 102760448 | tf_op jit(solution)/shard_map/attn_bwd/pallas_call | solution.py:1028
  606.7 3.9 pad_maximum_fusion.in_ref
  610.5 54.4 %swap_to_tokens.3 = bf16[3,16,64,512]{3,2,1,0:T(8,128)(2,1)} custom-call(bf16[3,64,8192]{2,1,0:T(8,128)(2,1)} %pad_maximum_fusion.in_ref), custom_call_target="tpu_custom_call" | custom-call | tf_op jit(solution)/shard_map/swap_to_tokens/pallas_call | solution.py:1117
  665.0 8.8 %add_bitcast_fusion = f32[1,512,1024]{2,1,0:T(8,128)} fusion(f32[512,1024]{1,0:T(8,128)S(1)} %copy-done.4, bf16[3072,512]{1,0:T(8,128)(2,1)} %bitcast.85, bf16[1024,3072]{1,0:T(8,128)(2,1)} %bitcast.109, f32[512]{0:T(512)S(1)} %negate_multiply_fusion), kind=kOutput, calls=%fused_computation.18 | convolution fusion | flops 3222274048 | bytes 13633536 | tf_op jit(solution)/shard_map/dot_general | solution.py:1258
  673.7 5.4 convolution_convert_fusion.2
  680.6 2.8 copy-done
  683.4 67.7 %final_reduce.1 = (f32[32,3072]{1,0:T(8,128)S(1)}, f32[8,128]{1,0:T(8,128)S(1)}) custom-call(bf16[2,4,2,2,32,3072]{5,4,3,2,1,0:T(8,128)(2,1)S(1)} %bitcast.82, f32[32,8,128]{2,1,0:T(8,128)S(1)} %bitcast.83), custom_call_target="tpu_custom_call" | custom-call | tf_op jit(solution)/shard_map/final_reduce/pallas_call | solution.py:619
  (104 shorter events, 21.9 us)
Async XLA Ops:
  125.5 3.7 copy-start.14
  332.8 34.8 %copy-start.9 = (bf16[1,512,1024]{2,1,0:T(8,128)(2,1)S(1)}, bf16[1,512,1024]{2,1,0:T(8,128)(2,1)}, u32[]{:S(2)}) copy-start(bf16[1,512,1024]{2,1,0:T(8,128)(2,1)} %param.18) | copy-start | bytes 3145732
  371.0 11.0 %slice-start.2 = ((s8[8388608]{0:T(1024)(128)(4,1)}), s8[4194304]{0:T(1024)(128)(4,1)S(1)}, s32[]{:S(2)}) async-start(s8[8388608]{0:T(1024)(128)(4,1)} %bitcast.115), calls=%async_computation.2 | async-start | bytes 8388608
  371.4 10.6 %slice-start.3 = ((s8[8388608]{0:T(1024)(128)(4,1)}), s8[4194304]{0:T(1024)(128)(4,1)S(1)}, s32[]{:S(2)}) async-start(s8[8388608]{0:T(1024)(128)(4,1)} %bitcast.115), calls=%async_computation.3 | async-start | bytes 8388608
  382.0 6.0 copy-start.15
  388.1 2.9 copy-start.2
  397.0 13.8 %slice-start = ((s8[8388608]{0:T(1024)(128)(4,1)}), s8[4194304]{0:T(1024)(128)(4,1)S(1)}, s32[]{:S(2)}) async-start(s8[8388608]{0:T(1024)(128)(4,1)} %bitcast.111), calls=%async_computation | async-start | bytes 8388608
  397.2 13.5 %copy-start.6 = (bf16[512,1024]{1,0:T(8,128)(2,1)}, bf16[512,1024]{1,0:T(8,128)(2,1)S(1)}, u32[]{:S(2)}) copy-start(bf16[512,1024]{1,0:T(8,128)(2,1)S(1)} %get-tuple-element.59) | copy-start | bytes 3145732
  397.2 13.5 %slice-start.1 = ((s8[8388608]{0:T(1024)(128)(4,1)}), s8[4194304]{0:T(1024)(128)(4,1)S(1)}, s32[]{:S(2)}) async-start(s8[8388608]{0:T(1024)(128)(4,1)} %bitcast.111), calls=%async_computation.1 | async-start | bytes 8388608
  418.7 5.0 copy-start.3
  418.7 2.7 copy-start.5
  418.9 4.7 copy-start.8
  451.1 4.3 copy-start.17
  455.3 7.5 copy-start.7
  455.3 7.5 copy-start.16
  610.5 54.4 %copy-start.4 = (f32[512,1024]{1,0:T(8,128)S(1)}, f32[512,1024]{1,0:T(8,128)}, u32[]{:S(2)}) copy-start(f32[512,1024]{1,0:T(8,128)} %copy-done.3) | copy-start | bytes 6291460
  664.9 8.8 %copy-start.1 = (bf16[3,16,64,512]{3,2,1,0:T(8,128)(2,1)S(1)}, bf16[3,16,64,512]{3,2,1,0:T(8,128)(2,1)}, u32[]{:S(2)}) copy-start(bf16[3,16,64,512]{3,2,1,0:T(8,128)(2,1)} %swap_to_tokens.3) | copy-start | bytes 9437188
  665.0 8.8 %copy-start.10 = (bf16[1,512,1024]{2,1,0:T(8,128)(2,1)S(1)}, bf16[1,512,1024]{2,1,0:T(8,128)(2,1)}, u32[]{:S(2)}) copy-start(bf16[1,512,1024]{2,1,0:T(8,128)(2,1)} %param.18) | copy-start | bytes 3145732
  680.6 2.8 copy-start
  683.4 69.6 %copy-start.13 = (f32[32,1024]{1,0:T(8,128)S(1)}, f32[32,1024]{1,0:T(8,128)}, u32[]{:S(2)}) copy-start(f32[32,1024]{1,0:T(8,128)} %get-tuple-element.120) | copy-start | bytes 393220
  683.4 70.3 %copy-start.12 = (f32[32,4096]{1,0:T(8,128)S(1)}, f32[32,4096]{1,0:T(8,128)}, u32[]{:S(2)}) copy-start(f32[32,4096]{1,0:T(8,128)} %get-tuple-element.121) | copy-start | bytes 1572868
  751.2 3.3 copy-start.11

commit v3 on v2

--- a/solution.py
+++ b/solution.py
@@ -354,6 +354,15 @@
         lane = lax.axis_index("head")
         self.y = lane // 2
         self.c = lax.rem(lane, 2)
+        self.index = self.z * 4 + lane
+        self.group = blks * 4
+
+    def peer(self, step):
+        index = lax.rem(self.index + step, self.group)
+        return index, self.member(index)
+
+    def member(self, index):
+        return {"seq": self.x, "blk": index // 4, "head": lax.rem(index, 4)}
 
     def at(self, x=None, z=None, y=None, c=None):
         x = self.x if x is None else x
@@ -419,13 +428,17 @@
 ALL = slice(None)
 
 
+def share_line(me, wires, ref, piece):
+    own = view(ref, (me.x, me.z, me.y, me.c), piece)
+    return [wires.copy(own, own, me.at(z=peer)) for peer in me.column()]
+
+
 class Gather:
     WIRES = 7
 
-    def __init__(self, me, wires, ref, piece, turned):
+    def __init__(self, me, wires, ref, piece, turned, ready=False):
         x, z, y, c = me.x, me.z, me.y, me.c
-        own = view(ref, (x, z, y, c), piece)
-        self.first = [wires.copy(own, own, me.at(z=peer)) for peer in me.column()]
+        self.first = [] if ready else share_line(me, wires, ref, piece)
         line = view(ref, (x, ALL, y, c), piece)
         if turned:
             half, rest = view(ref, (ALL, ALL, y, c), piece), view(ref, (ALL, ALL, 1 - y, c), piece)
@@ -466,8 +479,13 @@
     def __init__(self, me, wires, ref, piece, turned, own, own_sem, r0, r1, r2, r3, out, out_piece):
         x, z, y, c = me.x, me.z, me.y, me.c
         self.place, self.turned, self.out, self.out_piece = me, turned, out, out_piece
-        self.own, self.r0, self.r1, self.r2, self.r3 = own, r0, r1, r2, r3
-        self.load = pltpu.make_async_copy(view(ref, (ALL, ALL, ALL, c), piece), own, own_sem)
+        self.r0, self.r1, self.r2, self.r3 = r0, r1, r2, r3
+        if own is None:
+            self.load = None
+            self.own = lambda at: ref[at + (c, pl.ds(*piece[0]), pl.ds(*piece[1]))]
+        else:
+            self.load = pltpu.make_async_copy(view(ref, (ALL, ALL, ALL, c), piece), own, own_sem)
+            self.own = lambda at: own[at]
         self.zero = wires.copy(view(ref, (ALL, ALL, ALL, 1 - c), piece), r0, me.at(c=1 - c))
         if turned:
             self.one = wires.copy(r0.at[:, :, 1 - y], r1, me.at(y=1 - y))
@@ -494,13 +512,14 @@
         elif index == 1:
             self.load.start()
         elif index == 2:
-            self.load.wait()
+            if self.load is not None:
+                self.load.wait()
             self.zero.wait_recv()
 
             @pl.loop(0, 4 * blks)
             def _(i):
                 at = (i // (2 * blks), lax.rem(i // 2, blks), lax.rem(i, 2))
-                add(at, self.own[at])
+                add(at, self.own(at))
 
             self.one.start()
         elif index == 3:
@@ -537,117 +556,49 @@
                 copy.wait_send()
 
 
-def reduce_scratch(units, blks, dtype=jnp.bfloat16):
+def reduce_scratch(units, blks, cols=UNIT, dtype=jnp.bfloat16):
+    turned = units // 2
     return [
-        pltpu.VMEM((2, 2, blks, 2, EDGE, UNIT), dtype),
-        pltpu.VMEM((units, 2, blks, 2, EDGE, UNIT), dtype),
-        pltpu.VMEM((units // 2 + units % 2, blks, 2, EDGE, UNIT), dtype),
-        pltpu.VMEM((max(units // 2, 1), 2, blks, EDGE, UNIT), dtype),
-        pltpu.VMEM((units, blks, EDGE, UNIT), dtype),
-        pltpu.VMEM((units, blks - 1, EDGE, UNIT), dtype),
-        pltpu.SemaphoreType.DMA((2,)),
+        pltpu.VMEM((units, 2, blks, 2, EDGE, cols), dtype),
+        pltpu.VMEM((units - turned, blks, 2, EDGE, cols), dtype),
+        pltpu.VMEM((turned, 2, blks, EDGE, cols), dtype),
+        pltpu.VMEM((units, blks, EDGE, cols), dtype),
+        pltpu.VMEM((units, blks - 1, EDGE, cols), dtype),
         pltpu.SemaphoreType.DMA((Reduce.WIRES * units,)),
         pltpu.SemaphoreType.DMA((Reduce.WIRES * units,)),
     ]
 
 
-def final_kernel(blks, devices, grad, sums, out, sums_out, own, r0, r1a, r1b, r2, r3, own_sem, send, recv, landed, sums_send, sums_recv, sums_sem):
+def weight_units(edges):
+    out_rows, expand_cols, reduce_rows = edges
+    units = [(0, ((0, out_rows), (0, UNIT)))]
+    expand = [(1, ((0, EDGE), (first, UNIT))) for first in range(0, expand_cols, UNIT)]
+    reduce = [(2, ((first, EDGE), (0, UNIT))) for first in range(0, reduce_rows, EDGE)]
+    for pair in zip(expand, reduce):
+        units.extend(pair)
+    return units
+
+
+EARLY = 5
+
+
+def first_kernel(
+    blks, devices, wq, wk, wv, wo, we, wr, vec, out, go, ge, gr, vec_out,
+    own_sem, send, recv, vec_send, vec_recv,
+):
     me = Place(blks)
     index, others = me.others(devices)
-    greet(others)
-    wires = Wires(send, recv)
-    units = r0.shape[0]
-    plan = [
-        Reduce(
-            me,
-            wires,
-            grad,
-            ((0, EDGE), (unit * UNIT, UNIT)),
-            unit % 2 == 1,
-            own.at[unit % 2],
-            own_sem.at[unit % 2],
-            r0.at[unit],
-            (r1b if unit % 2 else r1a).at[unit // 2],
-            r2.at[unit],
-            r3.at[unit],
-            out,
-            ((0, EDGE), (unit * UNIT, UNIT)),
-        )
-        for unit in range(units)
-    ]
-    small = []
-    for slot, device in enumerate(others):
-        peer = (device["seq"] * blks + device["blk"]) * 4 + device["head"]
-        small.append(
-            pltpu.make_async_remote_copy(
-                src_ref=sums.at[peer],
-                dst_ref=landed.at[slot],
-                send_sem=sums_send.at[slot],
-                recv_sem=sums_recv.at[slot],
-                device_id=device,
-                device_id_type=MESH,
-            )
-        )
-    for unit in plan:
-        unit.stage(0)
-    plan[0].stage(1)
-    plan[1].stage(1)
-    for copy in small:
-        copy.start()
-    mine = pltpu.make_async_copy(sums.at[index], landed.at[devices - 1], sums_sem)
-    mine.start()
-    for number, unit in enumerate(plan):
-        unit.stage(2)
-        if number + 2 < units:
-            plan[number + 2].stage(1)
-    for index in (3, 4):
-        for unit in plan:
-            unit.stage(index)
-    mine.wait()
-    for copy in small:
-        copy.wait()
-    sums_out[...] = jnp.sum(landed[...], axis=0)
-    for unit in plan:
-        unit.stage(5)
-
-
-def final_reduce(grad, sums, collective_id):
-    seqs, blks, heads = (lax.axis_size(name) for name in EVERY)
-    devices = seqs * blks * heads
-    units = grad.shape[1] // UNIT
-    shares = grad.reshape(seqs, blks, heads // 2, 2, EDGE, grad.shape[1])
-    return pl.pallas_call(
-        functools.partial(final_kernel, blks, devices),
-        out_shape=[
-            jax.ShapeDtypeStruct((EDGE, grad.shape[1]), jnp.float32),
-            jax.ShapeDtypeStruct(sums.shape[1:], jnp.float32),
-        ],
-        in_specs=[pl.BlockSpec(memory_space=pl.ANY)] * 2,
-        out_specs=[pl.BlockSpec(memory_space=pltpu.VMEM)] * 2,
-        scratch_shapes=[
-            *reduce_scratch(units, blks),
-            pltpu.VMEM((devices,) + sums.shape[1:], jnp.float32),
-            pltpu.SemaphoreType.DMA((devices,)),
-            pltpu.SemaphoreType.DMA((devices,)),
-            pltpu.SemaphoreType.DMA,
-        ],
-        compiler_params=pltpu.CompilerParams(
-            collective_id=collective_id, has_side_effects=True, vmem_limit_bytes=40 * 2**20
-        ),
-        name="final_reduce",
-    )(shares, sums)
-
-
-def first_kernel(blks, devices, wq, wk, wv, vec, out, vec_out, own_sem, send, recv, vec_send, vec_recv):
-    me = Place(blks)
-    index, others = me.others(devices)
-    local = [
-        pltpu.make_async_copy(
-            ref, out.at[me.x, me.z, me.y, me.c, :, pl.ds(unit * UNIT, UNIT)], own_sem.at[unit]
-        )
+    here = (me.x, me.z, me.y, me.c)
+    pairs = [
+        (ref, out.at[here + (ALL, pl.ds(unit * UNIT, UNIT))])
         for unit, ref in enumerate((wq, wk, wv))
     ]
-    local.append(pltpu.make_async_copy(vec, vec_out.at[index], own_sem.at[3]))
+    pairs += [(ref, whole.at[here]) for ref, whole in zip((wo, we, wr), (go, ge, gr))]
+    pairs.append((vec, vec_out.at[index]))
+    local = [
+        pltpu.make_async_copy(source, target, own_sem.at[number])
+        for number, (source, target) in enumerate(pairs)
+    ]
     for copy in local:
         copy.start()
     greet(others)
@@ -658,6 +609,11 @@
         Gather(me, wires, out, ((0, EDGE), (half * UNIT // 2, UNIT // 2)), half % 2 == 1)
         for half in range(6)
     ]
+    wholes = (go, ge, gr)
+    units = weight_units((wo.shape[0], we.shape[1], wr.shape[0]))
+    lines = []
+    for which, piece in units[:EARLY]:
+        lines += share_line(me, wires, wholes[which], piece)
     small = []
     for slot, device in enumerate(others):
         small.append(
@@ -680,73 +636,160 @@
             if 1 <= index <= 4:
                 for unit in plan[2 * pair : 2 * pair + 2]:
                     unit.stage(index)
-    for copy in small:
+        if wave == 0:
+            for copy in lines:
+                copy.start()
+    for copy in lines + small:
         copy.wait()
 
 
-def first_gather(wq, wk, wv, vec, collective_id):
+def first_gather(wq, wk, wv, shares, vec, collective_id):
     seqs, blks, heads = (lax.axis_size(name) for name in EVERY)
     devices = seqs * blks * heads
+    lead = (seqs, blks, heads // 2, 2)
+    wires = 6 * Gather.WIRES + EARLY * (blks - 1)
     return pl.pallas_call(
         functools.partial(first_kernel, blks, devices),
-        out_shape=[
-            jax.ShapeDtypeStruct((seqs, blks, heads // 2, 2, EDGE, 3 * UNIT), wq.dtype),
-            jax.ShapeDtypeStruct((devices,) + vec.shape, vec.dtype),
-        ],
-        in_specs=[pl.BlockSpec(memory_space=pl.ANY)] * 4,
-        out_specs=[pl.BlockSpec(memory_space=pl.ANY)] * 2,
+        out_shape=[jax.ShapeDtypeStruct(lead + (EDGE, 3 * UNIT), wq.dtype)]
+        + [jax.ShapeDtypeStruct(lead + share.shape, share.dtype) for share in shares]
+        + [jax.ShapeDtypeStruct((devices,) + vec.shape, vec.dtype)],
+        in_specs=[pl.BlockSpec(memory_space=pl.ANY)] * 7,
+        out_specs=[pl.BlockSpec(memory_space=pl.ANY)] * 5,
         scratch_shapes=[
-            pltpu.SemaphoreType.DMA((4,)),
-            pltpu.SemaphoreType.DMA((6 * Gather.WIRES,)),
-            pltpu.SemaphoreType.DMA((6 * Gather.WIRES,)),
+            pltpu.SemaphoreType.DMA((7,)),
+            pltpu.SemaphoreType.DMA((wires,)),
+            pltpu.SemaphoreType.DMA((wires,)),
             pltpu.SemaphoreType.DMA((devices,)),
             pltpu.SemaphoreType.DMA((devices,)),
         ],
         compiler_params=pltpu.CompilerParams(collective_id=collective_id, has_side_effects=True),
         name="first_gather",
-    )(wq, wk, wv, vec)
+    )(wq, wk, wv, *shares, vec)
 
 
 LOG2E = 1.4426950408889634
 BY_LAST = (((1,), (1,)), ((), ()))
 
 
-def weight_units(edges):
-    out_rows, expand_cols, reduce_rows = edges
-    units = [(0, ((0, out_rows), (0, UNIT)))]
-    expand = [(1, ((0, EDGE), (first, UNIT))) for first in range(0, expand_cols, UNIT)]
-    reduce = [(2, ((first, EDGE), (0, UNIT))) for first in range(0, reduce_rows, EDGE)]
-    for pair in zip(expand, reduce):
-        units.extend(pair)
-    return units
+def lanes(ref, lead, first, width):
+    return ref.at[tuple(lead) + (pl.ds(pl.multiple_of(first, width), width),)]
+
+
+def wire(source, target, send_sem, recv_sem, device):
+    return pltpu.make_async_remote_copy(
+        src_ref=source,
+        dst_ref=target,
+        send_sem=send_sem,
+        recv_sem=recv_sem,
+        device_id=device,
+        device_id_type=MESH,
+    )
 
 
 def attn_fwd_kernel(
-    blks, rows, cols, q_ref, k_ref, v_ref, down_ref, across_ref, wo, we, wr,
-    p_ref, tail_ref, o_ref, inv_ref, go, ge, gr,
-    keys, values, s0, s1, m0, m1, own_sem, send, recv,
+    blks, rows, cols, qkv_ref, down_ref, across_ref, go_in, ge_in, gr_in,
+    p_ref, tail_ref, o_ref, inv_ref, kept_ref, tokens_ref, go, ge, gr,
+    land, keys, values, s0, s1, m0, m1,
+    own_sem, kv_send, kv_recv, q_send, q_recv, o_send, o_recv, send, recv,
 ):
     step, steps = pl.program_id(0), pl.num_programs(0)
-    length, long = q_ref.shape[1], p_ref.shape[1]
-    tail, chunks, blocks = length - long, long // cols, long // rows
+    length, long = land.shape[2], p_ref.shape[1]
+    width = 2 * rows
+    tail, chunks = length - long, long // cols
+    main = long // width
     scale = LOG2E * HEAD_DIM**-0.5
 
     me = Place(blks)
+    group = me.group
+
+    def block_at(turn):
+        return lax.rem(lax.rem(me.index, main) + turn, main)
+
+    def ahead(block):
+        return lax.rem(block + group - me.index, group)
+
+    kv_copies, q_copies = [], []
+    for ahead_by in range(1, group):
+        peer, device = me.peer(group - ahead_by)
+        kv_copies.append(
+            wire(
+                qkv_ref.at[1:3, peer],
+                lanes(land, (pl.ds(1, 2), ALL), me.index * width, width),
+                kv_send.at[ahead_by],
+                kv_recv.at[ahead_by],
+                device,
+            )
+        )
+        q_copies.append(
+            wire(
+                qkv_ref.at[0, peer],
+                lanes(land, (0, ALL), me.index * width, width),
+                q_send.at[ahead_by],
+                q_recv.at[ahead_by],
+                device,
+            )
+        )
+    own_in = pltpu.make_async_copy(
+        qkv_ref.at[:, me.index],
+        lanes(land, (ALL, ALL), me.index * width, width),
+        own_sem.at[0],
+    )
+    keep = pltpu.make_async_copy(land, kept_ref, own_sem.at[1])
+
+    def await_queries(block):
+        @pl.when(block != me.index)
+        def _():
+            wire(
+                qkv_ref.at[0, block],
+                lanes(land, (0, ALL), block * width, width),
+                q_send.at[0],
+                q_recv.at[ahead(block)],
+                me.member(block),
+            ).wait_recv()
+
+    def send_block(block, slot, start):
+        source = lanes(o_ref, (ALL,), block * width, width)
+        remote = wire(
+            source,
+            tokens_ref.at[me.index],
+            o_send.at[slot],
+            o_recv.at[lax.rem(me.index + group - block, group)],
+            me.member(block),
+        )
+        local = pltpu.make_async_copy(source, tokens_ref.at[me.index], own_sem.at[2])
+
+        @pl.when(block != me.index)
+        def _():
+            if start:
+                remote.start()
+            else:
+                remote.wait_send()
+
+        @pl.when(block == me.index)
+        def _():
+            if start:
+                local.start()
+            else:
+                local.wait()
+
     wires = Wires(send, recv)
-    shares, wholes = (wo, we, wr), (go, ge, gr)
-    units = weight_units((wo.shape[0], we.shape[1], wr.shape[0]))
+    wholes = (go, ge, gr)
+    units = weight_units((go.shape[4], ge.shape[5], gr.shape[4]))
     plan = [
-        Gather(me, wires, wholes[which], piece, number % 2 == 1)
+        Gather(me, wires, wholes[which], piece, number % 2 == 1, number < EARLY)
         for number, (which, piece) in enumerate(units)
     ]
-    moves = {0: []}
-    for number, unit in enumerate(plan):
-        begin = number if number < 2 else number - 1
-        for stage, at in enumerate((begin, begin + 1, begin + 2, begin + 4, blocks)):
-            moves.setdefault(min(at, blocks // 2 - 1), []).append((stage, number, unit))
+    late = len(units) - EARLY
+    moves = {}
+    for number in range(late):
+        for stage, at in enumerate((2, 6 + number // 2, 8 + number // 2)):
+            moves.setdefault(at, []).append((plan[EARLY + number], stage))
+        moves.setdefault(12, []).append((plan[EARLY + number], 3))
+    for number in range(EARLY):
+        moves.setdefault(1 + number // 2, []).append((plan[number], 3))
 
     def take_queries(start):
-        part = q_ref[:, pl.ds(pl.multiple_of(start, rows), rows)].astype(jnp.float32) * scale
+        part = land[0, :, pl.ds(pl.multiple_of(start, rows), rows)].astype(jnp.float32) * scale
         high = part.astype(jnp.bfloat16).astype(jnp.float32)
         return jnp.concatenate([high, part - high], 0).T.astype(jnp.bfloat16)
 
@@ -782,50 +825,62 @@
 
     @pl.when(step == 0)
     def _():
-        local = [
-            pltpu.make_async_copy(share, whole.at[me.x, me.z, me.y, me.c], own_sem.at[number])
-            for number, (share, whole) in enumerate(zip(shares, wholes))
-        ]
-        for copy in local:
+        own_in.start()
+        greet([me.peer(by)[1] for by in range(1, group)] + [me.at(x=1 - me.x)])
+        for copy in kv_copies:
             copy.start()
-        keys[0:HEAD_DIM, :] = k_ref[...]
-        keys[HEAD_DIM:, :] = k_ref[...]
-        values[0:HEAD_DIM, :] = v_ref[...]
+        for unit in plan[:EARLY]:
+            unit.stage(1)
+        for copy in q_copies:
+            copy.start()
+        for unit in plan[:EARLY]:
+            unit.stage(2)
+        own_in.wait()
+        for copy in kv_copies:
+            copy.wait_recv()
+        keys[0:HEAD_DIM, :] = land[1]
+        keys[HEAD_DIM:, :] = land[1]
+        values[0:HEAD_DIM, :] = land[2]
         values[HEAD_DIM:, :] = (
             (lax.broadcasted_iota(jnp.int32, (16, length), 0) == 0)
             .astype(jnp.float32)
             .astype(jnp.bfloat16)
         )
-        greet(me.near())
-        for copy in local:
-            copy.wait()
-
-    for at, todo in sorted(moves.items()):
-
-        @pl.when(step == at)
-        def _():
-            for stage, number, unit in sorted(todo, key=lambda entry: (-entry[0], entry[1])):
-                if stage < 4:
-                    unit.stage(stage)
-
-    @pl.when(step == 0)
-    def _():
-        queries, peak = take_queries(0), None
+        await_queries(block_at(0))
+        queries, peak = take_queries(block_at(0) * width), None
         for j in range(chunks):
             peak = score(queries, s0, j, peak)
         keep_peak(m0, peak)
 
+    for at, todo in sorted(moves.items()):
+
+        @pl.when(step == at)
+        def _():
+            for unit, stage in todo:
+                unit.stage(stage)
+
+    block = block_at(step)
+    later = block_at(jnp.minimum(step + 1, steps - 1))
+
+    @pl.when(step < steps - 1)
+    def _():
+        await_queries(later)
+
     for half, (old, old_peak, new, new_peak) in enumerate(((s0, m0, s1, m1), (s1, m1, s0, m0))):
-        queries = take_queries(jnp.minimum(2 * step + half + 1, blocks - 1) * rows)
+        queries = take_queries(block * width + rows if half == 0 else later * width)
         total, peak = None, None
         for j in range(chunks):
             total = weigh(old, old_peak, j, half * rows, total)
             peak = score(queries, new, j, peak)
         keep_peak(new_peak, peak)
-        finish(total, (2 * step + half) * rows)
+        finish(total, block * width + half * rows)
+    send_block(block, step, True)
 
     @pl.when(step == steps - 1)
     def _():
+        for number in range(tail // width):
+            await_queries(main + number)
+        keep.start()
         for first in range(0, tail, rows):
             queries = take_queries(long + first)
             found = jnp.dot(queries, keys[:, long:], preferred_element_type=jnp.float32)
@@ -838,46 +893,70 @@
                 values[:, long:], weights, BY_LAST, preferred_element_type=jnp.float32
             )
             finish(total, long + first)
+            if (first + rows) % width == 0:
+                number = main + first // width
+                send_block(number, number, True)
         for unit in plan:
             unit.stage(4)
+        for copy in kv_copies + q_copies:
+            copy.wait_send()
+        for turn in range(main):
+            send_block(block_at(turn), turn, False)
+        for number in range(main, group):
+            send_block(number, number, False)
+        for ahead_by in range(1, group):
+            source, device = me.peer(ahead_by)
+            wire(
+                lanes(o_ref, (ALL,), source * width, width),
+                tokens_ref.at[source],
+                o_send.at[0],
+                o_recv.at[ahead_by],
+                device,
+            ).wait_recv()
+        keep.wait()
 
 
 def once(shape):
     return pl.BlockSpec(shape, lambda step: (0,) * len(shape), pipeline_mode=pl.Buffered(1))
 
 
-def attn_fwd(query, key, value, seg, long, shares, collective_id, rows=256, cols=1024):
+def attn_fwd(qkv, seg, long, wholes, collective_id, cols=1024):
     blks = lax.axis_size("blk")
-    lead = (lax.axis_size("seq"), blks, lax.axis_size("head") // 2, 2)
-    length = query.shape[1]
+    group, width = qkv.shape[1], qkv.shape[3]
+    rows = width // 2
+    length = group * width
     tail = length - long
     down = jnp.broadcast_to(seg[:, None], (tail, 128))
     across = jnp.broadcast_to(seg[None, :], (8, tail))
     anywhere = pl.BlockSpec(memory_space=pl.ANY)
     wires = Gather.WIRES * len(
-        weight_units((shares[0].shape[0], shares[1].shape[1], shares[2].shape[0]))
-    )
+        weight_units((wholes[0].shape[4], wholes[1].shape[5], wholes[2].shape[4]))
+    )
+    kept = jax.ShapeDtypeStruct((3, HEAD_DIM, length), jnp.bfloat16)
+    pair = [pltpu.SemaphoreType.DMA((group,))] * 2
     return pl.pallas_call(
         functools.partial(attn_fwd_kernel, blks, rows, cols),
-        grid=(long // rows // 2,),
-        in_specs=[once((HEAD_DIM, length))] * 3
-        + [once((tail, 128)), once((8, tail))]
-        + [anywhere] * 3,
+        grid=(long // width,),
+        in_specs=[anywhere, once((tail, 128)), once((8, tail))] + [anywhere] * 3,
         out_specs=[
-            pl.BlockSpec((2 * rows, long), lambda step: (step, 0)),
+            pl.BlockSpec((width, long), lambda step: (step, 0)),
             once((tail, tail)),
             once((HEAD_DIM, length)),
             once((8, length)),
         ]
-        + [anywhere] * 3,
+        + [anywhere] * 5,
         out_shape=[
             jax.ShapeDtypeStruct((long, long), jnp.bfloat16),
             jax.ShapeDtypeStruct((tail, tail), jnp.bfloat16),
             jax.ShapeDtypeStruct((HEAD_DIM, length), jnp.bfloat16),
             jax.ShapeDtypeStruct((8, length), jnp.float32),
+            kept,
+            jax.ShapeDtypeStruct((group, HEAD_DIM, width), jnp.bfloat16),
         ]
-        + [jax.ShapeDtypeStruct(lead + share.shape, share.dtype) for share in shares],
+        + [jax.ShapeDtypeStruct(whole.shape, whole.dtype) for whole in wholes],
+        input_output_aliases={3: 6, 4: 7, 5: 8},
         scratch_shapes=[
+            pltpu.VMEM(kept.shape, kept.dtype),
             pltpu.VMEM((2 * HEAD_DIM, length), jnp.bfloat16),
             pltpu.VMEM((HEAD_DIM + 16, length), jnp.bfloat16),
             pltpu.VMEM((rows, long), jnp.float32),
@@ -885,6 +964,9 @@
             pltpu.VMEM((rows, 128), jnp.float32),
             pltpu.VMEM((rows, 128), jnp.float32),
             pltpu.SemaphoreType.DMA((3,)),
+            *pair,
+            *pair,
+            *pair,
             pltpu.SemaphoreType.DMA((wires,)),
             pltpu.SemaphoreType.DMA((wires,)),
         ],
@@ -897,24 +979,82 @@
             transcendentals=long * long,
         ),
         name="attn_fwd",
-    )(query, key, value, down, across, *shares)
+    )(qkv, down, across, *wholes)
 
 
 def attn_bwd_kernel(
-    blks, rows, cols, p_ref, tail_ref, q_ref, k_ref, v_ref, o_ref, do_ref, inv_ref, wo, we, wr,
-    dq_ref, dk_ref, dv_ref, go, ge, gr,
-    values, dk_sum, dv_sum, own, r0, r1a, r1b, r2, r3, own_sem, send, recv,
+    blks, rows, cols, p_ref, tail_ref, qkv_ref, o_ref, inv_ref, grads_ref, wo, we, wr,
+    dkv_ref, tokens_ref, go, ge, gr,
+    land, dq_out, values, dk_sum, dv_sum, own, r0, r1a, r1b, r2, r3, send, recv,
+    own_sem, do_send, do_recv, dq_send, dq_recv,
 ):
     step, steps = pl.program_id(0), pl.num_programs(0)
-    length, long = q_ref.shape[1], p_ref.shape[1]
+    length, long = land.shape[1], p_ref.shape[1]
     tail, chunks = length - long, long // cols
+    main = long // rows
     scale = HEAD_DIM**-0.5
 
     me = Place(blks)
+    group = me.group
+
+    def block_at(turn):
+        return lax.rem(lax.rem(me.index, main) + turn, main)
+
+    do_copies = []
+    for ahead_by in range(1, group):
+        peer, device = me.peer(group - ahead_by)
+        do_copies.append(
+            wire(
+                grads_ref.at[peer],
+                lanes(land, (ALL,), me.index * rows, rows),
+                do_send.at[ahead_by],
+                do_recv.at[ahead_by],
+                device,
+            )
+        )
+    own_in = pltpu.make_async_copy(
+        grads_ref.at[me.index], lanes(land, (ALL,), me.index * rows, rows), own_sem.at[2]
+    )
+
+    def await_grads(block):
+        @pl.when(block != me.index)
+        def _():
+            wire(
+                grads_ref.at[block],
+                lanes(land, (ALL,), block * rows, rows),
+                do_send.at[0],
+                do_recv.at[lax.rem(block + group - me.index, group)],
+                me.member(block),
+            ).wait_recv()
+
+    def send_block(block, slot, start):
+        source = lanes(dq_out, (ALL,), block * rows, rows)
+        remote = wire(
+            source,
+            tokens_ref.at[me.index],
+            dq_send.at[slot],
+            dq_recv.at[lax.rem(me.index + group - block, group)],
+            me.member(block),
+        )
+        local = pltpu.make_async_copy(source, tokens_ref.at[me.index], own_sem.at[3])
+
+        @pl.when(block != me.index)
+        def _():
+            if start:
+                remote.start()
+            else:
+                remote.wait_send()
+
+        @pl.when(block == me.index)
+        def _():
+            if start:
+                local.start()
+            else:
+                local.wait()
+
     wires = Wires(send, recv)
     partials, totals = (wo, we, wr), (go, ge, gr)
     units = weight_units((wo.shape[4], we.shape[5], wr.shape[4]))
-    last = long // rows - 1
     plan, moves = [], {}
     for number, (which, piece) in enumerate(units):
         turned = number % 2 == 1
@@ -934,12 +1074,13 @@
             piece,
         )
         plan.append(unit)
-        for stage, at in enumerate((0, number, number + 1, number + 3, number + 4)):
-            moves.setdefault(min(at, last), []).append((stage, number, unit))
+        pair = number // 2
+        for stage, at in enumerate((0, pair, pair + 1, 2 * pair + 3, 2 * pair + 5)):
+            moves.setdefault(min(at, main - 1), []).append((stage, number, unit))
 
     def prepare(start, width):
         place = pl.ds(pl.multiple_of(start, width), width)
-        grads, inverse = do_ref[:, place].astype(jnp.float32), inv_ref[:1, place]
+        grads, inverse = land[:, place].astype(jnp.float32), inv_ref[:1, place]
         delta = -jnp.sum(grads * o_ref[:, place].astype(jnp.float32), axis=0, keepdims=True)
         delta = delta * inverse
         high = delta.astype(jnp.bfloat16).astype(jnp.float32)
@@ -947,7 +1088,7 @@
         extra = jnp.where(row == 0, high, jnp.where(row == 1, delta - high, 0.0))
         grads = grads * inverse
         wide = jnp.concatenate([grads, extra], 0).T.astype(jnp.bfloat16)
-        return wide, grads.astype(jnp.bfloat16), q_ref[:, place]
+        return wide, grads.astype(jnp.bfloat16), qkv_ref[0, :, place]
 
     def part(wide, grads, queries, weights, keys_here, values_here, dq):
         dp = jnp.dot(wide, values_here, preferred_element_type=jnp.float32)
@@ -959,7 +1100,10 @@
 
     @pl.when(step == 0)
     def _():
-        greet(me.near())
+        own_in.start()
+        greet([me.peer(by)[1] for by in range(1, group)] + [me.at(x=1 - me.x)])
+        for copy in do_copies:
+            copy.start()
 
     for at, todo in sorted(moves.items()):
 
@@ -970,7 +1114,7 @@
 
     @pl.when(step == 0)
     def _():
-        values[0:HEAD_DIM, :] = v_ref[...]
+        values[0:HEAD_DIM, :] = qkv_ref[2]
         values[HEAD_DIM:, :] = (
             (lax.broadcasted_iota(jnp.int32, (16, length), 0) < 2)
             .astype(jnp.float32)
@@ -978,67 +1122,103 @@
         )
         dk_sum[...] = jnp.zeros_like(dk_sum)
         dv_sum[...] = jnp.zeros_like(dv_sum)
-
-    wide, grads, queries = prepare(step * rows, rows)
+        own_in.wait()
+
+    block = block_at(step)
+    await_grads(block)
+    wide, grads, queries = prepare(block * rows, rows)
     dq = None
     for j in range(chunks):
         here = slice(j * cols, (j + 1) * cols)
         dq, dk, dv = part(
-            wide, grads, queries, p_ref[:, here], k_ref[:, here], values[:, here], dq
+            wide, grads, queries, p_ref[:, here], qkv_ref[1, :, here], values[:, here], dq
         )
         dk_sum[:, here] += dk
         dv_sum[:, here] += dv
-    dq_ref[:, pl.ds(pl.multiple_of(step * rows, rows), rows)] = (dq * scale).astype(jnp.bfloat16)
+    dq_out[:, pl.ds(pl.multiple_of(block * rows, rows), rows)] = (dq * scale).astype(jnp.bfloat16)
+    send_block(block, step, True)
 
     @pl.when(step == steps - 1)
     def _():
-        for first in range(0, tail, rows):
+        for number in range(main, group):
+            await_grads(number)
+            first = (number - main) * rows
             wide, grads, queries = prepare(long + first, rows)
             dq, dk, dv = part(
                 wide,
                 grads,
                 queries,
                 tail_ref[first : first + rows, :],
-                k_ref[:, long:],
+                qkv_ref[1, :, long:],
                 values[:, long:],
                 None,
             )
             dk_sum[:, long:] += dk
             dv_sum[:, long:] += dv
-            dq_ref[:, long + first : long + first + rows] = (dq * scale).astype(jnp.bfloat16)
-        dk_ref[...] = (dk_sum[...] * scale).astype(jnp.bfloat16)
-        dv_ref[...] = dv_sum[...].astype(jnp.bfloat16)
+            dq_out[:, long + first : long + first + rows] = (dq * scale).astype(jnp.bfloat16)
+            send_block(number, number, True)
+        dkv_ref[0] = (dk_sum[...] * scale).astype(jnp.bfloat16)
+        dkv_ref[1] = dv_sum[...].astype(jnp.bfloat16)
         for unit in plan:
             unit.stage(5)
+        for copy in do_copies:
+            copy.wait_send()
+        for turn in range(main):
+            send_block(block_at(turn), turn, False)
+        for number in range(main, group):
+            send_block(number, number, False)
+        for ahead_by in range(1, group):
+            source, device = me.peer(ahead_by)
+            wire(
+                lanes(dq_out, (ALL,), source * rows, rows),
+                tokens_ref.at[source],
+                dq_send.at[0],
+                dq_recv.at[ahead_by],
+                device,
+            ).wait_recv()
 
 
 def attn_bwd(
-    probs, tail_probs, query, key, value, attn, grad_attn, inv_total, long, partials,
-    collective_id, rows=512, cols=1024,
+    probs, tail_probs, kept, attn, inv_total, grad_attn, long, partials, collective_id, cols=1024
 ):
     blks = lax.axis_size("blk")
     lead = (lax.axis_size("seq"), blks, lax.axis_size("head") // 2, 2)
     devices = math.prod(lead)
-    length = query.shape[1]
+    length = kept.shape[2]
     tail = length - long
+    group, _, rows = grad_attn.shape
     anywhere = pl.BlockSpec(memory_space=pl.ANY)
     edges = [(partial.shape[0] // devices, partial.shape[1]) for partial in partials]
     units = len(weight_units((edges[0][0], edges[1][1], edges[2][0])))
-    narrow = jax.ShapeDtypeStruct((HEAD_DIM, length), jnp.bfloat16)
+    pair = [pltpu.SemaphoreType.DMA((group,))] * 2
     return pl.pallas_call(
         functools.partial(attn_bwd_kernel, blks, rows, cols),
         grid=(long // rows,),
-        in_specs=[pl.BlockSpec((rows, long), lambda step: (step, 0)), once((tail, tail))]
-        + [once((HEAD_DIM, length))] * 5
-        + [once((8, length))]
-        + [anywhere] * 3,
-        out_specs=[once((HEAD_DIM, length))] * 3 + [once(edge) for edge in edges],
-        out_shape=[narrow] * 3 + [jax.ShapeDtypeStruct(edge, jnp.float32) for edge in edges],
+        in_specs=[
+            pl.BlockSpec((rows, long), lambda step: (step, 0)),
+            once((tail, tail)),
+            once(kept.shape),
+            once((HEAD_DIM, length)),
+            once((8, length)),
+        ]
+        + [anywhere] * 4,
+        out_specs=[once((2, HEAD_DIM, length)), anywhere] + [once(edge) for edge in edges],
+        out_shape=[
+            jax.ShapeDtypeStruct((2, HEAD_DIM, length), jnp.bfloat16),
+            jax.ShapeDtypeStruct((group, HEAD_DIM, rows), jnp.bfloat16),
+        ]
+        + [jax.ShapeDtypeStruct(edge, jnp.float32) for edge in edges],
         scratch_shapes=[
+            pltpu.VMEM((HEAD_DIM, length), jnp.bfloat16),
+            pltpu.VMEM((HEAD_DIM, length), jnp.bfloat16),
             pltpu.VMEM((HEAD_DIM + 16, length), jnp.bfloat16),
             pltpu.VMEM((HEAD_DIM, length), jnp.float32),
             pltpu.VMEM((HEAD_DIM, length), jnp.float32),
+            pltpu.VMEM((2, 2, blks, 2, EDGE, UNIT), jnp.bfloat16),
             *reduce_scratch(units, blks),
+            pltpu.SemaphoreType.DMA((4,)),
+            *pair,
+            *pair,
         ],
         compiler_params=pltpu.CompilerParams(
             collective_id=collective_id, has_side_effects=True, vmem_limit_bytes=62 * 2**20
@@ -1048,85 +1228,205 @@
         ),
         name="attn_bwd",
     )(
-        probs, tail_probs, query, key, value, attn, grad_attn, inv_total,
+        probs, tail_probs, kept, attn, inv_total, grad_attn,
         *[partial.reshape(lead + edge) for partial, edge in zip(partials, edges)],
     )
 
 
-GROUP = ("blk", "head")
-
-
-def greet_group(me, count, heads):
-    barrier = pltpu.get_barrier_semaphore()
-    for step in range(1, count):
-        peer = lax.rem(me + step, count)
-        pl.semaphore_signal(
-            barrier,
-            inc=1,
-            device_id={"blk": peer // heads, "head": lax.rem(peer, heads)},
-            device_id_type=MESH,
-        )
-    pl.semaphore_wait(barrier, count - 1)
-
-
-def swap_kernel(to_heads, blks, heads, in_ref, out_ref, send_sem, recv_sem, own_sem):
-    count = blks * heads
-    me = lax.axis_index("blk") * heads + lax.axis_index("head")
-    greet_group(me, count, heads)
-    if to_heads:
-        rows = in_ref.shape[2]
-        width = in_ref.shape[3]
-        take = lambda owner: in_ref.at[:, owner]
-        place = lambda source: out_ref.at[
-            :, :, pl.ds(pl.multiple_of(source * width, width), width)
-        ]
-    else:
-        rows = in_ref.shape[1]
-        width = in_ref.shape[2] // count
-        take = lambda owner: in_ref.at[:, :, pl.ds(pl.multiple_of(owner * width, width), width)]
-        place = lambda source: out_ref.at[:, source]
-    own = pltpu.make_async_copy(take(me), place(me), own_sem)
-    own.start()
-    copies = []
-    for step in range(1, count):
-        peer = lax.rem(me + step, count)
-        copy = pltpu.make_async_remote_copy(
-            src_ref=take(peer),
-            dst_ref=place(me),
-            send_sem=send_sem.at[step],
-            recv_sem=recv_sem.at[step],
-            device_id={"blk": peer // heads, "head": lax.rem(peer, heads)},
-            device_id_type=MESH,
-        )
+def last_kernel(
+    blks, devices, dkv_ref, dq_ref, x_ref, w_ref, base_ref, sums_ref,
+    dw_out, dx_out, sums_out,
+    grads, x, xt, weights, base, turned_dx, partial, bias, landed,
+    r0, r1a, r1b, r2, r3, send, recv,
+    own_sem, kv_send, kv_recv, sums_send, sums_recv,
+):
+    me = Place(blks)
+    group = me.group
+    width = x.shape[0]
+    depth = x.shape[1]
+    index, others = me.others(devices)
+    loads = [
+        pltpu.make_async_copy(source, target, own_sem.at[number])
+        for number, (source, target) in enumerate(
+            (
+                (x_ref, x),
+                (dq_ref, grads.at[0]),
+                (w_ref, weights),
+                (base_ref, base),
+                (sums_ref, bias),
+                (dkv_ref.at[0, :, pl.ds(pl.multiple_of(me.index * width, width), width)], grads.at[1, me.index]),
+                (dkv_ref.at[1, :, pl.ds(pl.multiple_of(me.index * width, width), width)], grads.at[2, me.index]),
+            )
+        )
+    ]
+    for copy in loads:
         copy.start()
-        copies.append(copy)
-    own.wait()
-    for copy in copies:
+    greet(others)
+    kv_copies = [[], []]
+    for which in range(2):
+        for ahead_by in range(1, group):
+            peer, device = me.peer(group - ahead_by)
+            slot = which * group + ahead_by
+            copy = wire(
+                lanes(dkv_ref, (which, ALL), peer * width, width),
+                grads.at[which + 1, me.index],
+                kv_send.at[slot],
+                kv_recv.at[slot],
+                device,
+            )
+            copy.start()
+            kv_copies[which].append(copy)
+
+    wires = Wires(send, recv)
+    plan = []
+    for number in range(6):
+        tensor, half = number // 2, number % 2
+        plan.append(
+            Reduce(
+                me,
+                wires,
+                partial.at[tensor],
+                ((0, EDGE), (half * UNIT // 2, UNIT // 2)),
+                half == 1,
+                None,
+                None,
+                r0.at[number],
+                (r1b if half else r1a).at[tensor],
+                r2.at[number],
+                r3.at[number],
+                dw_out,
+                ((0, EDGE), (tensor * UNIT + half * UNIT // 2, UNIT // 2)),
+            )
+        )
+
+    def work(tensor):
+        taken = grads[tensor].reshape(depth, width)
+        for first in range(0, depth, 256):
+            term = lax.dot_general(
+                xt[first : first + 256, :], taken, BY_LAST, preferred_element_type=jnp.float32
+            ).astype(jnp.bfloat16)
+            for share in range(first // EDGE, (first + 256) // EDGE):
+                at = (share // (blks * 4), share // 4 % blks, share // 2 % 2, share % 2)
+                partial[(tensor,) + at] = term[share * EDGE - first : (share + 1) * EDGE - first]
+        for unit in plan[2 * tensor : 2 * tensor + 2]:
+            unit.stage(0)
+
+    def work_input(tensor):
+        taken = grads[tensor].reshape(depth, width)
+        for first in range(0, depth, 256):
+            term = jnp.dot(
+                weights[first : first + 256, tensor * depth : (tensor + 1) * depth],
+                taken,
+                preferred_element_type=jnp.float32,
+            )
+            if tensor == 0:
+                turned_dx[first : first + 256, :] = term
+            elif tensor == 1:
+                turned_dx[first : first + 256, :] += term
+            else:
+                total = turned_dx[first : first + 256, :] + term
+                dx_out[:, first : first + 256] = base[:, first : first + 256] + total.T
+
+    def stages(tensor, *which):
+        for stage in which:
+            for unit in plan[2 * tensor : 2 * tensor + 2]:
+                unit.stage(stage)
+
+    def note_bias(tensor, row):
+        ones = jnp.ones((8, width), jnp.bfloat16)
+        found = lax.dot_general(
+            ones, grads[tensor].reshape(depth, width), BY_LAST, preferred_element_type=jnp.float32
+        )
+        per = 128 * devices // depth
+        for owner in range(devices):
+            first = owner // per * 128
+            bias[owner, row : row + 1, :] = found[:1, first : first + 128]
+
+    loads[0].wait()
+    xt[...] = x[...].astype(jnp.float32).T.astype(jnp.bfloat16)
+    loads[1].wait()
+    work(0)
+    stages(0, 2)
+    loads[4].wait()
+    note_bias(0, 3)
+    loads[2].wait()
+    work_input(0)
+    stages(0, 3)
+    loads[5].wait()
+    for copy in kv_copies[0]:
+        copy.wait_recv()
+    work(1)
+    stages(0, 4)
+    stages(1, 2)
+    work_input(1)
+    stages(1, 3)
+    loads[6].wait()
+    for copy in kv_copies[1]:
+        copy.wait_recv()
+    work(2)
+    note_bias(2, 4)
+    small = []
+    for slot, device in enumerate(others):
+        peer = (device["seq"] * blks + device["blk"]) * 4 + device["head"]
+        copy = wire(
+            bias.at[peer], landed.at[slot], sums_send.at[slot], sums_recv.at[slot], device
+        )
+        small.append(copy)
+    stages(2, 2)
+    for copy in small:
+        copy.start()
+    stages(1, 4)
+    loads[3].wait()
+    work_input(2)
+    stages(2, 3)
+    stages(0, 5)
+    stages(2, 4)
+    for copy in small:
+        copy.wait()
+    sums_out[...] = jnp.sum(landed[...], axis=0) + bias[index]
+    stages(1, 5)
+    stages(2, 5)
+    for copy in kv_copies[0] + kv_copies[1]:
         copy.wait_send()
-        copy.wait_recv()
-
-
-def swap(values, to_heads, collective_id):
-    blks, heads = lax.axis_size("blk"), lax.axis_size("head")
-    count = blks * heads
-    parts = values.shape[0]
-    if to_heads:
-        shape = (parts, values.shape[2], values.shape[3] * count)
-    else:
-        shape = (parts, count, values.shape[1], values.shape[2] // count)
+
+
+def last_reduce(dkv, dq, x, w_qkv, base, sums, collective_id):
+    seqs, blks, heads = (lax.axis_size(name) for name in EVERY)
+    devices = seqs * blks * heads
+    group = blks * heads
+    width, depth = x.shape
+    half = UNIT // 2
     return pl.pallas_call(
-        functools.partial(swap_kernel, to_heads, blks, heads),
-        out_shape=jax.ShapeDtypeStruct(shape, values.dtype),
-        in_specs=[pl.BlockSpec(memory_space=pl.ANY)],
-        out_specs=pl.BlockSpec(memory_space=pl.ANY),
+        functools.partial(last_kernel, blks, devices),
+        out_shape=[
+            jax.ShapeDtypeStruct((EDGE, 3 * depth), jnp.float32),
+            jax.ShapeDtypeStruct((width, depth), jnp.float32),
+            jax.ShapeDtypeStruct(sums.shape[1:], jnp.float32),
+        ],
+        in_specs=[pl.BlockSpec(memory_space=pl.ANY)] * 6,
+        out_specs=[pl.BlockSpec(memory_space=pltpu.VMEM)] * 3,
         scratch_shapes=[
-            pltpu.SemaphoreType.DMA((count,)),
-            pltpu.SemaphoreType.DMA((count,)),
-            pltpu.SemaphoreType.DMA,
+            pltpu.VMEM((3, group, HEAD_DIM, width), jnp.bfloat16),
+            pltpu.VMEM((width, depth), jnp.bfloat16),
+            pltpu.VMEM((depth, width), jnp.bfloat16),
+            pltpu.VMEM((depth, 3 * depth), jnp.bfloat16),
+            pltpu.VMEM((width, depth), jnp.float32),
+            pltpu.VMEM((depth, width), jnp.float32),
+            pltpu.VMEM((3, seqs, blks, heads // 2, 2, EDGE, UNIT), jnp.bfloat16),
+            pltpu.VMEM(sums.shape, jnp.float32),
+            pltpu.VMEM((devices - 1,) + sums.shape[1:], jnp.float32),
+            *reduce_scratch(6, blks, half),
+            pltpu.SemaphoreType.DMA((7,)),
+            pltpu.SemaphoreType.DMA((2 * group,)),
+            pltpu.SemaphoreType.DMA((2 * group,)),
+            pltpu.SemaphoreType.DMA((devices,)),
+            pltpu.SemaphoreType.DMA((devices,)),
         ],
-        compiler_params=pltpu.CompilerParams(collective_id=collective_id, has_side_effects=True),
-        name="swap_to_heads" if to_heads else "swap_to_tokens",
-    )(values)
+        compiler_params=pltpu.CompilerParams(
+            collective_id=collective_id, has_side_effects=True, vmem_limit_bytes=56 * 2**20
+        ),
+        name="last_reduce",
+    )(dkv, dq, x, w_qkv, base, sums)
 
 
 def tail_segments(doc_lengths, first, rows):
@@ -1173,14 +1473,19 @@
         bias_expand,
     )
     sizes = [vector.shape[0] for vector in vectors]
-    lanes = 128
-    spare = 16 * lanes - sum(sizes)
+    lane = 128
+    spare = 16 * lane - sum(sizes)
     packed = jnp.concatenate(vectors + (jnp.zeros((spare,), layer_input.dtype),))
-    w_qkv, packed = first_gather(
-        weight_query, weight_key, weight_value, packed.reshape(16, lanes), 4
+    w_qkv, *wholes, packed = first_gather(
+        weight_query,
+        weight_key,
+        weight_value,
+        (weight_output, weight_expand, weight_reduce),
+        packed.reshape(16, lane),
+        4,
     )
     w_qkv = w_qkv.reshape(model_width, 3 * model_width)
-    packed = packed.reshape(-1, 16 * lanes).astype(jnp.float32)
+    packed = packed.reshape(-1, 16 * lane).astype(jnp.float32)
     whole, start = [], 0
     for size in sizes:
         whole.append(packed[:, start : start + size].reshape(-1))
@@ -1192,22 +1497,14 @@
         w_qkv, flat_rows, (((0,), (1,)), ((), ())), preferred_element_type=jnp.float32
     )
     qkv = (qkv + b_qkv[:, None]).astype(jnp.bfloat16).reshape(3, HEADS, HEAD_DIM, tok_rows)
-    qkv = swap(qkv, True, 0)
-    query, key, value = qkv[0], qkv[1], qkv[2]
     seg = tail_segments(doc_lengths, long_rows, seq_len - long_rows)[0]
-    probs, tail_probs, attn, inv_total, w_output, w_expand, w_reduce = attn_fwd(
-        query,
-        key,
-        value,
-        seg,
-        long_rows,
-        (weight_output, weight_expand, weight_reduce),
-        5,
-    )
+    probs, tail_probs, attn, inv_total, kept, attn_flat, w_output, w_expand, w_reduce = attn_fwd(
+        qkv, seg, long_rows, wholes, 5
+    )
+    attn_flat = attn_flat.reshape(model_width, tok_rows)
     w_output = w_output.reshape(-1, weight_output.shape[1])
     w_expand = w_expand.reshape(-1, weight_expand.shape[1])
     w_reduce = w_reduce.reshape(-1, weight_reduce.shape[1])
-    attn_flat = swap(attn[None], False, 1).reshape(model_width, tok_rows)
 
     resid_one = flat_rows.astype(jnp.float32) + left_dot(attn_flat, w_output) + b_output
     normed_one, norm_one_pull = jax.vjp(layer_norm, resid_one, gain_one, shift_one)
@@ -1236,33 +1533,23 @@
     grad_w_output = plain_dot(attn_flat, grad_branch)
     grad_b_output = jnp.sum(grad_branch.astype(jnp.float32), axis=0)
     grad_attn = right_dot(w_output, grad_branch).astype(jnp.bfloat16)
-    grad_attn = swap(grad_attn.reshape(1, HEADS, HEAD_DIM, tok_rows), True, 2)[0]
-
-    *grad_qkv, grad_w_output, grad_w_expand, grad_w_reduce = attn_bwd(
+    grad_attn = grad_attn.reshape(HEADS, HEAD_DIM, tok_rows)
+
+    grad_kv, grad_query, grad_w_output, grad_w_expand, grad_w_reduce = attn_bwd(
         probs,
         tail_probs,
-        query,
-        key,
-        value,
+        kept,
         attn,
+        inv_total,
         grad_attn,
-        inv_total,
         long_rows,
         [grad.astype(jnp.bfloat16) for grad in (grad_w_output, grad_w_expand, grad_w_reduce)],
         6,
     )
-    grad_qkv = swap(jnp.stack(grad_qkv), False, 3).reshape(3 * model_width, tok_rows)
-    grad_w_qkv = lax.dot_general(
-        flat_rows, grad_qkv, (((0,), (1,)), ((), ())), preferred_element_type=jnp.float32
-    )
-    grad_input = grad_resid_one + lax.dot_general(
-        grad_qkv, w_qkv, (((0,), (1,)), ((), ())), preferred_element_type=jnp.float32
-    )
-    grad_b_qkv = jnp.sum(grad_qkv.astype(jnp.float32), axis=1)
 
     sums = (
-        grad_b_qkv[:model_width],
-        grad_b_qkv[2 * model_width :],
+        jnp.zeros_like(b_query),
+        jnp.zeros_like(b_value),
         grad_b_output,
         grad_b_reduce,
         grad_gain_one,
@@ -1272,14 +1559,21 @@
         grad_b_expand,
     )
     sums = jnp.concatenate([term.reshape(-1, size) for term, size in zip(sums, sizes)], axis=1)
-    sums = jnp.pad(sums, ((0, 0), (0, 8 * lanes - sums.shape[1]))).reshape(-1, 8, lanes)
-    grad_w_qkv, sums = final_reduce(grad_w_qkv.astype(jnp.bfloat16), sums, 7)
+    sums = jnp.pad(sums, ((0, 0), (0, 8 * lane - sums.shape[1]))).reshape(-1, 8, lane)
+    grad_w_qkv, grad_input, sums = last_reduce(
+        grad_kv, grad_query, flat_rows, w_qkv, grad_resid_one, sums, 7
+    )
+    owner = (lax.axis_index("seq") * blk_count + lax.axis_index("blk")) * head_count
+    owner = owner + lax.axis_index("head")
+    within = lax.rem(owner, lane // sizes[0]) * sizes[0]
+    g_query = lax.dynamic_slice_in_dim(sums[3], within, sizes[0])
+    g_value = lax.dynamic_slice_in_dim(sums[4], within, sizes[1])
     sums = sums.reshape(-1)
     parts, start = [], 0
     for size in sizes:
         parts.append(sums[start : start + size])
         start += size
-    g_query, g_value, g_output, g_reduce, g_gain_one, g_shift_one, g_gain_two, g_shift_two, g_expand = parts
+    g_output, g_reduce, g_gain_one, g_shift_one, g_gain_two, g_shift_two, g_expand = parts[2:]
     return (
         layer_output,
         grad_input.reshape(layer_input.shape),

time: 761 us -> 590 us (0.78)
  Pallas kernels: 630 us -> 479 us
  matrix products: 84.1 us -> 68 us
    pallas_call x5 -> x1, Pallas kernels: 239 us -> 87.5 us  [last_reduce(): pl.pallas_call(functools.partial(last_kernel, blks, devices), out_shape=[...]
    pallas_call x1, Pallas kernels: 200 us -> 164 us  [attn_fwd(): pl.pallas_call(functools.partial(attn_fwd_kernel, blks, rows, cols), grid...]
    pallas_call x1, Pallas kernels: 53.1 us -> 78.9 us  [first_gather(): pl.pallas_call(functools.partial(first_kernel, blks, devices), out_shape=...]
    dot_general x2 -> x0, matrix products: 14.1 us -> none  [the longest x1 8.75 us: shards_heads(): lax.dot_general(grad_qkv, w_qkv, (((0,), (1,)), ((), ())), preferred_elem...]
    pallas_call x1, Pallas kernels: 137 us -> 149 us  [attn_bwd(): pl.pallas_call(functools.partial(attn_bwd_kernel, blks, rows, cols), grid...]
where the time goes in v3:
time: 590 us; the launch traced here: 585 us
  Pallas kernels  479 us (81%)
  matrix products  68 us (12%)
  local copies, waits for them, and re-layouts  24.5 us (4%)
  other arithmetic  11.6 us (2%)
    pallas_call x1, Pallas kernels, attn_fwd(): pl.pallas_call(functools.partial(attn_fwd_kernel, blks, rows, cols), grid...  164 us
    pallas_call x1, Pallas kernels, attn_bwd(): pl.pallas_call(functools.partial(attn_bwd_kernel, blks, rows, cols), grid...  149 us
    pallas_call x1, Pallas kernels, last_reduce(): pl.pallas_call(functools.partial(last_kernel, blks, devices), out_shape=[...  87.5 us
    pallas_call x1, Pallas kernels, first_gather(): pl.pallas_call(functools.partial(first_kernel, blks, devices), out_shape=...  78.9 us
    dot_general x3, matrix products, right_dot(): lax.dot_general(left, right, (((1,), (1,)), ((), ())), preferred_element_...  22.6 us
    dot_general x3, matrix products, plain_dot(): return jnp.dot(left, right, preferred_element_type=jnp.float32)  19.2 us
    dot_general x3, matrix products, left_dot(): lax.dot_general(left, right, (((0,), (0,)), ((), ())), preferred_element_...  17.6 us

profile of v3, /device:TPU:0, one launch (start us, length us, event | category | flops | bytes accessed | tf_op | source)
XLA Modules:
  0.0 584.7 jit_solution(17975185503917173568)
XLA Ops:
  0.7 6.7 %concatenate.12 = bf16[2048]{0:T(1024)(128)(2,1)} concatenate(bf16[32]{0:T(256)(128)(2,1)} %param.25, bf16[32]{0:T(256)(128)(2,1)} %param.26, bf16[32]{0:T(256)(128)(2,1)} %param.27, bf16[32]{0:T(256)(128)(2,1)} %param.29, bf16[32]{0:T(256)(128)(2,1)} %param.30, bf16[32]{0:T(256)(128)(2,1)} %param.31, bf16[32]{0:T(256)(128)(2,1)} %param.32, bf16[32]{0:T(256)(128)(2,1)} %param.33, ...), dimensions={0} | concatenate | bytes 8192 | tf_op jit(solution)/shard_map/concatenate | solution.py:1478
  7.3 78.9 %first_gather.1 = (bf16[2,4,2,2,32,3072]{5,4,3,2,1,0:T(8,128)(2,1)}, bf16[2,4,2,2,32,1024]{5,4,3,2,1,0:T(8,128)(2,1)}, bf16[2,4,2,2,32,4096]{5,4,3,2,1,0:T(8,128...) custom-call(bf16[32,1024]{1,0:T(8,128)(2,1)} %wq.1, bf16[32,1024]{1,0:T(8,128)(2,1)} %wk.1, ...), custom_call_target="tpu_custom_call" | custom-call | tf_op jit(solution)/shard_map/first_gather/pallas_call | solution.py:651
  87.5 8.6 %add_convert_fusion.1 = bf16[3072,512]{1,0:T(8,128)(2,1)} fusion(bf16[1024,3072]{1,0:T(8,128)(2,1)} %bitcast.65, f32[3072]{0:T(1024)S(1)} %pad_maximum_fusion, bf16[1,512,1024]{2,1,0:T(8,128)(2,1)} %param.18), kind=kOutput, calls=%fused_computation.6 | convolution fusion | flops 3224371200 | bytes 10498048 | tf_op jit(solution)/shard_map/dot_general | solution.py:1496
  97.7 1.0 broadcast_in_dim.27.down_ref
  99.3 163.8 %attn_fwd.1 = (bf16[7168,7168]{1,0:T(8,128)(2,1)}, bf16[1024,1024]{1,0:T(8,128)(2,1)}, bf16[64,8192]{1,0:T(8,128)(2,1)}, f32[8,8192]{1,0:T(8,128)}, bf16[3,64,81...) custom-call(bf16[3,16,64,512]{3,2,1,0:T(8,128)(2,1)} %bitcast.92, ...), custom_call_target="tpu_custom_call", output_to_operand_aliasing={{6}: (3, {}), {7}: (4, {}), {8}: (5, {})} | custom-call | flops 13153337344 | bytes 102760448 | tf_op jit(solution)/shard_map/attn_fwd/pallas_call | solution.py:937
  263.2 3.3 fusion.18
  267.0 10.6 %multiply_convert_fusion = (bf16[512,4096]{1,0:T(8,128)(2,1)S(1)}, f32[512,4096]{1,0:T(8,128)}) fusion(f32[4096]{0:T(1024)S(1)} %slice_bitcast_fusion, bf16[1024,4096]{1,0:T(8,128)(2,1)} %bitcast.84, f32[512,1024]{1,0:T(8,128)S(1)} %get-tuple-element.98, f32[1024]{0:T(1024)S(1)} %add.180, f32[1024]{0:T(1024)S(1)} %mul.166, f32[512]{0:T(512)S(1)} %fusion.5, ...), kind=kOutput, calls=%fused_computation.2 | convolution fusion | flops 4310171648 | bytes 23097344 | tf_op jit(solution)/shard_map/dot_general | solution.py:36
  277.7 6.0 %fusion.19 = (f32[512]{0:T(512)S(1)}, f32[512,1024]{1,0:T(8,128)}) fusion(f32[1024]{0:T(1024)S(1)} %add.189, bf16[512,4096]{1,0:T(8,128)(2,1)S(1)} %get-tuple-element.99, bf16[4096,1024]{1,0:T(8,128)(2,1)S(1)} %bitcast.91, f32[1024]{0:T(1024)S(1)} %add.180, f32[1024]{0:T(1024)S(1)} %mul.166, f32[512]{0:T(512)S(1)} %fusion.5, ...), kind=kOutput, calls=%fused_computation.66 | convolution fusion | flops 4298636800 | bytes 16795648 | tf_op jit(solution)/shard_map/dot_general | solution.py:36
  284.5 1.9 multiply_reduce_fusion.3
  286.5 2.4 fusion
  289.0 3.6 fusion.14
  292.8 13.1 %convert_reduce_fusion = (f32[4096]{0:T(1024)S(1)}, bf16[512,4096]{1,0:T(8,128)(2,1)}) fusion(f32[512,4096]{1,0:T(8,128)} %get-tuple-element.100, f32[4096]{0:T(1024)S(1)} %slice_bitcast_fusion, bf16[512,1024]{1,0:T(8,128)(2,1)S(1)} %get-tuple-element.69, bf16[4096,1024]{1,0:T(8,128)(2,1)} %bitcast.88), kind=kOutput, calls=%fused_computation | convolution fusion | flops 4328517632 | bytes 22052864 | tf_op jit(solution)/shard_map/dot_general | solution.py:46
  306.0 7.2 %multiply_reduce_fusion = (f32[1024]{0:T(1024)S(1)}, f32[512]{0:T(512)S(1)}, f32[1024]{0:T(1024)S(1)}, f32[512,1024]{1,0:T(8,128)S(1)}) fusion(f32[512,1024]{1,0:T(8,128)S(1)} %get-tuple-element.98, f32[512]{0:T(512)S(1)} %fusion.5, f32[512]{0:T(512)S(1)} %broadcast_multiply_fusion.1, f32[1024]{0:T(1024)S(1)} %mul.166, ...), kind=kOutput, calls=%fused_computation.12 | convolution fusion | flops 4300207616 | bytes 18894848 | tf_op jit(solution)/shard_map/dot_general | solution.py:46
  314.2 2.1 copy-done.3
  316.2 2.3 convolution_convert_fusion.3
  318.6 2.6 convolution_convert_fusion.2
  321.1 7.3 %convolution_convert_fusion.1 = bf16[1024,4096]{1,0:T(8,128)(2,1)} fusion(bf16[512,4096]{1,0:T(8,128)(2,1)S(1)} %copy-done.11, f32[512,1024]{1,0:T(8,128)S(1)} %get-tuple-element.98, f32[1024]{0:T(1024)S(1)} %add.180, f32[1024]{0:T(1024)S(1)} %mul.166, f32[512]{0:T(512)S(1)} %fusion.5, f32[512]{0:T(512)S(1)} %broadcast_multiply_fusion.1), kind=kOutput, calls=%fused_computation.5 | convolution fusion | flops 4301783040 | bytes 14692352 | tf_op jit(solution)/shard_map/dot_general | solution.py:40
  328.4 7.0 %convolution_convert_fusion = bf16[4096,1024]{1,0:T(8,128)(2,1)} fusion(bf16[512,4096]{1,0:T(8,128)(2,1)S(1)} %copy-done.10, bf16[512,1024]{1,0:T(8,128)(2,1)S(1)} %get-tuple-element.69), kind=kOutput, calls=%fused_computation.4 | convolution fusion | flops 4299161600 | bytes 13631488 | tf_op jit(solution)/shard_map/dot_general | solution.py:40
  335.4 149.1 %attn_bwd.1 = (bf16[2,64,8192]{2,1,0:T(8,128)(2,1)}, bf16[16,64,512]{2,1,0:T(8,128)(2,1)}, f32[32,1024]{1,0:T(8,128)}, f32[32,4096]{1,0:T(8,128)}, f32[128,1024]{1,0:T(8,128)}) custom-call(bf16[7168,7168]{1,0:T(8,128)(2,1)} %get-tuple-element.48.p_ref, bf16[1024,1024]{1,0:T(8,128)(2,1)} %get-tuple-element.49.tail_ref, ...), custom_call_target="tpu_custom_call" | custom-call | flops 26306674688 | bytes 102760448 | tf_op jit(solution)/shard_map/attn_bwd/pallas_call | solution.py:1194
  486.1 87.5 %last_reduce.1 = (f32[32,3072]{1,0:T(8,128)}, f32[512,1024]{1,0:T(8,128)}, f32[8,128]{1,0:T(8,128)}) custom-call(bf16[2,64,8192]{2,1,0:T(8,128)(2,1)} %get-tuple-element.53.dkv_ref, bf16[16,64,512]{2,1,0:T(8,128)(2,1)} %get-tuple-element.54.dq_ref, bf16[512,1024]{1,0:T(8,128)(2,1)} %bitcast.67, bf16[1024,3072]{1,0:T(8,128)(2,1)} %bitcast.66, ...), custom_call_target="tpu_custom_call" | custom-call | tf_op jit(solution)/shard_map/last_reduce/pallas_call | solution.py:1399
  573.6 1.8 fusion.15
  575.3 1.3 slice_bitcast_fusion.1
  577.2 1.5 fusion.17
  578.7 3.3 copy.49
  (83 shorter events, 10.5 us)
Async XLA Ops:
  87.5 8.6 %copy-start.8 = (s32[1,32]{1,0:T(1,128)S(1)}, s32[1,32]{1,0:T(1,128)}, u32[]{:S(2)}) copy-start(s32[1,32]{1,0:T(1,128)} %param.35) | copy-start | bytes 388
  99.3 163.9 %copy-start.2 = (bf16[1,512,1024]{2,1,0:T(8,128)(2,1)S(1)}, bf16[1,512,1024]{2,1,0:T(8,128)(2,1)}, u32[]{:S(2)}) copy-start(bf16[1,512,1024]{2,1,0:T(8,128)(2,1)} %param.18) | copy-start | bytes 3145732
  266.6 11.0 %slice-start.2 = ((s8[8388608]{0:T(1024)(128)(4,1)}), s8[4194304]{0:T(1024)(128)(4,1)S(1)}, s32[]{:S(2)}) async-start(s8[8388608]{0:T(1024)(128)(4,1)} %bitcast.89), calls=%async_computation.2 | async-start | bytes 8388608
  267.0 10.6 %slice-start.3 = ((s8[8388608]{0:T(1024)(128)(4,1)}), s8[4194304]{0:T(1024)(128)(4,1)S(1)}, s32[]{:S(2)}) async-start(s8[8388608]{0:T(1024)(128)(4,1)} %bitcast.89), calls=%async_computation.3 | async-start | bytes 8388608
  277.6 6.0 %copy-start.9 = (bf16[512,4096]{1,0:T(8,128)(2,1)}, bf16[512,4096]{1,0:T(8,128)(2,1)S(1)}, u32[]{:S(2)}) copy-start(bf16[512,4096]{1,0:T(8,128)(2,1)S(1)} %get-tuple-element.99) | copy-start | bytes 12582916
  283.7 2.9 copy-start
  292.6 13.4 %slice-start = ((s8[8388608]{0:T(1024)(128)(4,1)}), s8[4194304]{0:T(1024)(128)(4,1)S(1)}, s32[]{:S(2)}) async-start(s8[8388608]{0:T(1024)(128)(4,1)} %bitcast.85), calls=%async_computation | async-start | bytes 8388608
  292.8 13.2 %slice-start.1 = ((s8[8388608]{0:T(1024)(128)(4,1)}), s8[4194304]{0:T(1024)(128)(4,1)S(1)}, s32[]{:S(2)}) async-start(s8[8388608]{0:T(1024)(128)(4,1)} %bitcast.85), calls=%async_computation.1 | async-start | bytes 8388608
  313.9 2.4 copy-start.3
  314.2 4.4 copy-start.1
  316.2 2.3 copy-start.4
  318.6 2.6 copy-start.11
  321.1 7.3 %copy-start.10 = (bf16[512,4096]{1,0:T(8,128)(2,1)S(1)}, bf16[512,4096]{1,0:T(8,128)(2,1)}, u32[]{:S(2)}) copy-start(bf16[512,4096]{1,0:T(8,128)(2,1)} %copy-done.9) | copy-start | bytes 12582916
  578.7 3.3 copy-start.7
  578.7 3.9 copy-start.6
  578.7 4.7 copy-start.5

commit v4 on v3

--- a/solution.py
+++ b/solution.py
@@ -428,17 +428,18 @@
 ALL = slice(None)
 
 
-def share_line(me, wires, ref, piece):
+def share_line(me, wires, ref, piece, source=None):
     own = view(ref, (me.x, me.z, me.y, me.c), piece)
-    return [wires.copy(own, own, me.at(z=peer)) for peer in me.column()]
+    source = own if source is None else source
+    return [wires.copy(source, own, me.at(z=peer)) for peer in me.column()]
 
 
 class Gather:
     WIRES = 7
 
-    def __init__(self, me, wires, ref, piece, turned, ready=False):
+    def __init__(self, me, wires, ref, piece, turned, ready=False, source=None):
         x, z, y, c = me.x, me.z, me.y, me.c
-        self.first = [] if ready else share_line(me, wires, ref, piece)
+        self.first = [] if ready else share_line(me, wires, ref, piece, source)
         line = view(ref, (x, ALL, y, c), piece)
         if turned:
             half, rest = view(ref, (ALL, ALL, y, c), piece), view(ref, (ALL, ALL, 1 - y, c), piece)
@@ -471,6 +472,58 @@
             self.far.wait_recv()
             for copy in (*self.first, self.second, self.third, self.near, self.far):
                 copy.wait_send()
+
+
+class Relay(Gather):
+    WIRES = 7
+
+    def __init__(self, me, wires, ref, piece, turned, source):
+        super().__init__(me, wires, ref, piece, turned, ready=True)
+        x, z, y, c = me.x, me.z, me.y, me.c
+        own = view(ref, (x, z, y, c), piece)
+        beside = me.at(z=z + 1 - 2 * lax.rem(z, 2))
+        pair = view(ref, (x, pl.ds(z // 2 * 2, 2), y, c), piece)
+        other = view(ref, (x, pl.ds(2 - z // 2 * 2, 2), y, c), piece)
+        self.inner = (z == 1) | (z == 2)
+        self.own = wires.copy(source, own, beside)
+        self.cross = wires.copy(pair, pair, me.at(z=lax.rem(3 - z, 4)))
+        self.outward = wires.copy(other, other, beside)
+
+    def stage(self, index):
+        if index == 0:
+            self.own.start()
+        elif index == 1:
+            self.own.wait_recv()
+
+            @pl.when(self.inner)
+            def _():
+                self.cross.start()
+
+        elif index == 2:
+
+            @pl.when(self.inner)
+            def _():
+                self.cross.wait_recv()
+                self.outward.start()
+
+        elif index == 3:
+
+            @pl.when(jnp.logical_not(self.inner))
+            def _():
+                self.outward.wait_recv()
+
+            super().stage(1)
+        elif index < 6:
+            super().stage(index - 2)
+        else:
+
+            @pl.when(self.inner)
+            def _():
+                self.cross.wait_send()
+                self.outward.wait_send()
+
+            self.own.wait_send()
+            super().stage(4)
 
 
 class Reduce:
@@ -570,101 +623,17 @@
 
 
 def weight_units(edges):
-    out_rows, expand_cols, reduce_rows = edges
-    units = [(0, ((0, out_rows), (0, UNIT)))]
-    expand = [(1, ((0, EDGE), (first, UNIT))) for first in range(0, expand_cols, UNIT)]
-    reduce = [(2, ((first, EDGE), (0, UNIT))) for first in range(0, reduce_rows, EDGE)]
-    for pair in zip(expand, reduce):
-        units.extend(pair)
-    return units
-
-
-EARLY = 5
-
-
-def first_kernel(
-    blks, devices, wq, wk, wv, wo, we, wr, vec, out, go, ge, gr, vec_out,
-    own_sem, send, recv, vec_send, vec_recv,
-):
-    me = Place(blks)
-    index, others = me.others(devices)
-    here = (me.x, me.z, me.y, me.c)
-    pairs = [
-        (ref, out.at[here + (ALL, pl.ds(unit * UNIT, UNIT))])
-        for unit, ref in enumerate((wq, wk, wv))
-    ]
-    pairs += [(ref, whole.at[here]) for ref, whole in zip((wo, we, wr), (go, ge, gr))]
-    pairs.append((vec, vec_out.at[index]))
-    local = [
-        pltpu.make_async_copy(source, target, own_sem.at[number])
-        for number, (source, target) in enumerate(pairs)
-    ]
-    for copy in local:
-        copy.start()
-    greet(others)
-    for copy in local:
-        copy.wait()
-    wires = Wires(send, recv)
-    plan = [
-        Gather(me, wires, out, ((0, EDGE), (half * UNIT // 2, UNIT // 2)), half % 2 == 1)
-        for half in range(6)
-    ]
-    wholes = (go, ge, gr)
-    units = weight_units((wo.shape[0], we.shape[1], wr.shape[0]))
-    lines = []
-    for which, piece in units[:EARLY]:
-        lines += share_line(me, wires, wholes[which], piece)
-    small = []
-    for slot, device in enumerate(others):
-        small.append(
-            pltpu.make_async_remote_copy(
-                src_ref=vec,
-                dst_ref=vec_out.at[index],
-                send_sem=vec_send.at[slot],
-                recv_sem=vec_recv.at[slot],
-                device_id=device,
-                device_id_type=MESH,
-            )
-        )
-    for unit in plan:
-        unit.stage(0)
-    for copy in small:
-        copy.start()
-    for wave in range(3 + 4):
-        for pair in range(3):
-            index = wave - pair + 1
-            if 1 <= index <= 4:
-                for unit in plan[2 * pair : 2 * pair + 2]:
-                    unit.stage(index)
-        if wave == 0:
-            for copy in lines:
-                copy.start()
-    for copy in lines + small:
-        copy.wait()
-
-
-def first_gather(wq, wk, wv, shares, vec, collective_id):
-    seqs, blks, heads = (lax.axis_size(name) for name in EVERY)
-    devices = seqs * blks * heads
-    lead = (seqs, blks, heads // 2, 2)
-    wires = 6 * Gather.WIRES + EARLY * (blks - 1)
-    return pl.pallas_call(
-        functools.partial(first_kernel, blks, devices),
-        out_shape=[jax.ShapeDtypeStruct(lead + (EDGE, 3 * UNIT), wq.dtype)]
-        + [jax.ShapeDtypeStruct(lead + share.shape, share.dtype) for share in shares]
-        + [jax.ShapeDtypeStruct((devices,) + vec.shape, vec.dtype)],
-        in_specs=[pl.BlockSpec(memory_space=pl.ANY)] * 7,
-        out_specs=[pl.BlockSpec(memory_space=pl.ANY)] * 5,
-        scratch_shapes=[
-            pltpu.SemaphoreType.DMA((7,)),
-            pltpu.SemaphoreType.DMA((wires,)),
-            pltpu.SemaphoreType.DMA((wires,)),
-            pltpu.SemaphoreType.DMA((devices,)),
-            pltpu.SemaphoreType.DMA((devices,)),
-        ],
-        compiler_params=pltpu.CompilerParams(collective_id=collective_id, has_side_effects=True),
-        name="first_gather",
-    )(wq, wk, wv, *shares, vec)
+    columns = []
+    for which, (rows, cols) in enumerate(edges):
+        columns.append(
+            [
+                (which, ((row, EDGE), (col, UNIT)))
+                for row in range(0, rows, EDGE)
+                for col in range(0, cols, UNIT)
+            ]
+        )
+    most = max(len(column) for column in columns)
+    return [column[place] for place in range(most) for column in columns if place < len(column)]
 
 
 LOG2E = 1.4426950408889634
@@ -686,12 +655,28 @@
     )
 
 
+def TURNED(number):
+    return number % 2 == 1
+
+
+def SCHEDULE(number):
+    if number < 2:
+        return (-2, -1, -0.9, -0.8, 1)
+    begin = (number - 2) // 2
+    return (begin, begin + 1, begin + 2, begin + 4, begin + 7)
+
+
 def attn_fwd_kernel(
-    blks, rows, cols, qkv_ref, down_ref, across_ref, go_in, ge_in, gr_in,
-    p_ref, tail_ref, o_ref, inv_ref, kept_ref, tokens_ref, go, ge, gr,
-    land, keys, values, s0, s1, m0, m1,
+    blks, rows, cols, count, *refs
+):
+    x_ref, vec_ref, down_ref, across_ref, wq, wk, wv = refs[:7]
+    shares, refs = refs[7 : 7 + count], refs[7 + count :]
+    p_ref, tail_ref, o_ref, inv_ref, kept_ref, tokens_ref, qkv_out, vec_out = refs[:8]
+    wholes, refs = refs[8 : 8 + count], refs[8 + count :]
+    (
+    weights, vecs, qkv_ref, land, keys, values, s0, s1, m0, m1,
     own_sem, kv_send, kv_recv, q_send, q_recv, o_send, o_recv, send, recv,
-):
+    ) = refs
     step, steps = pl.program_id(0), pl.num_programs(0)
     length, long = land.shape[2], p_ref.shape[1]
     width = 2 * rows
@@ -708,32 +693,20 @@
     def ahead(block):
         return lax.rem(block + group - me.index, group)
 
-    kv_copies, q_copies = [], []
-    for ahead_by in range(1, group):
-        peer, device = me.peer(group - ahead_by)
-        kv_copies.append(
-            wire(
-                qkv_ref.at[1:3, peer],
-                lanes(land, (pl.ds(1, 2), ALL), me.index * width, width),
-                kv_send.at[ahead_by],
-                kv_recv.at[ahead_by],
-                device,
+    swaps = [[], [], []]
+    for tensor, send_sem, recv_sem in ((0, q_send, q_recv), (1, kv_send, kv_recv), (2, kv_send, kv_recv)):
+        for ahead_by in range(1, group):
+            peer, device = me.peer(group - ahead_by)
+            slot = ahead_by + (group if tensor == 2 else 0)
+            swaps[tensor].append(
+                wire(
+                    qkv_ref.at[tensor, peer],
+                    lanes(land, (tensor, ALL), me.index * width, width),
+                    send_sem.at[slot],
+                    recv_sem.at[slot],
+                    device,
+                )
             )
-        )
-        q_copies.append(
-            wire(
-                qkv_ref.at[0, peer],
-                lanes(land, (0, ALL), me.index * width, width),
-                q_send.at[ahead_by],
-                q_recv.at[ahead_by],
-                device,
-            )
-        )
-    own_in = pltpu.make_async_copy(
-        qkv_ref.at[:, me.index],
-        lanes(land, (ALL, ALL), me.index * width, width),
-        own_sem.at[0],
-    )
     keep = pltpu.make_async_copy(land, kept_ref, own_sem.at[1])
 
     def await_queries(block):
@@ -773,20 +746,60 @@
                 local.wait()
 
     wires = Wires(send, recv)
-    wholes = (go, ge, gr)
-    units = weight_units((go.shape[4], ge.shape[5], gr.shape[4]))
+    here = (me.x, me.z, me.y, me.c)
+    half = UNIT // 2
+    fronts = []
+    for unit, ref in enumerate((wq, wk, wv)):
+        for side in range(2):
+            piece = ((0, EDGE), (unit * UNIT + side * half, half))
+            source = ref.at[:, pl.ds(side * half, half)]
+            fronts.append(Gather(me, wires, weights, piece, side == 1, source=source))
+    vectors = Gather(me, wires, vecs, ((0, EDGE), (0, vecs.shape[5])), False)
+    units = weight_units([share.shape for share in shares])
     plan = [
-        Gather(me, wires, wholes[which], piece, number % 2 == 1, number < EARLY)
+        Relay(
+            me,
+            wires,
+            wholes[which],
+            piece,
+            TURNED(number),
+            source=shares[which].at[pl.ds(*piece[0]), pl.ds(*piece[1])],
+        )
         for number, (which, piece) in enumerate(units)
     ]
-    late = len(units) - EARLY
+    targets = [weights.at[here + (ALL, pl.ds(unit * UNIT, UNIT))] for unit in range(3)]
+    targets += [whole.at[here] for whole in wholes]
+    local = [
+        pltpu.make_async_copy(source, target, own_sem.at[3 + number])
+        for number, (source, target) in enumerate(zip((wq, wk, wv) + tuple(shares), targets))
+    ]
+    keep_weights = pltpu.make_async_copy(weights, qkv_out, own_sem.at[9])
+    keep_vectors = pltpu.make_async_copy(vecs, vec_out, own_sem.at[10])
     moves = {}
-    for number in range(late):
-        for stage, at in enumerate((2, 6 + number // 2, 8 + number // 2)):
-            moves.setdefault(at, []).append((plan[EARLY + number], stage))
-        moves.setdefault(12, []).append((plan[EARLY + number], 3))
-    for number in range(EARLY):
-        moves.setdefault(1 + number // 2, []).append((plan[number], 3))
+    for number in range(len(units)):
+        for stage, at in enumerate(SCHEDULE(number), 1):
+            moves.setdefault(at, []).append((plan[number], stage))
+
+    def front(tensor, *stages):
+        for stage in stages:
+            for unit in fronts[2 * tensor : 2 * tensor + 2]:
+                unit.stage(stage)
+
+    def project(tensor, column):
+        for first in range(0, UNIT, 256):
+            taken = weights[:, :, :, :, :, tensor * UNIT + first : tensor * UNIT + first + 256]
+            found = jnp.dot(
+                x_ref[...], taken.reshape(UNIT, 256), preferred_element_type=jnp.float32
+            ).T
+            if column is not None:
+                bias = vecs[...].reshape(UNIT, vecs.shape[5])[first : first + 256]
+                found = found + bias[:, column : column + 1].astype(jnp.float32)
+            heads = first // HEAD_DIM, (first + 256) // HEAD_DIM
+            qkv_ref[tensor, heads[0] : heads[1]] = found.astype(jnp.bfloat16).reshape(
+                heads[1] - heads[0], HEAD_DIM, width
+            )
+        own = pl.ds(pl.multiple_of(me.index * width, width), width)
+        land[tensor, :, own] = qkv_ref[tensor, me.index]
 
     def take_queries(start):
         part = land[0, :, pl.ds(pl.multiple_of(start, rows), rows)].astype(jnp.float32) * scale
@@ -825,18 +838,53 @@
 
     @pl.when(step == 0)
     def _():
-        own_in.start()
+        for copy in local:
+            copy.start()
+        turned = jnp.concatenate(
+            [vec_ref[...].astype(jnp.float32), jnp.zeros((112, 128), jnp.float32)], 0
+        ).T
+        vecs[here] = turned[:EDGE].astype(jnp.bfloat16)
         greet([me.peer(by)[1] for by in range(1, group)] + [me.at(x=1 - me.x)])
-        for copy in kv_copies:
+        vectors.stage(0)
+        for tensor in (1, 2, 0):
+            front(tensor, 0)
+        for unit in plan:
+            unit.stage(0)
+        for copy in local:
+            copy.wait()
+        vectors.stage(1)
+        front(1, 1)
+        front(1, 2)
+        vectors.stage(2)
+        front(2, 1)
+        front(1, 3)
+        front(2, 2)
+        vectors.stage(3)
+        front(0, 1)
+        front(1, 4)
+        project(1, None)
+        for copy in swaps[1]:
             copy.start()
-        for unit in plan[:EARLY]:
-            unit.stage(1)
-        for copy in q_copies:
+        front(2, 3)
+        front(0, 2)
+        vectors.stage(4)
+        front(2, 4)
+        project(2, 1)
+        for copy in swaps[2]:
             copy.start()
-        for unit in plan[:EARLY]:
-            unit.stage(2)
-        own_in.wait()
-        for copy in kv_copies:
+        front(0, 3)
+        for unit, stage in moves.get(-2, []):
+            unit.stage(stage)
+        front(0, 4)
+        keep_weights.start()
+        keep_vectors.start()
+        project(0, 0)
+        for copy in swaps[0]:
+            copy.start()
+        for at in (-1, -0.9, -0.8, -0.7, -0.6):
+            for unit, stage in moves.get(at, []):
+                unit.stage(stage)
+        for copy in swaps[1] + swaps[2]:
             copy.wait_recv()
         keys[0:HEAD_DIM, :] = land[1]
         keys[HEAD_DIM:, :] = land[1]
@@ -852,7 +900,7 @@
             peak = score(queries, s0, j, peak)
         keep_peak(m0, peak)
 
-    for at, todo in sorted(moves.items()):
+    for at, todo in sorted((entry for entry in moves.items() if entry[0] >= 0), key=lambda entry: entry[0]):
 
         @pl.when(step == at)
         def _():
@@ -897,9 +945,11 @@
                 number = main + first // width
                 send_block(number, number, True)
         for unit in plan:
-            unit.stage(4)
-        for copy in kv_copies + q_copies:
+            unit.stage(6)
+        for copy in swaps[0] + swaps[1] + swaps[2]:
             copy.wait_send()
+        keep_weights.wait()
+        keep_vectors.wait()
         for turn in range(main):
             send_block(block_at(turn), turn, False)
         for number in range(main, group):
@@ -920,31 +970,35 @@
     return pl.BlockSpec(shape, lambda step: (0,) * len(shape), pipeline_mode=pl.Buffered(1))
 
 
-def attn_fwd(qkv, seg, long, wholes, collective_id, cols=1024):
-    blks = lax.axis_size("blk")
-    group, width = qkv.shape[1], qkv.shape[3]
+def attn_fwd(x, vec, seg, fronts, shares, collective_id, cols=1024):
+    seqs, blks, heads = (lax.axis_size(name) for name in EVERY)
+    lead = (seqs, blks, heads // 2, 2)
+    group, width = blks * heads, x.shape[0]
     rows = width // 2
     length = group * width
-    tail = length - long
+    tail = seg.shape[0]
+    long = length - tail
     down = jnp.broadcast_to(seg[:, None], (tail, 128))
     across = jnp.broadcast_to(seg[None, :], (8, tail))
     anywhere = pl.BlockSpec(memory_space=pl.ANY)
-    wires = Gather.WIRES * len(
-        weight_units((wholes[0].shape[4], wholes[1].shape[5], wholes[2].shape[4]))
-    )
+    count = len(weight_units([share.shape for share in shares])) if shares else 0
+    wires = Gather.WIRES * (count + 7)
     kept = jax.ShapeDtypeStruct((3, HEAD_DIM, length), jnp.bfloat16)
+    gathered = jax.ShapeDtypeStruct(lead + (EDGE, 3 * UNIT), jnp.bfloat16)
+    vectors = jax.ShapeDtypeStruct(lead + (EDGE, 128), jnp.bfloat16)
     pair = [pltpu.SemaphoreType.DMA((group,))] * 2
     return pl.pallas_call(
-        functools.partial(attn_fwd_kernel, blks, rows, cols),
+        functools.partial(attn_fwd_kernel, blks, rows, cols, len(shares)),
         grid=(long // width,),
-        in_specs=[anywhere, once((tail, 128)), once((8, tail))] + [anywhere] * 3,
+        in_specs=[once(x.shape), once(vec.shape), once((tail, 128)), once((8, tail))]
+        + [once(share.shape) for share in fronts + shares],
         out_specs=[
             pl.BlockSpec((width, long), lambda step: (step, 0)),
             once((tail, tail)),
             once((HEAD_DIM, length)),
             once((8, length)),
         ]
-        + [anywhere] * 5,
+        + [anywhere] * (4 + len(shares)),
         out_shape=[
             jax.ShapeDtypeStruct((long, long), jnp.bfloat16),
             jax.ShapeDtypeStruct((tail, tail), jnp.bfloat16),
@@ -952,10 +1006,14 @@
             jax.ShapeDtypeStruct((8, length), jnp.float32),
             kept,
             jax.ShapeDtypeStruct((group, HEAD_DIM, width), jnp.bfloat16),
+            gathered,
+            vectors,
         ]
-        + [jax.ShapeDtypeStruct(whole.shape, whole.dtype) for whole in wholes],
-        input_output_aliases={3: 6, 4: 7, 5: 8},
+        + [jax.ShapeDtypeStruct(lead + share.shape, share.dtype) for share in shares],
         scratch_shapes=[
+            pltpu.VMEM(gathered.shape, gathered.dtype),
+            pltpu.VMEM(vectors.shape, vectors.dtype),
+            pltpu.VMEM((3, group, HEAD_DIM, width), jnp.bfloat16),
             pltpu.VMEM(kept.shape, kept.dtype),
             pltpu.VMEM((2 * HEAD_DIM, length), jnp.bfloat16),
             pltpu.VMEM((HEAD_DIM + 16, length), jnp.bfloat16),
@@ -963,15 +1021,16 @@
             pltpu.VMEM((rows, long), jnp.float32),
             pltpu.VMEM((rows, 128), jnp.float32),
             pltpu.VMEM((rows, 128), jnp.float32),
-            pltpu.SemaphoreType.DMA((3,)),
-            *pair,
+            pltpu.SemaphoreType.DMA((11,)),
+            pltpu.SemaphoreType.DMA((2 * group,)),
+            pltpu.SemaphoreType.DMA((2 * group,)),
             *pair,
             *pair,
             pltpu.SemaphoreType.DMA((wires,)),
             pltpu.SemaphoreType.DMA((wires,)),
         ],
         compiler_params=pltpu.CompilerParams(
-            collective_id=collective_id, has_side_effects=True, vmem_limit_bytes=56 * 2**20
+            collective_id=collective_id, has_side_effects=True, vmem_limit_bytes=62 * 2**20
         ),
         cost_estimate=pl.CostEstimate(
             flops=4 * long * long * HEAD_DIM,
@@ -979,7 +1038,7 @@
             transcendentals=long * long,
         ),
         name="attn_fwd",
-    )(qkv, down, across, *wholes)
+    )(x, vec, down, across, *fronts, *shares)
 
 
 def attn_bwd_kernel(
@@ -1054,7 +1113,7 @@
 
     wires = Wires(send, recv)
     partials, totals = (wo, we, wr), (go, ge, gr)
-    units = weight_units((wo.shape[4], we.shape[5], wr.shape[4]))
+    units = weight_units([partial.shape[4:] for partial in partials])
     plan, moves = [], {}
     for number, (which, piece) in enumerate(units):
         turned = number % 2 == 1
@@ -1075,7 +1134,7 @@
         )
         plan.append(unit)
         pair = number // 2
-        for stage, at in enumerate((0, pair, pair + 1, 2 * pair + 3, 2 * pair + 5)):
+        for stage, at in enumerate((0, pair, pair + 1, 2 * pair + 4, 2 * pair + 6)):
             moves.setdefault(min(at, main - 1), []).append((stage, number, unit))
 
     def prepare(start, width):
@@ -1189,7 +1248,7 @@
     group, _, rows = grad_attn.shape
     anywhere = pl.BlockSpec(memory_space=pl.ANY)
     edges = [(partial.shape[0] // devices, partial.shape[1]) for partial in partials]
-    units = len(weight_units((edges[0][0], edges[1][1], edges[2][0])))
+    units = len(weight_units(edges))
     pair = [pltpu.SemaphoreType.DMA((group,))] * 2
     return pl.pallas_call(
         functools.partial(attn_bwd_kernel, blks, rows, cols),
@@ -1433,6 +1492,9 @@
     return segment_ids(doc_lengths, first + lax.iota(jnp.int32, rows))
 
 
+BESIDE = ()
+
+
 def shards_heads(
     layer_input,
     weight_query,
@@ -1474,37 +1536,36 @@
     )
     sizes = [vector.shape[0] for vector in vectors]
     lane = 128
-    spare = 16 * lane - sum(sizes)
-    packed = jnp.concatenate(vectors + (jnp.zeros((spare,), layer_input.dtype),))
-    w_qkv, *wholes, packed = first_gather(
-        weight_query,
-        weight_key,
-        weight_value,
-        (weight_output, weight_expand, weight_reduce),
-        packed.reshape(16, lane),
-        4,
-    )
+    rows = [vector.reshape(1, -1) for vector in vectors[:-1]] + [bias_expand.reshape(-1, sizes[0])]
+    vec, at = jnp.zeros((16, lane), layer_input.dtype), 0
+    for row in rows:
+        count_here = row.shape[0]
+        vec = vec + jnp.pad(row, ((at, 16 - at - count_here), (0, lane - sizes[0])))
+        at = at + count_here
+    seg = tail_segments(doc_lengths, long_rows, seq_len - long_rows)[0]
+    rest = (weight_output, weight_expand, weight_reduce)
+    beside = {which: lax.all_gather(rest[which], EVERY, axis=0, tiled=True) for which in BESIDE}
+    (
+        probs, tail_probs, attn, inv_total, kept, attn_flat, w_qkv, vec, *wholes,
+    ) = attn_fwd(
+        flat_rows,
+        vec,
+        seg,
+        (weight_query, weight_key, weight_value),
+        tuple(share for which, share in enumerate(rest) if which not in BESIDE),
+        5,
+    )
+    attn_flat = attn_flat.reshape(model_width, tok_rows)
     w_qkv = w_qkv.reshape(model_width, 3 * model_width)
-    packed = packed.reshape(-1, 16 * lane).astype(jnp.float32)
-    whole, start = [], 0
-    for size in sizes:
-        whole.append(packed[:, start : start + size].reshape(-1))
-        start += size
-    b_query, b_value, b_output, b_reduce, gain_one, shift_one, gain_two, shift_two, b_expand = whole
-
-    b_qkv = jnp.concatenate((b_query, jnp.zeros_like(b_query), b_value))
-    qkv = lax.dot_general(
-        w_qkv, flat_rows, (((0,), (1,)), ((), ())), preferred_element_type=jnp.float32
-    )
-    qkv = (qkv + b_qkv[:, None]).astype(jnp.bfloat16).reshape(3, HEADS, HEAD_DIM, tok_rows)
-    seg = tail_segments(doc_lengths, long_rows, seq_len - long_rows)[0]
-    probs, tail_probs, attn, inv_total, kept, attn_flat, w_output, w_expand, w_reduce = attn_fwd(
-        qkv, seg, long_rows, wholes, 5
-    )
-    attn_flat = attn_flat.reshape(model_width, tok_rows)
-    w_output = w_output.reshape(-1, weight_output.shape[1])
-    w_expand = w_expand.reshape(-1, weight_expand.shape[1])
-    w_reduce = w_reduce.reshape(-1, weight_reduce.shape[1])
+    vec = vec.reshape(-1, sizes[0], lane)[:, :, :16].transpose(2, 0, 1).astype(jnp.float32)
+    _, _, b_output, b_reduce, gain_one, shift_one, gain_two, shift_two = [
+        vec[number].reshape(-1) for number in range(8)
+    ]
+    b_expand = vec[8:at].transpose(1, 0, 2).reshape(-1)
+    w_output, w_expand, w_reduce = [
+        beside[which] if which in BESIDE else wholes.pop(0).reshape(-1, share.shape[1])
+        for which, share in enumerate(rest)
+    ]
 
     resid_one = flat_rows.astype(jnp.float32) + left_dot(attn_flat, w_output) + b_output
     normed_one, norm_one_pull = jax.vjp(layer_norm, resid_one, gain_one, shift_one)
@@ -1548,8 +1609,8 @@
     )
 
     sums = (
-        jnp.zeros_like(b_query),
-        jnp.zeros_like(b_value),
+        jnp.zeros_like(b_output),
+        jnp.zeros_like(b_output),
         grad_b_output,
         grad_b_reduce,
         grad_gain_one,

time: 590 us -> 563 us (0.954); the launches traced: 585 us -> 552 us
  Pallas kernels: 479 us -> 459 us
  matrix products: 68 us -> 58.8 us
    pallas_call x2 -> x1, Pallas kernels: 243 us -> 227 us  [attn_fwd(): pl.pallas_call(functools.partial(attn_fwd_kernel, blks, rows, cols, len(s...]
    dot_general x1 -> x0, matrix products: 8.61 us -> none  [shards_heads(): lax.dot_general(w_qkv, flat_rows, (((0,), (1,)), ((), ())), preferred_ele...]
    concatenate x1 -> x0, local copies, waits for them, and re-layouts: 6.68 us -> none  [shards_heads(): jnp.concatenate(vectors + (jnp.zeros((spare,), layer_input.dtype),))]
where the time goes in v4:
time: 563 us; the launch traced here: 552 us
  Pallas kernels  459 us (82%)
  matrix products  58.8 us (10%)
  local copies, waits for them, and re-layouts  18.8 us (3%)
  other arithmetic  13.6 us (2%)
    pallas_call x1, Pallas kernels, attn_fwd(): pl.pallas_call(functools.partial(attn_fwd_kernel, blks, rows, cols, len(s...  227 us
    pallas_call x1, Pallas kernels, attn_bwd(): pl.pallas_call(functools.partial(attn_bwd_kernel, blks, rows, cols), grid...  146 us
    pallas_call x1, Pallas kernels, last_reduce(): pl.pallas_call(functools.partial(last_kernel, blks, devices), out_shape=[...  86.5 us
    dot_general x3, matrix products, right_dot(): lax.dot_general(left, right, (((1,), (1,)), ((), ())), preferred_element_...  22.6 us
    dot_general x3, matrix products, plain_dot(): return jnp.dot(left, right, preferred_element_type=jnp.float32)  18.6 us
    dot_general x3, matrix products, left_dot(): lax.dot_general(left, right, (((0,), (0,)), ((), ())), preferred_element_...  17.6 us

profile of v4, /device:TPU:0, one launch (start us, length us, event | category | flops | bytes accessed | tf_op | source)
XLA Modules:
  0.0 551.8 jit_solution(7027773094171790585)
XLA Ops:
  1.4 1.4 pad_add_fusion.refs_1_
  2.8 0.9 reduce_window_sum.12
  5.0 1.0 broadcast_in_dim.21.refs_2_
  6.6 226.6 %attn_fwd.1 = (bf16[7168,7168]{1,0:T(8,128)(2,1)}, bf16[1024,1024]{1,0:T(8,128)(2,1)}, bf16[64,8192]{1,0:T(8,128)(2,1)}, f32[8,8192]{1,0:T(8,128)}, bf16[3,64,81...) custom-call(bf16[512,1024]{1,0:T(8,128)(2,1)} %bitcast.68, ...), custom_call_target="tpu_custom_call" | custom-call | flops 13153337344 | bytes 102760448 | tf_op jit(solution)/shard_map/attn_fwd/pallas_call | solution.py:990
  233.2 1.3 copy.39
  234.8 3.3 fusion.17
  238.6 10.0 %multiply_convert_fusion = (bf16[512,4096]{1,0:T(8,128)(2,1)S(1)}, f32[512,4096]{1,0:T(8,128)}) fusion(f32[4096]{0:T(1024)S(1)} %add.223, bf16[1024,4096]{1,0:T(8,128)(2,1)} %bitcast.91, f32[512,1024]{1,0:T(8,128)S(1)} %get-tuple-element.90, f32[1024]{0:T(1024)S(1)} %add.220, f32[1024]{0:T(1024)S(1)} %mul.166, f32[512]{0:T(512)S(1)} %fusion.5, ...), kind=kOutput, calls=%fused_computation.2 | convolution fusion | flops 4310171648 | bytes 23097344 | tf_op jit(solution)/shard_map/dot_general | solution.py:36
  248.7 6.0 %fusion.18 = (f32[512]{0:T(512)S(1)}, f32[512,1024]{1,0:T(8,128)}) fusion(f32[1024]{0:T(1024)S(1)} %add.229, bf16[512,4096]{1,0:T(8,128)(2,1)S(1)} %get-tuple-element.91, bf16[4096,1024]{1,0:T(8,128)(2,1)S(1)} %bitcast.98, f32[1024]{0:T(1024)S(1)} %add.220, f32[1024]{0:T(1024)S(1)} %mul.166, f32[512]{0:T(512)S(1)} %fusion.5, ...), kind=kOutput, calls=%fused_computation.64 | convolution fusion | flops 4298636800 | bytes 16795648 | tf_op jit(solution)/shard_map/dot_general | solution.py:36
  255.5 1.9 multiply_reduce_fusion.3
  257.6 2.4 fusion
  260.1 3.6 fusion.13
  263.9 13.1 %convert_reduce_fusion = (f32[4096]{0:T(1024)S(1)}, bf16[512,4096]{1,0:T(8,128)(2,1)}) fusion(f32[512,4096]{1,0:T(8,128)} %get-tuple-element.92, f32[4096]{0:T(1024)S(1)} %add.223, bf16[512,1024]{1,0:T(8,128)(2,1)S(1)} %get-tuple-element.63, bf16[4096,1024]{1,0:T(8,128)(2,1)} %bitcast.95), kind=kOutput, calls=%fused_computation | convolution fusion | flops 4328517632 | bytes 22052864 | tf_op jit(solution)/shard_map/dot_general | solution.py:46
  277.0 7.2 %multiply_reduce_fusion = (f32[1024]{0:T(1024)S(1)}, f32[512]{0:T(512)S(1)}, f32[1024]{0:T(1024)S(1)}, f32[512,1024]{1,0:T(8,128)S(1)}) fusion(f32[512,1024]{1,0:T(8,128)S(1)} %get-tuple-element.90, f32[512]{0:T(512)S(1)} %fusion.5, f32[512]{0:T(512)S(1)} %broadcast_multiply_fusion.1, f32[1024]{0:T(1024)S(1)} %mul.166, ...), kind=kOutput, calls=%fused_computation.11 | convolution fusion | flops 4300207616 | bytes 18894848 | tf_op jit(solution)/shard_map/dot_general | solution.py:46
  285.2 2.1 copy-done.3
  287.3 2.3 convolution_convert_fusion.3
  289.6 2.6 convolution_convert_fusion.2
  292.2 7.3 %convolution_convert_fusion.1 = bf16[1024,4096]{1,0:T(8,128)(2,1)} fusion(bf16[512,4096]{1,0:T(8,128)(2,1)S(1)} %copy-done.10, f32[512,1024]{1,0:T(8,128)S(1)} %get-tuple-element.90, f32[1024]{0:T(1024)S(1)} %add.220, f32[1024]{0:T(1024)S(1)} %mul.166, f32[512]{0:T(512)S(1)} %fusion.5, f32[512]{0:T(512)S(1)} %broadcast_multiply_fusion.1), kind=kOutput, calls=%fused_computation.5 | convolution fusion | flops 4301783040 | bytes 14692352 | tf_op jit(solution)/shard_map/dot_general | solution.py:40
  299.5 7.0 %convolution_convert_fusion = bf16[4096,1024]{1,0:T(8,128)(2,1)} fusion(bf16[512,4096]{1,0:T(8,128)(2,1)S(1)} %copy-done.9, bf16[512,1024]{1,0:T(8,128)(2,1)S(1)} %get-tuple-element.63), kind=kOutput, calls=%fused_computation.4 | convolution fusion | flops 4299161600 | bytes 13631488 | tf_op jit(solution)/shard_map/dot_general | solution.py:40
  306.5 146.1 %attn_bwd.1 = (bf16[2,64,8192]{2,1,0:T(8,128)(2,1)}, bf16[16,64,512]{2,1,0:T(8,128)(2,1)}, f32[32,1024]{1,0:T(8,128)}, f32[32,4096]{1,0:T(8,128)}, f32[128,1024]{1,0:T(8,128)}) custom-call(bf16[7168,7168]{1,0:T(8,128)(2,1)} %get-tuple-element.41.p_ref, bf16[1024,1024]{1,0:T(8,128)(2,1)} %get-tuple-element.42.tail_ref, ...), custom_call_target="tpu_custom_call" | custom-call | flops 26306674688 | bytes 102760448 | tf_op jit(solution)/shard_map/attn_bwd/pallas_call | solution.py:1253
  454.1 86.5 %last_reduce.1 = (f32[32,3072]{1,0:T(8,128)}, f32[512,1024]{1,0:T(8,128)}, f32[8,128]{1,0:T(8,128)}) custom-call(bf16[2,64,8192]{2,1,0:T(8,128)(2,1)} %get-tuple-element.46.dkv_ref, bf16[16,64,512]{2,1,0:T(8,128)(2,1)} %get-tuple-element.47.dq_ref, bf16[512,1024]{1,0:T(8,128)(2,1)} %bitcast.69, bf16[1024,3072]{1,0:T(8,128)(2,1)} %bitcast.67, ...), custom_call_target="tpu_custom_call" | custom-call | tf_op jit(solution)/shard_map/last_reduce/pallas_call | solution.py:1458
  540.6 1.8 fusion.14
  542.4 1.3 slice_bitcast_fusion.1
  544.3 1.5 fusion.16
  545.8 3.3 copy.45
  (78 shorter events, 10.1 us)
Async XLA Ops:
  233.2 1.6 copy-start.2
  238.3 10.4 %slice-start.2 = ((s8[8388608]{0:T(1024)(128)(4,1)}), s8[4194304]{0:T(1024)(128)(4,1)S(1)}, s32[]{:S(2)}) async-start(s8[8388608]{0:T(1024)(128)(4,1)} %bitcast.96), calls=%async_computation.2 | async-start | bytes 8388608
  238.6 10.0 %slice-start.3 = ((s8[8388608]{0:T(1024)(128)(4,1)}), s8[4194304]{0:T(1024)(128)(4,1)S(1)}, s32[]{:S(2)}) async-start(s8[8388608]{0:T(1024)(128)(4,1)} %bitcast.96), calls=%async_computation.3 | async-start | bytes 8388608
  248.7 6.0 %copy-start.8 = (bf16[512,4096]{1,0:T(8,128)(2,1)}, bf16[512,4096]{1,0:T(8,128)(2,1)S(1)}, u32[]{:S(2)}) copy-start(bf16[512,4096]{1,0:T(8,128)(2,1)S(1)} %get-tuple-element.91) | copy-start | bytes 12582916
  254.7 2.9 copy-start
  263.6 13.4 %slice-start = ((s8[8388608]{0:T(1024)(128)(4,1)}), s8[4194304]{0:T(1024)(128)(4,1)S(1)}, s32[]{:S(2)}) async-start(s8[8388608]{0:T(1024)(128)(4,1)} %bitcast.92), calls=%async_computation | async-start | bytes 8388608
  263.9 13.2 %slice-start.1 = ((s8[8388608]{0:T(1024)(128)(4,1)}), s8[4194304]{0:T(1024)(128)(4,1)S(1)}, s32[]{:S(2)}) async-start(s8[8388608]{0:T(1024)(128)(4,1)} %bitcast.92), calls=%async_computation.1 | async-start | bytes 8388608
  284.9 2.4 copy-start.3
  285.2 4.4 copy-start.1
  287.3 2.3 copy-start.4
  289.6 2.6 copy-start.10
  292.2 7.3 %copy-start.9 = (bf16[512,4096]{1,0:T(8,128)(2,1)S(1)}, bf16[512,4096]{1,0:T(8,128)(2,1)}, u32[]{:S(2)}) copy-start(bf16[512,4096]{1,0:T(8,128)(2,1)} %copy-done.8) | copy-start | bytes 12582916
  545.8 3.3 copy-start.7
  545.8 3.9 copy-start.6
  545.8 4.7 copy-start.5

commit v5 on v4

--- a/solution.py
+++ b/solution.py
@@ -632,7 +632,7 @@
                 for col in range(0, cols, UNIT)
             ]
         )
-    most = max(len(column) for column in columns)
+    most = max([len(column) for column in columns] + [0])
     return [column[place] for place in range(most) for column in columns if place < len(column)]
 
 
@@ -660,10 +660,15 @@
 
 
 def SCHEDULE(number):
-    if number < 2:
-        return (-2, -1, -0.9, -0.8, 1)
-    begin = (number - 2) // 2
-    return (begin, begin + 1, begin + 2, begin + 4, begin + 7)
+    return (-4, -2, -1, -0.9 if number < 4 else number / 2, 5 + number)
+
+
+def home(block, main):
+    return jnp.where(block < main, block // 2 + main // 2 * lax.rem(block, 2), block)
+
+
+def cuts(width, cols):
+    return [(first, min(first + cols, width)) for first in range(0, width, cols)]
 
 
 def attn_fwd_kernel(
@@ -674,14 +679,16 @@
     p_ref, tail_ref, o_ref, inv_ref, kept_ref, tokens_ref, qkv_out, vec_out = refs[:8]
     wholes, refs = refs[8 : 8 + count], refs[8 + count :]
     (
-    weights, vecs, qkv_ref, land, keys, values, s0, s1, m0, m1,
+    weights, vecs, qkv_ref, land, keys, values, s0, s1, m0, m1, now, peaks, acc, top,
     own_sem, kv_send, kv_recv, q_send, q_recv, o_send, o_recv, send, recv,
     ) = refs
     step, steps = pl.program_id(0), pl.num_programs(0)
-    length, long = land.shape[2], p_ref.shape[1]
+    length, part = land.shape[2], p_ref.shape[1]
+    long = 2 * part
     width = 2 * rows
-    tail, chunks = length - long, long // cols
+    tail, pieces = length - long, cuts(part, cols)
     main = long // width
+    side, turn = step // main, lax.rem(step, main)
     scale = LOG2E * HEAD_DIM**-0.5
 
     me = Place(blks)
@@ -693,6 +700,10 @@
     def ahead(block):
         return lax.rem(block + group - me.index, group)
 
+    def spot(tensor, block):
+        return home(block, main) if tensor else block
+
+    early = (me.index < main) & (lax.rem(me.index, 2) == 0)
     swaps = [[], [], []]
     for tensor, send_sem, recv_sem in ((0, q_send, q_recv), (1, kv_send, kv_recv), (2, kv_send, kv_recv)):
         for ahead_by in range(1, group):
@@ -701,7 +712,7 @@
             swaps[tensor].append(
                 wire(
                     qkv_ref.at[tensor, peer],
-                    lanes(land, (tensor, ALL), me.index * width, width),
+                    lanes(land, (tensor, ALL), spot(tensor, me.index) * width, width),
                     send_sem.at[slot],
                     recv_sem.at[slot],
                     device,
@@ -709,16 +720,34 @@
             )
     keep = pltpu.make_async_copy(land, kept_ref, own_sem.at[1])
 
-    def await_queries(block):
+    def await_from(tensor, block):
         @pl.when(block != me.index)
         def _():
+            send_sem, recv_sem = (kv_send, kv_recv) if tensor else (q_send, q_recv)
             wire(
-                qkv_ref.at[0, block],
-                lanes(land, (0, ALL), block * width, width),
-                q_send.at[0],
-                q_recv.at[ahead(block)],
+                qkv_ref.at[tensor, block],
+                lanes(land, (tensor, ALL), spot(tensor, block) * width, width),
+                send_sem.at[0],
+                recv_sem.at[ahead(block) + (group if tensor == 2 else 0)],
                 me.member(block),
             ).wait_recv()
+
+    def await_keys(first):
+        for block in range(first, main, 2):
+            await_from(1, block)
+            await_from(2, block)
+        here = slice(first * part, (first + 1) * part)
+        keys[first, 0:HEAD_DIM, :] = land[1, :, here]
+        keys[first, HEAD_DIM:, :] = land[1, :, here]
+        values[first, 0:HEAD_DIM, :] = land[2, :, here]
+        values[first, HEAD_DIM:, :] = ones_row(part)
+
+    def ones_row(columns):
+        return (
+            (lax.broadcasted_iota(jnp.int32, (16, columns), 0) == 0)
+            .astype(jnp.float32)
+            .astype(jnp.bfloat16)
+        )
 
     def send_block(block, slot, start):
         source = lanes(o_ref, (ALL,), block * width, width)
@@ -750,10 +779,10 @@
     half = UNIT // 2
     fronts = []
     for unit, ref in enumerate((wq, wk, wv)):
-        for side in range(2):
-            piece = ((0, EDGE), (unit * UNIT + side * half, half))
-            source = ref.at[:, pl.ds(side * half, half)]
-            fronts.append(Gather(me, wires, weights, piece, side == 1, source=source))
+        for flank in range(2):
+            piece = ((0, EDGE), (unit * UNIT + flank * half, half))
+            source = ref.at[:, pl.ds(flank * half, half)]
+            fronts.append(Gather(me, wires, weights, piece, flank == 1, source=source))
     vectors = Gather(me, wires, vecs, ((0, EDGE), (0, vecs.shape[5])), False)
     units = weight_units([share.shape for share in shares])
     plan = [
@@ -778,7 +807,12 @@
     moves = {}
     for number in range(len(units)):
         for stage, at in enumerate(SCHEDULE(number), 1):
+            at = min(int(2 * at), 2 * main - 1) if at >= 0 else at
             moves.setdefault(at, []).append((plan[number], stage))
+
+    def pace(at):
+        for unit, stage in moves.get(at, []):
+            unit.stage(stage)
 
     def front(tensor, *stages):
         for stage in stages:
@@ -798,7 +832,7 @@
             qkv_ref[tensor, heads[0] : heads[1]] = found.astype(jnp.bfloat16).reshape(
                 heads[1] - heads[0], HEAD_DIM, width
             )
-        own = pl.ds(pl.multiple_of(me.index * width, width), width)
+        own = pl.ds(pl.multiple_of(spot(tensor, me.index) * width, width), width)
         land[tensor, :, own] = qkv_ref[tensor, me.index]
 
     def take_queries(start):
@@ -806,35 +840,29 @@
         high = part.astype(jnp.bfloat16).astype(jnp.float32)
         return jnp.concatenate([high, part - high], 0).T.astype(jnp.bfloat16)
 
-    def score(queries, store, j, peak):
+    def score(queries, at, store, piece, peak):
         found = jnp.dot(
-            queries, keys[:, j * cols : (j + 1) * cols], preferred_element_type=jnp.float32
-        )
-        store[:, j * cols : (j + 1) * cols] = found
-        for first in range(0, cols, 128):
-            piece = found[:, first : first + 128]
-            peak = piece if peak is None else jnp.maximum(peak, piece)
+            queries, keys[at, :, piece[0] : piece[1]], preferred_element_type=jnp.float32
+        )
+        store[:, piece[0] : piece[1]] = found
+        for first in range(0, piece[1] - piece[0], 128):
+            some = found[:, first : first + 128]
+            peak = some if peak is None else jnp.maximum(peak, some)
         return peak
 
     def keep_peak(store, peak):
         store[...] = jnp.broadcast_to(jnp.max(peak, axis=1, keepdims=True), store.shape)
 
-    def weigh(store, peak, j, row, total):
-        weights = jnp.exp2(store[:, j * cols : (j + 1) * cols] - peak[:, :1]).astype(jnp.bfloat16)
-        p_ref[row : row + rows, j * cols : (j + 1) * cols] = weights
+    def weigh(store, peak, piece, row, total):
+        weights = jnp.exp2(store[:, piece[0] : piece[1]] - peak[:, :1]).astype(jnp.bfloat16)
+        p_ref[row : row + rows, piece[0] : piece[1]] = weights
         term = lax.dot_general(
-            values[:, j * cols : (j + 1) * cols],
+            values[side, :, piece[0] : piece[1]],
             weights,
             BY_LAST,
             preferred_element_type=jnp.float32,
         )
         return term if total is None else total + term
-
-    def finish(total, start):
-        place = pl.ds(pl.multiple_of(start, rows), rows)
-        inverse = 1.0 / total[HEAD_DIM : HEAD_DIM + 1]
-        o_ref[:, place] = (total[:HEAD_DIM] * inverse).astype(jnp.bfloat16)
-        inv_ref[:, place] = jnp.broadcast_to(inverse, (8, rows))
 
     @pl.when(step == 0)
     def _():
@@ -846,58 +874,65 @@
         vecs[here] = turned[:EDGE].astype(jnp.bfloat16)
         greet([me.peer(by)[1] for by in range(1, group)] + [me.at(x=1 - me.x)])
         vectors.stage(0)
-        for tensor in (1, 2, 0):
-            front(tensor, 0)
-        for unit in plan:
-            unit.stage(0)
+        front(1, 0)
         for copy in local:
             copy.wait()
         vectors.stage(1)
         front(1, 1)
+        front(2, 0)
         front(1, 2)
+        front(0, 0)
+        for unit in plan:
+            unit.stage(0)
         vectors.stage(2)
         front(2, 1)
+        pace(-5)
         front(1, 3)
         front(2, 2)
         vectors.stage(3)
         front(0, 1)
+        pace(-4)
         front(1, 4)
         project(1, None)
-        for copy in swaps[1]:
-            copy.start()
+
+        @pl.when(early)
+        def _():
+            for copy in swaps[1]:
+                copy.start()
+
+        pace(-3)
         front(2, 3)
         front(0, 2)
         vectors.stage(4)
         front(2, 4)
         project(2, 1)
-        for copy in swaps[2]:
-            copy.start()
+
+        @pl.when(early)
+        def _():
+            for copy in swaps[2]:
+                copy.start()
+
         front(0, 3)
-        for unit, stage in moves.get(-2, []):
-            unit.stage(stage)
+        pace(-2)
         front(0, 4)
         keep_weights.start()
         keep_vectors.start()
         project(0, 0)
         for copy in swaps[0]:
             copy.start()
+
+        @pl.when(jnp.logical_not(early))
+        def _():
+            for copy in swaps[1] + swaps[2]:
+                copy.start()
+
         for at in (-1, -0.9, -0.8, -0.7, -0.6):
-            for unit, stage in moves.get(at, []):
-                unit.stage(stage)
-        for copy in swaps[1] + swaps[2]:
-            copy.wait_recv()
-        keys[0:HEAD_DIM, :] = land[1]
-        keys[HEAD_DIM:, :] = land[1]
-        values[0:HEAD_DIM, :] = land[2]
-        values[HEAD_DIM:, :] = (
-            (lax.broadcasted_iota(jnp.int32, (16, length), 0) == 0)
-            .astype(jnp.float32)
-            .astype(jnp.bfloat16)
-        )
-        await_queries(block_at(0))
+            pace(at)
+        await_keys(0)
+        await_from(0, block_at(0))
         queries, peak = take_queries(block_at(0) * width), None
-        for j in range(chunks):
-            peak = score(queries, s0, j, peak)
+        for piece in pieces:
+            peak = score(queries, 0, s0, piece, peak)
         keep_peak(m0, peak)
 
     for at, todo in sorted((entry for entry in moves.items() if entry[0] >= 0), key=lambda entry: entry[0]):
@@ -907,40 +942,71 @@
             for unit, stage in todo:
                 unit.stage(stage)
 
-    block = block_at(step)
-    later = block_at(jnp.minimum(step + 1, steps - 1))
-
-    @pl.when(step < steps - 1)
+    @pl.when(step == main - 1)
     def _():
-        await_queries(later)
+        await_keys(1)
+
+    next_step = jnp.minimum(step + 1, steps - 1)
+    block = block_at(turn)
+    later, later_side = block_at(lax.rem(next_step, main)), next_step // main
+    place = pl.ds(pl.multiple_of(block * width, width), width)
+
+    @pl.when(step < main - 1)
+    def _():
+        await_from(0, later)
 
     for half, (old, old_peak, new, new_peak) in enumerate(((s0, m0, s1, m1), (s1, m1, s0, m0))):
         queries = take_queries(block * width + rows if half == 0 else later * width)
+        at = side if half == 0 else later_side
         total, peak = None, None
-        for j in range(chunks):
-            total = weigh(old, old_peak, j, half * rows, total)
-            peak = score(queries, new, j, peak)
+        for piece in pieces:
+            total = weigh(old, old_peak, piece, half * rows, total)
+            peak = score(queries, at, new, piece, peak)
+        here = slice(half * rows, (half + 1) * rows)
+        peaks[:, here] = old_peak[...].T[0:8]
+        now[:, here] = total
         keep_peak(new_peak, peak)
-        finish(total, block * width + half * rows)
-    send_block(block, step, True)
+
+    @pl.when(side == 0)
+    def _():
+        acc[:, place] = now[...]
+        top[:, place] = peaks[...]
+
+    @pl.when(side == 1)
+    def _():
+        first, second = top[0:1, place], peaks[0:1, :]
+        peak = jnp.maximum(first, second)
+        first, second = jnp.exp2(first - peak), jnp.exp2(second - peak)
+        total = acc[:, place] * first + now[...] * second
+        inverse = 1.0 / total[HEAD_DIM : HEAD_DIM + 1]
+        o_ref[:, place] = (total[:HEAD_DIM] * inverse).astype(jnp.bfloat16)
+        row = lax.broadcasted_iota(jnp.int32, (8, width), 0)
+        inv_ref[:, place] = jnp.where(row == 0, first * inverse, second * inverse)
+        send_block(block, turn, True)
 
     @pl.when(step == steps - 1)
     def _():
-        for number in range(tail // width):
-            await_queries(main + number)
+        for block in range(main, group):
+            for tensor in range(3):
+                await_from(tensor, block)
         keep.start()
+        tail_keys = jnp.concatenate([land[1, :, long:], land[1, :, long:]], 0)
+        tail_values = jnp.concatenate([land[2, :, long:], ones_row(tail)], 0)
         for first in range(0, tail, rows):
             queries = take_queries(long + first)
-            found = jnp.dot(queries, keys[:, long:], preferred_element_type=jnp.float32)
+            found = jnp.dot(queries, tail_keys, preferred_element_type=jnp.float32)
             allowed = down_ref[first : first + rows, :1] == across_ref[:1, :]
             found = jnp.where(allowed, found, -1e30)
             peak = jnp.max(found, axis=1, keepdims=True)
             weights = jnp.exp2(found - peak).astype(jnp.bfloat16)
             tail_ref[first : first + rows, :] = weights
             total = lax.dot_general(
-                values[:, long:], weights, BY_LAST, preferred_element_type=jnp.float32
+                tail_values, weights, BY_LAST, preferred_element_type=jnp.float32
             )
-            finish(total, long + first)
+            here = slice(long + first, long + first + rows)
+            inverse = 1.0 / total[HEAD_DIM : HEAD_DIM + 1]
+            o_ref[:, here] = (total[:HEAD_DIM] * inverse).astype(jnp.bfloat16)
+            inv_ref[:, here] = jnp.broadcast_to(inverse, (8, rows))
             if (first + rows) % width == 0:
                 number = main + first // width
                 send_block(number, number, True)
@@ -950,8 +1016,8 @@
             copy.wait_send()
         keep_weights.wait()
         keep_vectors.wait()
-        for turn in range(main):
-            send_block(block_at(turn), turn, False)
+        for number in range(main):
+            send_block(block_at(number), number, False)
         for number in range(main, group):
             send_block(number, number, False)
         for ahead_by in range(1, group):
@@ -978,6 +1044,7 @@
     length = group * width
     tail = seg.shape[0]
     long = length - tail
+    main = long // width
     down = jnp.broadcast_to(seg[:, None], (tail, 128))
     across = jnp.broadcast_to(seg[None, :], (8, tail))
     anywhere = pl.BlockSpec(memory_space=pl.ANY)
@@ -989,11 +1056,11 @@
     pair = [pltpu.SemaphoreType.DMA((group,))] * 2
     return pl.pallas_call(
         functools.partial(attn_fwd_kernel, blks, rows, cols, len(shares)),
-        grid=(long // width,),
+        grid=(2 * (long // width),),
         in_specs=[once(x.shape), once(vec.shape), once((tail, 128)), once((8, tail))]
         + [once(share.shape) for share in fronts + shares],
         out_specs=[
-            pl.BlockSpec((width, long), lambda step: (step, 0)),
+            pl.BlockSpec((width, long // 2), lambda step: (lax.rem(step, main), step // main)),
             once((tail, tail)),
             once((HEAD_DIM, length)),
             once((8, length)),
@@ -1015,12 +1082,16 @@
             pltpu.VMEM(vectors.shape, vectors.dtype),
             pltpu.VMEM((3, group, HEAD_DIM, width), jnp.bfloat16),
             pltpu.VMEM(kept.shape, kept.dtype),
-            pltpu.VMEM((2 * HEAD_DIM, length), jnp.bfloat16),
-            pltpu.VMEM((HEAD_DIM + 16, length), jnp.bfloat16),
-            pltpu.VMEM((rows, long), jnp.float32),
-            pltpu.VMEM((rows, long), jnp.float32),
+            pltpu.VMEM((2, 2 * HEAD_DIM, long // 2), jnp.bfloat16),
+            pltpu.VMEM((2, HEAD_DIM + 16, long // 2), jnp.bfloat16),
+            pltpu.VMEM((rows, long // 2), jnp.float32),
+            pltpu.VMEM((rows, long // 2), jnp.float32),
             pltpu.VMEM((rows, 128), jnp.float32),
             pltpu.VMEM((rows, 128), jnp.float32),
+            pltpu.VMEM((HEAD_DIM + 16, width), jnp.float32),
+            pltpu.VMEM((8, width), jnp.float32),
+            pltpu.VMEM((HEAD_DIM + 16, long), jnp.float32),
+            pltpu.VMEM((8, long), jnp.float32),
             pltpu.SemaphoreType.DMA((11,)),
             pltpu.SemaphoreType.DMA((2 * group,)),
             pltpu.SemaphoreType.DMA((2 * group,)),
@@ -1042,15 +1113,22 @@
 
 
 def attn_bwd_kernel(
-    blks, rows, cols, p_ref, tail_ref, qkv_ref, o_ref, inv_ref, grads_ref, wo, we, wr,
-    dkv_ref, tokens_ref, go, ge, gr,
-    land, dq_out, values, dk_sum, dv_sum, own, r0, r1a, r1b, r2, r3, send, recv,
-    own_sem, do_send, do_recv, dq_send, dq_recv,
+    blks, rows, cols, count, *refs
 ):
+    p_ref, tail_ref, qkv_ref, o_ref, inv_ref, grads_ref = refs[:6]
+    partials, refs = refs[6 : 6 + count], refs[6 + count :]
+    dkv_ref, tokens_ref, kv_tokens = refs[:3]
+    totals, refs = refs[3 : 3 + count], refs[3 + count :]
+    (
+    land, dq_out, dq_sum, keys, values, dk_sum, dv_sum, tail_dkv, early_dkv, own, r0, r1a, r1b, r2, r3, send, recv,
+    own_sem, do_send, do_recv, dq_send, dq_recv, kv_send, kv_recv,
+    ) = refs
     step, steps = pl.program_id(0), pl.num_programs(0)
-    length, long = land.shape[1], p_ref.shape[1]
-    tail, chunks = length - long, long // cols
+    length, part = land.shape[1], p_ref.shape[1]
+    long = 2 * part
+    tail, pieces = length - long, cuts(part, cols)
     main = long // rows
+    side, turn = step // main, lax.rem(step, main)
     scale = HEAD_DIM**-0.5
 
     me = Place(blks)
@@ -1111,8 +1189,42 @@
             else:
                 local.wait()
 
+    early = (me.index >= main) | (lax.rem(me.index, 2) == 0)
+
+    def early_sends():
+        for number in range(main // 2):
+            block = 2 * lax.rem(number + me.index // 2, main // 2)
+            yield number, block, lanes(early_dkv, (ALL, ALL), block // 2 * rows, rows)
+        for block in range(main, group):
+            source = tail_dkv.at[:, :, pl.ds((block - main) * rows, rows)]
+            yield main // 2 + block - main, block, source
+
+    def send_early(start):
+        for slot, block, source in early_sends():
+            remote = wire(
+                source,
+                kv_tokens.at[:, me.index],
+                kv_send.at[slot],
+                kv_recv.at[lax.rem(me.index + group - block, group)],
+                me.member(block),
+            )
+            local = pltpu.make_async_copy(source, kv_tokens.at[:, me.index], own_sem.at[4])
+
+            @pl.when(block != me.index)
+            def _():
+                if start:
+                    remote.start()
+                else:
+                    remote.wait_send()
+
+            @pl.when(block == me.index)
+            def _():
+                if start:
+                    local.start()
+                else:
+                    local.wait()
+
     wires = Wires(send, recv)
-    partials, totals = (wo, we, wr), (go, ge, gr)
     units = weight_units([partial.shape[4:] for partial in partials])
     plan, moves = [], {}
     for number, (which, piece) in enumerate(units):
@@ -1134,12 +1246,13 @@
         )
         plan.append(unit)
         pair = number // 2
-        for stage, at in enumerate((0, pair, pair + 1, 2 * pair + 4, 2 * pair + 6)):
-            moves.setdefault(min(at, main - 1), []).append((stage, number, unit))
-
-    def prepare(start, width):
+        for stage, at in enumerate((1.5 * pair, 1.5 * pair, 1.5 * pair + 1, 2 * pair + 4, 2 * pair + 6)):
+            moves.setdefault(min(int(2 * at), 2 * main - 1), []).append((stage, number, unit))
+
+    def prepare(start, width, at):
         place = pl.ds(pl.multiple_of(start, width), width)
-        grads, inverse = land[:, place].astype(jnp.float32), inv_ref[:1, place]
+        grads = land[:, place].astype(jnp.float32)
+        inverse = jnp.where(at == 0, inv_ref[0:1, place], inv_ref[1:2, place])
         delta = -jnp.sum(grads * o_ref[:, place].astype(jnp.float32), axis=0, keepdims=True)
         delta = delta * inverse
         high = delta.astype(jnp.bfloat16).astype(jnp.float32)
@@ -1149,7 +1262,7 @@
         wide = jnp.concatenate([grads, extra], 0).T.astype(jnp.bfloat16)
         return wide, grads.astype(jnp.bfloat16), qkv_ref[0, :, place]
 
-    def part(wide, grads, queries, weights, keys_here, values_here, dq):
+    def terms(wide, grads, queries, weights, keys_here, values_here, dq):
         dp = jnp.dot(wide, values_here, preferred_element_type=jnp.float32)
         ds = (weights.astype(jnp.float32) * dp).astype(jnp.bfloat16)
         dv = jnp.dot(grads, weights, preferred_element_type=jnp.float32)
@@ -1157,6 +1270,13 @@
         term = lax.dot_general(keys_here, ds, BY_LAST, preferred_element_type=jnp.float32)
         return (term if dq is None else dq + term), dk, dv
 
+    def ones_rows(columns):
+        return (
+            (lax.broadcasted_iota(jnp.int32, (16, columns), 0) < 2)
+            .astype(jnp.float32)
+            .astype(jnp.bfloat16)
+        )
+
     @pl.when(step == 0)
     def _():
         own_in.start()
@@ -1173,59 +1293,87 @@
 
     @pl.when(step == 0)
     def _():
-        values[0:HEAD_DIM, :] = qkv_ref[2]
-        values[HEAD_DIM:, :] = (
-            (lax.broadcasted_iota(jnp.int32, (16, length), 0) < 2)
-            .astype(jnp.float32)
-            .astype(jnp.bfloat16)
-        )
+        for at in range(2):
+            here = slice(at * part, (at + 1) * part)
+            keys[at] = qkv_ref[1, :, here]
+            values[at, 0:HEAD_DIM, :] = qkv_ref[2, :, here]
+            values[at, HEAD_DIM:, :] = ones_rows(part)
         dk_sum[...] = jnp.zeros_like(dk_sum)
         dv_sum[...] = jnp.zeros_like(dv_sum)
         own_in.wait()
 
-    block = block_at(step)
-    await_grads(block)
-    wide, grads, queries = prepare(block * rows, rows)
+    block = block_at(turn)
+    place = pl.ds(pl.multiple_of(block * rows, rows), rows)
+
+    @pl.when(side == 0)
+    def _():
+        await_grads(block)
+
+    wide, grads, queries = prepare(block * rows, rows, side)
     dq = None
-    for j in range(chunks):
-        here = slice(j * cols, (j + 1) * cols)
-        dq, dk, dv = part(
-            wide, grads, queries, p_ref[:, here], qkv_ref[1, :, here], values[:, here], dq
-        )
-        dk_sum[:, here] += dk
-        dv_sum[:, here] += dv
-    dq_out[:, pl.ds(pl.multiple_of(block * rows, rows), rows)] = (dq * scale).astype(jnp.bfloat16)
-    send_block(block, step, True)
-
-    @pl.when(step == steps - 1)
+    for first, end in pieces:
+        dq, dk, dv = terms(
+            wide,
+            grads,
+            queries,
+            p_ref[:, first:end],
+            keys[side, :, first:end],
+            values[side, :, first:end],
+            dq,
+        )
+        dk_sum[side, :, first:end] += dk
+        dv_sum[side, :, first:end] += dv
+
+    @pl.when(side == 0)
     def _():
+        dq_sum[:, place] = dq
+
+    @pl.when(side == 1)
+    def _():
+        dq_out[:, place] = ((dq_sum[:, place] + dq) * scale).astype(jnp.bfloat16)
+        send_block(block, turn, True)
+
+    @pl.when(step == main - 1)
+    def _():
+        tail_keys = qkv_ref[1, :, long:]
+        tail_values = jnp.concatenate([qkv_ref[2, :, long:], ones_rows(tail)], 0)
+        dk_total, dv_total = None, None
         for number in range(main, group):
             await_grads(number)
             first = (number - main) * rows
-            wide, grads, queries = prepare(long + first, rows)
-            dq, dk, dv = part(
+            wide, grads, queries = prepare(long + first, rows, 0)
+            dq, dk, dv = terms(
                 wide,
                 grads,
                 queries,
                 tail_ref[first : first + rows, :],
-                qkv_ref[1, :, long:],
-                values[:, long:],
+                tail_keys,
+                tail_values,
                 None,
             )
-            dk_sum[:, long:] += dk
-            dv_sum[:, long:] += dv
+            dk_total = dk if dk_total is None else dk_total + dk
+            dv_total = dv if dv_total is None else dv_total + dv
             dq_out[:, long + first : long + first + rows] = (dq * scale).astype(jnp.bfloat16)
             send_block(number, number, True)
-        dkv_ref[0] = (dk_sum[...] * scale).astype(jnp.bfloat16)
-        dkv_ref[1] = dv_sum[...].astype(jnp.bfloat16)
+        tail_dkv[0] = (dk_total * scale).astype(jnp.bfloat16)
+        tail_dkv[1] = dv_total.astype(jnp.bfloat16)
+        early_dkv[0] = (dk_sum[0] * scale).astype(jnp.bfloat16)
+        early_dkv[1] = dv_sum[0].astype(jnp.bfloat16)
+        send_early(True)
+
+    @pl.when(step == steps - 1)
+    def _():
+        dkv_ref[0] = (dk_sum[1] * scale).astype(jnp.bfloat16)
+        dkv_ref[1] = dv_sum[1].astype(jnp.bfloat16)
         for unit in plan:
             unit.stage(5)
         for copy in do_copies:
             copy.wait_send()
-        for turn in range(main):
-            send_block(block_at(turn), turn, False)
+        for number in range(main):
+            send_block(block_at(number), number, False)
         for number in range(main, group):
             send_block(number, number, False)
+        send_early(False)
         for ahead_by in range(1, group):
             source, device = me.peer(ahead_by)
             wire(
@@ -1236,6 +1384,18 @@
                 device,
             ).wait_recv()
 
+        @pl.when(early)
+        def _():
+            for ahead_by in range(1, group):
+                source, device = me.peer(ahead_by)
+                wire(
+                    tail_dkv.at[:, :, pl.ds(0, rows)],
+                    kv_tokens.at[:, source],
+                    kv_send.at[0],
+                    kv_recv.at[ahead_by],
+                    device,
+                ).wait_recv()
+
 
 def attn_bwd(
     probs, tail_probs, kept, attn, inv_total, grad_attn, long, partials, collective_id, cols=1024
@@ -1246,36 +1406,43 @@
     length = kept.shape[2]
     tail = length - long
     group, _, rows = grad_attn.shape
+    main, part = long // rows, long // 2
     anywhere = pl.BlockSpec(memory_space=pl.ANY)
     edges = [(partial.shape[0] // devices, partial.shape[1]) for partial in partials]
     units = len(weight_units(edges))
     pair = [pltpu.SemaphoreType.DMA((group,))] * 2
     return pl.pallas_call(
-        functools.partial(attn_bwd_kernel, blks, rows, cols),
-        grid=(long // rows,),
+        functools.partial(attn_bwd_kernel, blks, rows, cols, len(partials)),
+        grid=(2 * main,),
         in_specs=[
-            pl.BlockSpec((rows, long), lambda step: (step, 0)),
+            pl.BlockSpec((rows, part), lambda step: (lax.rem(step, main), step // main)),
             once((tail, tail)),
             once(kept.shape),
             once((HEAD_DIM, length)),
             once((8, length)),
         ]
-        + [anywhere] * 4,
-        out_specs=[once((2, HEAD_DIM, length)), anywhere] + [once(edge) for edge in edges],
+        + [anywhere] * (1 + len(partials)),
+        out_specs=[once((2, HEAD_DIM, part)), anywhere, anywhere] + [once(edge) for edge in edges],
         out_shape=[
-            jax.ShapeDtypeStruct((2, HEAD_DIM, length), jnp.bfloat16),
+            jax.ShapeDtypeStruct((2, HEAD_DIM, part), jnp.bfloat16),
             jax.ShapeDtypeStruct((group, HEAD_DIM, rows), jnp.bfloat16),
+            jax.ShapeDtypeStruct((2, group, HEAD_DIM, rows), jnp.bfloat16),
         ]
         + [jax.ShapeDtypeStruct(edge, jnp.float32) for edge in edges],
         scratch_shapes=[
             pltpu.VMEM((HEAD_DIM, length), jnp.bfloat16),
             pltpu.VMEM((HEAD_DIM, length), jnp.bfloat16),
-            pltpu.VMEM((HEAD_DIM + 16, length), jnp.bfloat16),
-            pltpu.VMEM((HEAD_DIM, length), jnp.float32),
-            pltpu.VMEM((HEAD_DIM, length), jnp.float32),
+            pltpu.VMEM((HEAD_DIM, long), jnp.float32),
+            pltpu.VMEM((2, HEAD_DIM, part), jnp.bfloat16),
+            pltpu.VMEM((2, HEAD_DIM + 16, part), jnp.bfloat16),
+            pltpu.VMEM((2, HEAD_DIM, part), jnp.float32),
+            pltpu.VMEM((2, HEAD_DIM, part), jnp.float32),
+            pltpu.VMEM((2, HEAD_DIM, tail), jnp.bfloat16),
+            pltpu.VMEM((2, HEAD_DIM, part), jnp.bfloat16),
             pltpu.VMEM((2, 2, blks, 2, EDGE, UNIT), jnp.bfloat16),
-            *reduce_scratch(units, blks),
-            pltpu.SemaphoreType.DMA((4,)),
+            *reduce_scratch(max(units, 2), blks),
+            pltpu.SemaphoreType.DMA((5,)),
+            *pair,
             *pair,
             *pair,
         ],
@@ -1293,7 +1460,7 @@
 
 
 def last_kernel(
-    blks, devices, dkv_ref, dq_ref, x_ref, w_ref, base_ref, sums_ref,
+    blks, devices, dkv_ref, kv_tokens, dq_ref, x_ref, w_ref, base_ref, sums_ref,
     dw_out, dx_out, sums_out,
     grads, x, xt, weights, base, turned_dx, partial, bias, landed,
     r0, r1a, r1b, r2, r3, send, recv,
@@ -1313,28 +1480,79 @@
                 (w_ref, weights),
                 (base_ref, base),
                 (sums_ref, bias),
-                (dkv_ref.at[0, :, pl.ds(pl.multiple_of(me.index * width, width), width)], grads.at[1, me.index]),
-                (dkv_ref.at[1, :, pl.ds(pl.multiple_of(me.index * width, width), width)], grads.at[2, me.index]),
             )
         )
     ]
     for copy in loads:
         copy.start()
     greet(others)
-    kv_copies = [[], []]
+    main = 2 * (dkv_ref.shape[2] // width)
+    odd = (me.index < main) & (lax.rem(me.index, 2) == 1)
+
+    def late_sends(which, start):
+        for number in range(main // 2):
+            block = 2 * lax.rem(number + me.index // 2, main // 2) + 1
+            source = lanes(dkv_ref, (which, ALL), block // 2 * width, width)
+            remote = wire(
+                source,
+                grads.at[which + 1, me.index],
+                kv_send.at[which * group + number],
+                kv_recv.at[which * group + lax.rem(me.index + group - block, group)],
+                me.member(block),
+            )
+            local = pltpu.make_async_copy(
+                source, grads.at[which + 1, me.index], own_sem.at[5 + which]
+            )
+
+            @pl.when(block != me.index)
+            def _():
+                if start:
+                    remote.start()
+                else:
+                    remote.wait_send()
+
+            if start:
+
+                @pl.when(block == me.index)
+                def _():
+                    local.start()
+
+    def await_late(which):
+        @pl.when(odd)
+        def _():
+            pltpu.make_async_copy(
+                dkv_ref.at[which, :, pl.ds(0, width)],
+                grads.at[which + 1, me.index],
+                own_sem.at[5 + which],
+            ).wait()
+            for ahead_by in range(1, group):
+                source, device = me.peer(ahead_by)
+                wire(
+                    dkv_ref.at[which, :, pl.ds(0, width)],
+                    grads.at[which + 1, source],
+                    kv_send.at[0],
+                    kv_recv.at[which * group + ahead_by],
+                    device,
+                ).wait_recv()
+
+        @pl.when(jnp.logical_not(odd))
+        def _():
+            pltpu.make_async_copy(
+                kv_tokens.at[pl.ds(which, 1)],
+                grads.at[pl.ds(which + 1, 1)],
+                own_sem.at[5 + which],
+            ).wait()
+
     for which in range(2):
-        for ahead_by in range(1, group):
-            peer, device = me.peer(group - ahead_by)
-            slot = which * group + ahead_by
-            copy = wire(
-                lanes(dkv_ref, (which, ALL), peer * width, width),
-                grads.at[which + 1, me.index],
-                kv_send.at[slot],
-                kv_recv.at[slot],
-                device,
-            )
-            copy.start()
-            kv_copies[which].append(copy)
+        late_sends(which, True)
+
+        @pl.when(jnp.logical_not(odd))
+        def _():
+            pltpu.make_async_copy(
+                kv_tokens.at[pl.ds(which, 1)],
+                grads.at[pl.ds(which + 1, 1)],
+                own_sem.at[5 + which],
+            ).start()
 
     wires = Wires(send, recv)
     plan = []
@@ -1411,17 +1629,13 @@
     loads[2].wait()
     work_input(0)
     stages(0, 3)
-    loads[5].wait()
-    for copy in kv_copies[0]:
-        copy.wait_recv()
+    await_late(0)
     work(1)
     stages(0, 4)
     stages(1, 2)
     work_input(1)
     stages(1, 3)
-    loads[6].wait()
-    for copy in kv_copies[1]:
-        copy.wait_recv()
+    await_late(1)
     work(2)
     note_bias(2, 4)
     small = []
@@ -1445,11 +1659,11 @@
     sums_out[...] = jnp.sum(landed[...], axis=0) + bias[index]
     stages(1, 5)
     stages(2, 5)
-    for copy in kv_copies[0] + kv_copies[1]:
-        copy.wait_send()
-
-
-def last_reduce(dkv, dq, x, w_qkv, base, sums, collective_id):
+    for which in range(2):
+        late_sends(which, False)
+
+
+def last_reduce(dkv, kv_tokens, dq, x, w_qkv, base, sums, collective_id):
     seqs, blks, heads = (lax.axis_size(name) for name in EVERY)
     devices = seqs * blks * heads
     group = blks * heads
@@ -1462,7 +1676,7 @@
             jax.ShapeDtypeStruct((width, depth), jnp.float32),
             jax.ShapeDtypeStruct(sums.shape[1:], jnp.float32),
         ],
-        in_specs=[pl.BlockSpec(memory_space=pl.ANY)] * 6,
+        in_specs=[pl.BlockSpec(memory_space=pl.ANY)] * 7,
         out_specs=[pl.BlockSpec(memory_space=pltpu.VMEM)] * 3,
         scratch_shapes=[
             pltpu.VMEM((3, group, HEAD_DIM, width), jnp.bfloat16),
@@ -1485,7 +1699,7 @@
             collective_id=collective_id, has_side_effects=True, vmem_limit_bytes=56 * 2**20
         ),
         name="last_reduce",
-    )(dkv, dq, x, w_qkv, base, sums)
+    )(dkv, kv_tokens, dq, x, w_qkv, base, sums)
 
 
 def tail_segments(doc_lengths, first, rows):
@@ -1493,6 +1707,9 @@
 
 
 BESIDE = ()
+
+
+AFTER = ()
 
 
 def shards_heads(
@@ -1596,7 +1813,14 @@
     grad_attn = right_dot(w_output, grad_branch).astype(jnp.bfloat16)
     grad_attn = grad_attn.reshape(HEADS, HEAD_DIM, tok_rows)
 
-    grad_kv, grad_query, grad_w_output, grad_w_expand, grad_w_reduce = attn_bwd(
+    grads = [grad.astype(jnp.bfloat16) for grad in (grad_w_output, grad_w_expand, grad_w_reduce)]
+    beside = {
+        which: lax.psum_scatter(grads[which], EVERY, scatter_dimension=0, tiled=True).astype(
+            jnp.float32
+        )
+        for which in AFTER
+    }
+    grad_kv, grad_query, kv_tokens, *totals = attn_bwd(
         probs,
         tail_probs,
         kept,
@@ -1604,9 +1828,12 @@
         inv_total,
         grad_attn,
         long_rows,
-        [grad.astype(jnp.bfloat16) for grad in (grad_w_output, grad_w_expand, grad_w_reduce)],
+        [grad for which, grad in enumerate(grads) if which not in AFTER],
         6,
     )
+    grad_w_output, grad_w_expand, grad_w_reduce = [
+        beside[which] if which in AFTER else totals.pop(0) for which in range(3)
+    ]
 
     sums = (
         jnp.zeros_like(b_output),
@@ -1622,7 +1849,7 @@
     sums = jnp.concatenate([term.reshape(-1, size) for term, size in zip(sums, sizes)], axis=1)
     sums = jnp.pad(sums, ((0, 0), (0, 8 * lane - sums.shape[1]))).reshape(-1, 8, lane)
     grad_w_qkv, grad_input, sums = last_reduce(
-        grad_kv, grad_query, flat_rows, w_qkv, grad_resid_one, sums, 7
+        grad_kv, kv_tokens, grad_query, flat_rows, w_qkv, grad_resid_one, sums, 7
     )
     owner = (lax.axis_index("seq") * blk_count + lax.axis_index("blk")) * head_count
     owner = owner + lax.axis_index("head")

time: 563 us -> 541 us (0.961)
  Pallas kernels: 459 us -> 440 us
    pallas_call x1, Pallas kernels: 86.5 us -> 66.1 us  [last_reduce(): pl.pallas_call(functools.partial(last_kernel, blks, devices), out_shape=[...]
    pallas_call x1, Pallas kernels: 146 us -> 164 us  [attn_bwd(): pl.pallas_call(functools.partial(attn_bwd_kernel, blks, rows, cols, len(p...]
    pallas_call x1, Pallas kernels: 227 us -> 210 us  [attn_fwd(): pl.pallas_call(functools.partial(attn_fwd_kernel, blks, rows, cols, len(s...]
where the time goes in v5:
time: 541 us; the launch traced here: 532 us
  Pallas kernels  440 us (81%)
  matrix products  58.8 us (11%)
  local copies, waits for them, and re-layouts  18.8 us (3%)
  other arithmetic  13.6 us (3%)
    pallas_call x1, Pallas kernels, attn_fwd(): pl.pallas_call(functools.partial(attn_fwd_kernel, blks, rows, cols, len(s...  210 us
    pallas_call x1, Pallas kernels, attn_bwd(): pl.pallas_call(functools.partial(attn_bwd_kernel, blks, rows, cols, len(p...  164 us
    pallas_call x1, Pallas kernels, last_reduce(): pl.pallas_call(functools.partial(last_kernel, blks, devices), out_shape=[...  66.1 us
    dot_general x3, matrix products, right_dot(): lax.dot_general(left, right, (((1,), (1,)), ((), ())), preferred_element_...  22.6 us
    dot_general x3, matrix products, plain_dot(): return jnp.dot(left, right, preferred_element_type=jnp.float32)  18.6 us
    dot_general x3, matrix products, left_dot(): lax.dot_general(left, right, (((0,), (0,)), ((), ())), preferred_element_...  17.6 us

profile of v5, /device:TPU:0, one launch (start us, length us, event | category | flops | bytes accessed | tf_op | source)
XLA Modules:
  0.0 532.5 jit_solution(1378968447410324146)
XLA Ops:
  1.4 1.4 pad_add_fusion.refs_1_
  2.8 0.9 reduce_window_sum.12
  5.0 1.0 broadcast_in_dim.21.refs_2_
  6.6 209.8 %attn_fwd.1 = (bf16[7168,7168]{1,0:T(8,128)(2,1)}, bf16[1024,1024]{1,0:T(8,128)(2,1)}, bf16[64,8192]{1,0:T(8,128)(2,1)}, f32[8,8192]{1,0:T(8,128)}, bf16[3,64,81...) custom-call(bf16[512,1024]{1,0:T(8,128)(2,1)} %bitcast.68, ...), custom_call_target="tpu_custom_call" | custom-call | flops 13153337344 | bytes 102760448 | tf_op jit(solution)/shard_map/attn_fwd/pallas_call | solution.py:1057
  216.4 1.3 copy.39
  218.1 3.3 fusion.17
  221.9 10.0 %multiply_convert_fusion = (bf16[512,4096]{1,0:T(8,128)(2,1)S(1)}, f32[512,4096]{1,0:T(8,128)}) fusion(f32[4096]{0:T(1024)S(1)} %add.223, bf16[1024,4096]{1,0:T(8,128)(2,1)} %bitcast.91, f32[512,1024]{1,0:T(8,128)S(1)} %get-tuple-element.92, f32[1024]{0:T(1024)S(1)} %add.220, f32[1024]{0:T(1024)S(1)} %mul.166, f32[512]{0:T(512)S(1)} %fusion.5, ...), kind=kOutput, calls=%fused_computation.2 | convolution fusion | flops 4310171648 | bytes 23097344 | tf_op jit(solution)/shard_map/dot_general | solution.py:36
  231.9 6.0 %fusion.18 = (f32[512]{0:T(512)S(1)}, f32[512,1024]{1,0:T(8,128)}) fusion(f32[1024]{0:T(1024)S(1)} %add.229, bf16[512,4096]{1,0:T(8,128)(2,1)S(1)} %get-tuple-element.93, bf16[4096,1024]{1,0:T(8,128)(2,1)S(1)} %bitcast.98, f32[1024]{0:T(1024)S(1)} %add.220, f32[1024]{0:T(1024)S(1)} %mul.166, f32[512]{0:T(512)S(1)} %fusion.5, ...), kind=kOutput, calls=%fused_computation.64 | convolution fusion | flops 4298636800 | bytes 16795648 | tf_op jit(solution)/shard_map/dot_general | solution.py:36
  238.8 1.9 multiply_reduce_fusion.3
  240.8 2.4 fusion
  243.3 3.6 fusion.13
  247.1 13.1 %convert_reduce_fusion = (f32[4096]{0:T(1024)S(1)}, bf16[512,4096]{1,0:T(8,128)(2,1)}) fusion(f32[512,4096]{1,0:T(8,128)} %get-tuple-element.94, f32[4096]{0:T(1024)S(1)} %add.223, bf16[512,1024]{1,0:T(8,128)(2,1)S(1)} %get-tuple-element.65, bf16[4096,1024]{1,0:T(8,128)(2,1)} %bitcast.95), kind=kOutput, calls=%fused_computation | convolution fusion | flops 4328517632 | bytes 22052864 | tf_op jit(solution)/shard_map/dot_general | solution.py:46
  260.3 7.2 %multiply_reduce_fusion = (f32[1024]{0:T(1024)S(1)}, f32[512]{0:T(512)S(1)}, f32[1024]{0:T(1024)S(1)}, f32[512,1024]{1,0:T(8,128)S(1)}) fusion(f32[512,1024]{1,0:T(8,128)S(1)} %get-tuple-element.92, f32[512]{0:T(512)S(1)} %fusion.5, f32[512]{0:T(512)S(1)} %broadcast_multiply_fusion.1, f32[1024]{0:T(1024)S(1)} %mul.166, ...), kind=kOutput, calls=%fused_computation.11 | convolution fusion | flops 4300207616 | bytes 18894848 | tf_op jit(solution)/shard_map/dot_general | solution.py:46
  268.4 2.1 copy-done.3
  270.5 2.3 convolution_convert_fusion.3
  272.8 2.6 convolution_convert_fusion.2
  275.4 7.3 %convolution_convert_fusion.1 = bf16[1024,4096]{1,0:T(8,128)(2,1)} fusion(bf16[512,4096]{1,0:T(8,128)(2,1)S(1)} %copy-done.10, f32[512,1024]{1,0:T(8,128)S(1)} %get-tuple-element.92, f32[1024]{0:T(1024)S(1)} %add.220, f32[1024]{0:T(1024)S(1)} %mul.166, f32[512]{0:T(512)S(1)} %fusion.5, f32[512]{0:T(512)S(1)} %broadcast_multiply_fusion.1), kind=kOutput, calls=%fused_computation.5 | convolution fusion | flops 4301783040 | bytes 14692352 | tf_op jit(solution)/shard_map/dot_general | solution.py:40
  282.7 7.0 %convolution_convert_fusion = bf16[4096,1024]{1,0:T(8,128)(2,1)} fusion(bf16[512,4096]{1,0:T(8,128)(2,1)S(1)} %copy-done.9, bf16[512,1024]{1,0:T(8,128)(2,1)S(1)} %get-tuple-element.65), kind=kOutput, calls=%fused_computation.4 | convolution fusion | flops 4299161600 | bytes 13631488 | tf_op jit(solution)/shard_map/dot_general | solution.py:40
  289.7 164.1 %attn_bwd.1 = (bf16[2,64,3584]{2,1,0:T(8,128)(2,1)}, bf16[16,64,512]{2,1,0:T(8,128)(2,1)}, bf16[2,16,64,512]{3,2,1,0:T(8,128)(2,1)}, f32[32,1024]{1,0:T(8,128)},...) custom-call(bf16[7168,7168]{1,0:T(8,128)(2,1)} %get-tuple-element.42.refs_0_, bf16[1024,1024]{1,0:T(8,128)(2,1)} %get-tuple-element.43.refs_1_, ...), custom_call_target="tpu_custom_call" | custom-call | flops 26306674688 | bytes 102760448 | tf_op jit(solution)/shard_map/attn_bwd/pallas_call | solution.py:1414
  455.3 66.1 %last_reduce.1 = (f32[32,3072]{1,0:T(8,128)}, f32[512,1024]{1,0:T(8,128)}, f32[8,128]{1,0:T(8,128)}) custom-call(bf16[2,64,3584]{2,1,0:T(8,128)(2,1)} %get-tuple-element.47.dkv_ref, bf16[2,16,64,512]{3,2,1,0:T(8,128)(2,1)} %get-tuple-element.48.kv_tokens, bf16[16,64,512]{2,1,0:T(8,128)(2,1)} %get-tuple-element.49.dq_ref, bf16[512,1024]{1,0:T(8,128)(2,1)} %bitcast.69, ...), custom_call_target="tpu_custom_call" | custom-call | tf_op jit(solution)/shard_map/last_reduce/pallas_call | solution.py:1672
  521.4 1.8 fusion.14
  523.2 1.3 slice_bitcast_fusion.1
  525.0 1.5 fusion.16
  526.5 3.3 copy.45
  (78 shorter events, 10.1 us)
Async XLA Ops:
  216.4 1.6 copy-start.2
  221.5 10.4 %slice-start.2 = ((s8[8388608]{0:T(1024)(128)(4,1)}), s8[4194304]{0:T(1024)(128)(4,1)S(1)}, s32[]{:S(2)}) async-start(s8[8388608]{0:T(1024)(128)(4,1)} %bitcast.96), calls=%async_computation.2 | async-start | bytes 8388608
  221.9 10.0 %slice-start.3 = ((s8[8388608]{0:T(1024)(128)(4,1)}), s8[4194304]{0:T(1024)(128)(4,1)S(1)}, s32[]{:S(2)}) async-start(s8[8388608]{0:T(1024)(128)(4,1)} %bitcast.96), calls=%async_computation.3 | async-start | bytes 8388608
  231.9 6.0 %copy-start.8 = (bf16[512,4096]{1,0:T(8,128)(2,1)}, bf16[512,4096]{1,0:T(8,128)(2,1)S(1)}, u32[]{:S(2)}) copy-start(bf16[512,4096]{1,0:T(8,128)(2,1)S(1)} %get-tuple-element.93) | copy-start | bytes 12582916
  237.9 2.9 copy-start
  246.8 13.4 %slice-start = ((s8[8388608]{0:T(1024)(128)(4,1)}), s8[4194304]{0:T(1024)(128)(4,1)S(1)}, s32[]{:S(2)}) async-start(s8[8388608]{0:T(1024)(128)(4,1)} %bitcast.92), calls=%async_computation | async-start | bytes 8388608
  247.1 13.2 %slice-start.1 = ((s8[8388608]{0:T(1024)(128)(4,1)}), s8[4194304]{0:T(1024)(128)(4,1)S(1)}, s32[]{:S(2)}) async-start(s8[8388608]{0:T(1024)(128)(4,1)} %bitcast.92), calls=%async_computation.1 | async-start | bytes 8388608
  268.1 2.4 copy-start.3
  268.4 4.4 copy-start.1
  270.5 2.3 copy-start.4
  272.8 2.6 copy-start.10
  275.4 7.3 %copy-start.9 = (bf16[512,4096]{1,0:T(8,128)(2,1)S(1)}, bf16[512,4096]{1,0:T(8,128)(2,1)}, u32[]{:S(2)}) copy-start(bf16[512,4096]{1,0:T(8,128)(2,1)} %copy-done.8) | copy-start | bytes 12582916
  526.5 3.3 copy-start.7
  526.5 3.9 copy-start.6
  526.5 4.7 copy-start.5

commit v6 on v5

--- a/solution.py
+++ b/solution.py
@@ -674,8 +674,8 @@
 def attn_fwd_kernel(
     blks, rows, cols, count, *refs
 ):
-    x_ref, vec_ref, down_ref, across_ref, wq, wk, wv = refs[:7]
-    shares, refs = refs[7 : 7 + count], refs[7 + count :]
+    x_ref, vec_ref, doc_ref, wq, wk, wv = refs[:6]
+    shares, refs = refs[6 : 6 + count], refs[6 + count :]
     p_ref, tail_ref, o_ref, inv_ref, kept_ref, tokens_ref, qkv_out, vec_out = refs[:8]
     wholes, refs = refs[8 : 8 + count], refs[8 + count :]
     (
@@ -992,10 +992,17 @@
         keep.start()
         tail_keys = jnp.concatenate([land[1, :, long:], land[1, :, long:]], 0)
         tail_values = jnp.concatenate([land[2, :, long:], ones_row(tail)], 0)
+        spots = long + lax.broadcasted_iota(jnp.int32, (8, tail), 1)
+        ended, end = jnp.zeros((8, tail), jnp.int32), jnp.int32(0)
+        for number in range(doc_ref.shape[1]):
+            end = end + doc_ref[0, number]
+            ended = ended + (end <= spots).astype(jnp.int32)
+        across = jnp.where(spots < end, ended + 1, 0).astype(jnp.float32)
+        down = jnp.broadcast_to(across[:1], (128, tail)).T
         for first in range(0, tail, rows):
             queries = take_queries(long + first)
             found = jnp.dot(queries, tail_keys, preferred_element_type=jnp.float32)
-            allowed = down_ref[first : first + rows, :1] == across_ref[:1, :]
+            allowed = down[first : first + rows, :1] == across[:1, :]
             found = jnp.where(allowed, found, -1e30)
             peak = jnp.max(found, axis=1, keepdims=True)
             weights = jnp.exp2(found - peak).astype(jnp.bfloat16)
@@ -1036,17 +1043,14 @@
     return pl.BlockSpec(shape, lambda step: (0,) * len(shape), pipeline_mode=pl.Buffered(1))
 
 
-def attn_fwd(x, vec, seg, fronts, shares, collective_id, cols=1024):
+def attn_fwd(x, vec, doc_lengths, long, fronts, shares, collective_id, cols=1024):
     seqs, blks, heads = (lax.axis_size(name) for name in EVERY)
     lead = (seqs, blks, heads // 2, 2)
     group, width = blks * heads, x.shape[0]
     rows = width // 2
     length = group * width
-    tail = seg.shape[0]
-    long = length - tail
+    tail = length - long
     main = long // width
-    down = jnp.broadcast_to(seg[:, None], (tail, 128))
-    across = jnp.broadcast_to(seg[None, :], (8, tail))
     anywhere = pl.BlockSpec(memory_space=pl.ANY)
     count = len(weight_units([share.shape for share in shares])) if shares else 0
     wires = Gather.WIRES * (count + 7)
@@ -1057,7 +1061,7 @@
     return pl.pallas_call(
         functools.partial(attn_fwd_kernel, blks, rows, cols, len(shares)),
         grid=(2 * (long // width),),
-        in_specs=[once(x.shape), once(vec.shape), once((tail, 128)), once((8, tail))]
+        in_specs=[once(x.shape), once(vec.shape), pl.BlockSpec(memory_space=pltpu.SMEM)]
         + [once(share.shape) for share in fronts + shares],
         out_specs=[
             pl.BlockSpec((width, long // 2), lambda step: (lax.rem(step, main), step // main)),
@@ -1109,7 +1113,7 @@
             transcendentals=long * long,
         ),
         name="attn_fwd",
-    )(x, vec, down, across, *fronts, *shares)
+    )(x, vec, doc_lengths, *fronts, *shares)
 
 
 def attn_bwd_kernel(
@@ -1246,7 +1250,7 @@
         )
         plan.append(unit)
         pair = number // 2
-        for stage, at in enumerate((1.5 * pair, 1.5 * pair, 1.5 * pair + 1, 2 * pair + 4, 2 * pair + 6)):
+        for stage, at in enumerate((1.5 * pair, 1.5 * pair, 1.5 * pair + 1, 2 * pair + 3.5, 2 * pair + 5.5)):
             moves.setdefault(min(int(2 * at), 2 * main - 1), []).append((stage, number, unit))
 
     def prepare(start, width, at):
@@ -1461,7 +1465,7 @@
 
 def last_kernel(
     blks, devices, dkv_ref, kv_tokens, dq_ref, x_ref, w_ref, base_ref, sums_ref,
-    dw_out, dx_out, sums_out,
+    dwq, dwk, dwv, dx_out, sums_out,
     grads, x, xt, weights, base, turned_dx, partial, bias, landed,
     r0, r1a, r1b, r2, r3, send, recv,
     own_sem, kv_send, kv_recv, sums_send, sums_recv,
@@ -1571,8 +1575,8 @@
                 (r1b if half else r1a).at[tensor],
                 r2.at[number],
                 r3.at[number],
-                dw_out,
-                ((0, EDGE), (tensor * UNIT + half * UNIT // 2, UNIT // 2)),
+                (dwq, dwk, dwv)[tensor],
+                ((0, EDGE), (half * UNIT // 2, UNIT // 2)),
             )
         )
 
@@ -1631,8 +1635,8 @@
     stages(0, 3)
     await_late(0)
     work(1)
+    stages(1, 2)
     stages(0, 4)
-    stages(1, 2)
     work_input(1)
     stages(1, 3)
     await_late(1)
@@ -1672,12 +1676,12 @@
     return pl.pallas_call(
         functools.partial(last_kernel, blks, devices),
         out_shape=[
-            jax.ShapeDtypeStruct((EDGE, 3 * depth), jnp.float32),
+            *[jax.ShapeDtypeStruct((EDGE, depth), jnp.float32)] * 3,
             jax.ShapeDtypeStruct((width, depth), jnp.float32),
             jax.ShapeDtypeStruct(sums.shape[1:], jnp.float32),
         ],
         in_specs=[pl.BlockSpec(memory_space=pl.ANY)] * 7,
-        out_specs=[pl.BlockSpec(memory_space=pltpu.VMEM)] * 3,
+        out_specs=[pl.BlockSpec(memory_space=pltpu.VMEM)] * 5,
         scratch_shapes=[
             pltpu.VMEM((3, group, HEAD_DIM, width), jnp.bfloat16),
             pltpu.VMEM((width, depth), jnp.bfloat16),
@@ -1700,10 +1704,6 @@
         ),
         name="last_reduce",
     )(dkv, kv_tokens, dq, x, w_qkv, base, sums)
-
-
-def tail_segments(doc_lengths, first, rows):
-    return segment_ids(doc_lengths, first + lax.iota(jnp.int32, rows))
 
 
 BESIDE = ()
@@ -1759,7 +1759,6 @@
         count_here = row.shape[0]
         vec = vec + jnp.pad(row, ((at, 16 - at - count_here), (0, lane - sizes[0])))
         at = at + count_here
-    seg = tail_segments(doc_lengths, long_rows, seq_len - long_rows)[0]
     rest = (weight_output, weight_expand, weight_reduce)
     beside = {which: lax.all_gather(rest[which], EVERY, axis=0, tiled=True) for which in BESIDE}
     (
@@ -1767,7 +1766,8 @@
     ) = attn_fwd(
         flat_rows,
         vec,
-        seg,
+        doc_lengths,
+        long_rows,
         (weight_query, weight_key, weight_value),
         tuple(share for which, share in enumerate(rest) if which not in BESIDE),
         5,
@@ -1848,7 +1848,7 @@
     )
     sums = jnp.concatenate([term.reshape(-1, size) for term, size in zip(sums, sizes)], axis=1)
     sums = jnp.pad(sums, ((0, 0), (0, 8 * lane - sums.shape[1]))).reshape(-1, 8, lane)
-    grad_w_qkv, grad_input, sums = last_reduce(
+    grad_w_query, grad_w_key, grad_w_value, grad_input, sums = last_reduce(
         grad_kv, kv_tokens, grad_query, flat_rows, w_qkv, grad_resid_one, sums, 7
     )
     owner = (lax.axis_index("seq") * blk_count + lax.axis_index("blk")) * head_count
@@ -1865,9 +1865,9 @@
     return (
         layer_output,
         grad_input.reshape(layer_input.shape),
-        grad_w_qkv[:, :model_width],
-        grad_w_qkv[:, model_width : 2 * model_width],
-        grad_w_qkv[:, 2 * model_width :],
+        grad_w_query,
+        grad_w_key,
+        grad_w_value,
         grad_w_output,
         grad_w_expand,
         grad_w_reduce,

time: 541 us -> 535 us (0.989)
    pallas_call x1, Pallas kernels: 66.1 us -> 60 us  [last_reduce(): pl.pallas_call(functools.partial(last_kernel, blks, devices), out_shape=[...]
    unnamed x37 -> x48, local copies, waits for them, and re-layouts: 9.62 us -> 11.6 us
where the time goes in v6:
time: 535 us; the launch traced here: 526 us
  Pallas kernels  437 us (82%)
  matrix products  58.8 us (11%)
  local copies, waits for them, and re-layouts  17.4 us (3%)
  other arithmetic  12.1 us (2%)
    pallas_call x1, Pallas kernels, attn_fwd(): pl.pallas_call(functools.partial(attn_fwd_kernel, blks, rows, cols, len(s...  210 us
    pallas_call x1, Pallas kernels, attn_bwd(): pl.pallas_call(functools.partial(attn_bwd_kernel, blks, rows, cols, len(p...  167 us
    pallas_call x1, Pallas kernels, last_reduce(): pl.pallas_call(functools.partial(last_kernel, blks, devices), out_shape=[...  60 us
    dot_general x3, matrix products, right_dot(): lax.dot_general(left, right, (((1,), (1,)), ((), ())), preferred_element_...  22.6 us
    dot_general x3, matrix products, plain_dot(): return jnp.dot(left, right, preferred_element_type=jnp.float32)  18.6 us
    dot_general x3, matrix products, left_dot(): lax.dot_general(left, right, (((0,), (0,)), ((), ())), preferred_element_...  17.6 us
    unnamed x48, local copies, waits for them, and re-layouts  11.6 us

profile of v6, /device:TPU:0, one launch (start us, length us, event | category | flops | bytes accessed | tf_op | source)
XLA Modules:
  0.0 526.3 jit_solution(16721512952340811044)
XLA Ops:
  0.7 0.7 reshape.295
  1.4 1.4 pad_add_fusion.refs_1_
  2.8 209.9 %attn_fwd.1 = (bf16[7168,7168]{1,0:T(8,128)(2,1)}, bf16[1024,1024]{1,0:T(8,128)(2,1)}, bf16[64,8192]{1,0:T(8,128)(2,1)}, f32[8,8192]{1,0:T(8,128)}, bf16[3,64,81...) custom-call(bf16[512,1024]{1,0:T(8,128)(2,1)} %bitcast.68, ...), custom_call_target="tpu_custom_call" | custom-call | flops 13153337344 | bytes 102760448 | tf_op jit(solution)/shard_map/attn_fwd/pallas_call | solution.py:1061
  212.7 1.3 copy.39
  214.3 3.3 fusion.16
  218.1 10.0 %multiply_convert_fusion = (bf16[512,4096]{1,0:T(8,128)(2,1)S(1)}, f32[512,4096]{1,0:T(8,128)}) fusion(f32[4096]{0:T(1024)S(1)} %add.184, bf16[1024,4096]{1,0:T(8,128)(2,1)} %bitcast.90, f32[512,1024]{1,0:T(8,128)S(1)} %get-tuple-element.93, f32[1024]{0:T(1024)S(1)} %add.181, f32[1024]{0:T(1024)S(1)} %mul.166, f32[512]{0:T(512)S(1)} %fusion.5, ...), kind=kOutput, calls=%fused_computation.2 | convolution fusion | flops 4310171648 | bytes 23097344 | tf_op jit(solution)/shard_map/dot_general | solution.py:36
  228.2 6.0 %fusion.17 = (f32[512]{0:T(512)S(1)}, f32[512,1024]{1,0:T(8,128)}) fusion(f32[1024]{0:T(1024)S(1)} %add.190, bf16[512,4096]{1,0:T(8,128)(2,1)S(1)} %get-tuple-element.94, bf16[4096,1024]{1,0:T(8,128)(2,1)S(1)} %bitcast.97, f32[1024]{0:T(1024)S(1)} %add.181, f32[1024]{0:T(1024)S(1)} %mul.166, f32[512]{0:T(512)S(1)} %fusion.5, ...), kind=kOutput, calls=%fused_computation.60 | convolution fusion | flops 4298636800 | bytes 16795648 | tf_op jit(solution)/shard_map/dot_general | solution.py:36
  235.8 1.9 multiply_reduce_fusion.3
  237.8 2.4 fusion
  240.3 3.6 fusion.13
  244.1 13.1 %convert_reduce_fusion = (f32[4096]{0:T(1024)S(1)}, bf16[512,4096]{1,0:T(8,128)(2,1)}) fusion(f32[512,4096]{1,0:T(8,128)} %get-tuple-element.95, f32[4096]{0:T(1024)S(1)} %add.184, bf16[512,1024]{1,0:T(8,128)(2,1)S(1)} %get-tuple-element.69, bf16[4096,1024]{1,0:T(8,128)(2,1)} %bitcast.94), kind=kOutput, calls=%fused_computation | convolution fusion | flops 4328517632 | bytes 22052864 | tf_op jit(solution)/shard_map/dot_general | solution.py:46
  257.3 7.2 %multiply_reduce_fusion = (f32[1024]{0:T(1024)S(1)}, f32[512]{0:T(512)S(1)}, f32[1024]{0:T(1024)S(1)}, f32[512,1024]{1,0:T(8,128)S(1)}) fusion(f32[512,1024]{1,0:T(8,128)S(1)} %get-tuple-element.93, f32[512]{0:T(512)S(1)} %fusion.5, f32[512]{0:T(512)S(1)} %broadcast_multiply_fusion.1, f32[1024]{0:T(1024)S(1)} %mul.166, ...), kind=kOutput, calls=%fused_computation.11 | convolution fusion | flops 4300207616 | bytes 18894848 | tf_op jit(solution)/shard_map/dot_general | solution.py:46
  265.4 2.1 copy-done.3
  267.5 2.3 convolution_convert_fusion.3
  269.8 2.6 convolution_convert_fusion.2
  272.4 7.3 %convolution_convert_fusion.1 = bf16[1024,4096]{1,0:T(8,128)(2,1)} fusion(bf16[512,4096]{1,0:T(8,128)(2,1)S(1)} %copy-done.14, f32[512,1024]{1,0:T(8,128)S(1)} %get-tuple-element.93, f32[1024]{0:T(1024)S(1)} %add.181, f32[1024]{0:T(1024)S(1)} %mul.166, f32[512]{0:T(512)S(1)} %fusion.5, f32[512]{0:T(512)S(1)} %broadcast_multiply_fusion.1), kind=kOutput, calls=%fused_computation.5 | convolution fusion | flops 4301783040 | bytes 14692352 | tf_op jit(solution)/shard_map/dot_general | solution.py:40
  279.7 7.0 %convolution_convert_fusion = bf16[4096,1024]{1,0:T(8,128)(2,1)} fusion(bf16[512,4096]{1,0:T(8,128)(2,1)S(1)} %copy-done.13, bf16[512,1024]{1,0:T(8,128)(2,1)S(1)} %get-tuple-element.69), kind=kOutput, calls=%fused_computation.4 | convolution fusion | flops 4299161600 | bytes 13631488 | tf_op jit(solution)/shard_map/dot_general | solution.py:40
  286.7 166.7 %attn_bwd.1 = (bf16[2,64,3584]{2,1,0:T(8,128)(2,1)}, bf16[16,64,512]{2,1,0:T(8,128)(2,1)}, bf16[2,16,64,512]{3,2,1,0:T(8,128)(2,1)}, f32[32,1024]{1,0:T(8,128)},...) custom-call(bf16[7168,7168]{1,0:T(8,128)(2,1)} %get-tuple-element.44.refs_0_, bf16[1024,1024]{1,0:T(8,128)(2,1)} %get-tuple-element.45.refs_1_, ...), custom_call_target="tpu_custom_call" | custom-call | flops 26306674688 | bytes 102760448 | tf_op jit(solution)/shard_map/attn_bwd/pallas_call | solution.py:1418
  455.0 60.0 %last_reduce.1 = (f32[32,1024]{1,0:T(8,128)}, f32[32,1024]{1,0:T(8,128)}, f32[32,1024]{1,0:T(8,128)}, f32[512,1024]{1,0:T(8,128)}, f32[8,128]{1,0:T(8,128)}) custom-call(bf16[2,64,3584]{2,1,0:T(8,128)(2,1)} %get-tuple-element.49.dkv_ref, bf16[2,16,64,512]{3,2,1,0:T(8,128)(2,1)} %get-tuple-element.50.kv_tokens, ...), custom_call_target="tpu_custom_call" | custom-call | tf_op jit(solution)/shard_map/last_reduce/pallas_call | solution.py:1676
  515.0 1.3 slice_bitcast_fusion.1
  516.8 1.5 fusion.15
  518.4 3.3 copy.48
  524.3 0.8 copy.53
  525.1 0.8 copy.54
  (83 shorter events, 8.5 us)
Async XLA Ops:
  212.7 1.6 copy-start.2
  217.8 10.4 %slice-start.2 = ((s8[8388608]{0:T(1024)(128)(4,1)}), s8[4194304]{0:T(1024)(128)(4,1)S(1)}, s32[]{:S(2)}) async-start(s8[8388608]{0:T(1024)(128)(4,1)} %bitcast.95), calls=%async_computation.2 | async-start | bytes 8388608
  218.1 10.0 %slice-start.3 = ((s8[8388608]{0:T(1024)(128)(4,1)}), s8[4194304]{0:T(1024)(128)(4,1)S(1)}, s32[]{:S(2)}) async-start(s8[8388608]{0:T(1024)(128)(4,1)} %bitcast.95), calls=%async_computation.3 | async-start | bytes 8388608
  228.2 6.0 %copy-start.12 = (bf16[512,4096]{1,0:T(8,128)(2,1)}, bf16[512,4096]{1,0:T(8,128)(2,1)S(1)}, u32[]{:S(2)}) copy-start(bf16[512,4096]{1,0:T(8,128)(2,1)S(1)} %get-tuple-element.94) | copy-start | bytes 12582916
  228.2 6.0 %copy-start.11 = (s32[1,32]{1,0:T(1,128)S(1)}, s32[1,32]{1,0:T(1,128)}, u32[]{:S(2)}) copy-start(s32[1,32]{1,0:T(1,128)} %refs_2_.1) | copy-start | bytes 388
  234.2 3.6 copy-start
  243.8 13.4 %slice-start = ((s8[8388608]{0:T(1024)(128)(4,1)}), s8[4194304]{0:T(1024)(128)(4,1)S(1)}, s32[]{:S(2)}) async-start(s8[8388608]{0:T(1024)(128)(4,1)} %bitcast.91), calls=%async_computation | async-start | bytes 8388608
  244.1 13.2 %slice-start.1 = ((s8[8388608]{0:T(1024)(128)(4,1)}), s8[4194304]{0:T(1024)(128)(4,1)S(1)}, s32[]{:S(2)}) async-start(s8[8388608]{0:T(1024)(128)(4,1)} %bitcast.91), calls=%async_computation.1 | async-start | bytes 8388608
  265.2 2.4 copy-start.3
  265.4 4.4 copy-start.1
  267.5 2.3 copy-start.4
  269.8 2.6 copy-start.14
  272.4 7.3 %copy-start.13 = (bf16[512,4096]{1,0:T(8,128)(2,1)S(1)}, bf16[512,4096]{1,0:T(8,128)(2,1)}, u32[]{:S(2)}) copy-start(bf16[512,4096]{1,0:T(8,128)(2,1)} %copy-done.12) | copy-start | bytes 12582916
  518.3 3.3 copy-start.10
  518.3 4.0 copy-start.9
  518.3 4.6 copy-start.8
  518.3 5.3 %copy-start.7 = (f32[32,1024]{1,0:T(8,128)S(1)}, f32[32,1024]{1,0:T(8,128)}, u32[]{:S(2)}) copy-start(f32[32,1024]{1,0:T(8,128)} %get-tuple-element.123) | copy-start | bytes 393220
  518.4 5.9 %copy-start.6 = (f32[32,4096]{1,0:T(8,128)S(1)}, f32[32,4096]{1,0:T(8,128)}, u32[]{:S(2)}) copy-start(f32[32,4096]{1,0:T(8,128)} %get-tuple-element.124) | copy-start | bytes 1572868
  518.4 6.7 %copy-start.5 = (f32[128,1024]{1,0:T(8,128)S(1)}, f32[128,1024]{1,0:T(8,128)}, u32[]{:S(2)}) copy-start(f32[128,1024]{1,0:T(8,128)} %get-tuple-element.125) | copy-start | bytes 1572868
